TPU v7x, 32 devices: a whole 2x2x4 slice. The times are simulated.
32 devices in a mesh: shot: 4 (over y, x), depth: 2 (over core), inline: 4 (over z).
Axes of the slice: x: 2, y: 2, z: 4, core: 2. Of those that a mesh axis runs over, the one named last changes fastest.
Arguments:
- gradient: float32 [4, 32, 512, 512], P('shot', 'depth', 'inline'), may hold values from -8 to 8
- signs: int32 [4, 512], P('shot'), may hold values from 0 to 1
- model: float32 [32, 512, 512], P('depth', 'inline'), may hold values from 1.5 to 4.5
Outputs:
- updated: float32 [32, 512, 512], P('depth', 'inline')
Inputs may be any that keep to these rules, and one draw needn't show every extreme that they name: `signs`: each bit s gives the sign 2 s - 1 of one crossline column of one group's partial.
All inputs are finite; a program needn't handle non-finite values.
Results may differ from a plain program's by a relative error of at most 0.00002.
Values sent between devices are 32-bit elements; how exact they have to be, the bound alone decides.
No kernel may reach another device: no remote copies, remote signals or barrier semaphores. Data moves between devices by JAX's collectives and lax.ppermute only.
A program may use at most 128 MiB of HBM per device.

v0:
```python
import jax
import jax.numpy as jnp
from jax import lax
from jax.sharding import PartitionSpec as P

ITERS = 3


step_tau = 0.28
step_sigma = 0.28
radius = 0.3
rate = 0.5


def padded_2(x, sides, width):
    for axis, dim in sides:
        size, length = (lax.axis_size(axis), x.shape[dim])
        up = [(i, (i + 1) % size) for i in range(size - 1)]
        down = [(j, i) for i, j in up]
        last = lax.slice_in_dim(x, length - width, length, axis=dim)
        first = lax.slice_in_dim(x, 0, width, axis=dim)
        before = lax.ppermute(last, axis, up)
        after = lax.ppermute(first, axis, down)
        x = jnp.concatenate([before, x, after], axis=dim)
    return x


def coords(start, count, total):
    place = start - 1 + jnp.arange(count + 1, dtype=jnp.int32)
    keeps = (place <= total - 2).astype(jnp.float32)
    inside = (place >= 0).astype(jnp.float32)
    return (keeps, inside)


def iterate(target, padder, starts, totals):
    shape = target.shape
    keep_z, in_z = coords(starts[0], shape[0], totals[0])
    keep_x, in_x = coords(starts[1], shape[1], totals[1])
    keep_y, in_y = coords(starts[2], shape[2], totals[2])
    inside = in_z[:, None, None] * in_x[None, :, None] * in_y[None, None, :]
    primal = target
    extrapolated = target
    dual = jnp.zeros((3,) + shape, jnp.float32)
    for step in range(ITERS):
        stacked = jnp.concatenate([extrapolated[None], dual], axis=0)
        padded = padder(stacked)
        ahead = padded[0]
        center = ahead[:-1, :-1, :-1]
        old = padded[1:, :-1, :-1, :-1]
        qz = old[0] + step_sigma * (ahead[1:, :-1, :-1] - center) * keep_z[:, None, None]
        qx = old[1] + step_sigma * (ahead[:-1, 1:, :-1] - center) * keep_x[None, :, None]
        qy = old[2] + step_sigma * (ahead[:-1, :-1, 1:] - center) * keep_y[None, None, :]
        length = jnp.sqrt(qz * qz + qx * qx + qy * qy)
        scale = inside / jnp.maximum(1.0, length / radius)
        qz, qx, qy = (qz * scale, qx * scale, qy * scale)
        diverge = (
            qz[1:, 1:, 1:]
            - qz[:-1, 1:, 1:]
            + (qx[1:, 1:, 1:] - qx[1:, :-1, 1:])
            + (qy[1:, 1:, 1:] - qy[1:, 1:, :-1])
        )
        dual = jnp.stack([qz[1:, 1:, 1:], qx[1:, 1:, 1:], qy[1:, 1:, 1:]], axis=0)
        fresh = (primal + step_tau * diverge + step_tau * target) / (1.0 + step_tau)
        extrapolated = 2.0 * fresh - primal
        primal = fresh
    return primal


def body(gradient, signs, model):
    factor = (2 * signs[0] - 1).astype(jnp.float32)
    signed = gradient[0] * factor[None, None, :]
    cz, cx = (model.shape[0], model.shape[1])
    start_z = lax.axis_index("depth") * cz
    start_x = lax.axis_index("inline") * cx
    total_z = cz * lax.axis_size("depth")
    total_x = cx * lax.axis_size("inline")
    summed = lax.psum_scatter(signed, "shot", scatter_dimension=2, tiled=True)
    cy = summed.shape[2]
    start_y = lax.axis_index("shot") * cy
    model_part = lax.dynamic_slice_in_dim(model, start_y, cy, 2)
    target = model_part - rate * summed
    starts = (start_z, start_x, start_y)
    totals = (total_z, total_x, cy * lax.axis_size("shot"))

    def padder(stacked):
        return padded_2(stacked, (("shot", 3), ("depth", 1), ("inline", 2)), 1)

    primal = iterate(target, padder, starts, totals)
    return lax.all_gather(primal, "shot", axis=2, tiled=True)


def solution(mesh):
    placed = (P("shot", "depth", "inline", None), P("shot", None), P("depth", "inline", None))
    return jax.shard_map(
        body, mesh=mesh, in_specs=placed, out_specs=P("depth", "inline", None), check_vma=False
    )
```

profile of v0, /device:TPU:0, one launch (start us, length us, event | category | flops | bytes accessed | tf_op | source)
XLA Modules:
  0.0 445.2 jit_solution(6346657756927112208)
XLA Ops:
  6.5 5.4 %copy.8 = f32[1,16,128,512]{2,1,3,0:T(8,128)} copy(f32[1,16,128,512]{3,2,1,0:T(8,128)} %param.3) | data formatting | bytes 8388608 | tf_op args[0]
  12.0 4.4 bitcast_multiply_fusion
  18.3 53.6 %reduce-scatter.2.cloned.1.call-done = f32[16,128,128]{1,0,2:T(8,128)} async-done(((f32[16,128,512]{1,0,2:T(8,128)}), f32[16,128,128]{1,0,2:T(8,128)}) %reduce-scatter.2.cloned.1.call-update) | async-done | bytes 1048592 | tf_op jit(solution)/shard_map/reduce_scatter | solution.py:77
  74.7 4.5 %collective-permute-start = (f32[4,16,128,1]{2,1,3,0:T(8,128)S(1)}, f32[4,16,128,1]{2,1,3,0:T(8,128)S(1)}, u32[]{:S(2)}, u32[]{:S(2)}) collective-permute-start(f32[4,16,128,1]{2,1,3,0:T(8,128)S(1)} %get-tuple-element.49), channel_id=1, source_target_pairs={{0,8},{8,16},{16,24},{1,9},{9,17},{17,25},{2,10},{10,18},{18,26},{... | collective-permute-start | bytes 98312 | tf_op jit(solution)/shard_map/ppermute | solution.py:22
  82.5 3.1 collective-permute-start.2
  86.7 3.3 pad_maximum_fusion.2
  90.0 11.0 %fusion.60 = (f32[4,18,1,130]{2,1,3,0:T(8,128)}, f32[4,18,1,130]{2,1,3,0:T(8,128)}) fusion(f32[4,18,128,130]{2,1,3,0:T(8,128)} %pad_maximum_fusion.2), kind=kLoop, calls=%fused_computation.155 | loop fusion | bytes 149760 | tf_op jit(solution)/shard_map/slice | solution.py:20
  100.9 5.7 %copy.11 = f32[4,18,1,130]{3,0,2,1:T(4,128)S(1)} copy(f32[4,18,1,130]{2,1,3,0:T(8,128)} %get-tuple-element.32) | data formatting | bytes 74880 | tf_op jit(solution)/shard_map/slice | solution.py:21
  107.9 5.7 %copy.9 = f32[4,18,1,130]{3,0,2,1:T(4,128)S(1)} copy(f32[4,18,1,130]{2,1,3,0:T(8,128)} %get-tuple-element.31) | data formatting | bytes 74880 | tf_op jit(solution)/shard_map/slice | solution.py:20
  113.7 5.0 %collective-permute-start.4 = (f32[4,18,1,130]{3,0,2,1:T(4,128)S(1)}, f32[4,18,1,130]{3,0,2,1:T(4,128)S(1)}, u32[]{:S(2)}, u32[]{:S(2)}) collective-permute-start(f32[4,18,1,130]{3,0,2,1:T(4,128)S(1)} %copy.9), channel_id=1, source_target_pairs={{0,1},{1,2},{2,3},{4,5},{5,6},{6,7},{8,9},{9,10},{10,11},{12,13},{... | collective-permute-start | bytes 112328 | tf_op jit(solution)/shard_map/ppermute | solution.py:22
  118.7 5.3 %copy.13 = f32[4,18,1,130]{2,1,3,0:T(8,128)} copy(f32[4,18,1,130]{3,0,2,1:T(4,128)S(1)} %collective-permute-done.5) | data formatting | bytes 74880 | tf_op jit(solution)/shard_map/ppermute | solution.py:23
  124.1 5.4 %copy.10 = f32[4,18,1,130]{2,1,3,0:T(8,128)} copy(f32[4,18,1,130]{3,0,2,1:T(4,128)S(1)} %collective-permute-done.4) | data formatting | bytes 74880 | tf_op jit(solution)/shard_map/ppermute | solution.py:22
  129.5 4.2 fusion.2
  134.9 10.8 %fusion.40 = (f32[17,129,129]{1,0,2:T(8,128)}, f32[17,129,129]{1,0,2:T(8,128)S(1)}, f32[17,129,129]{1,0,2:T(8,128)S(1)}, f32[17,129,129]{1,0,2:T(8,128)S(1)}) fusion(f32[129]{0:T(256)S(1)} %compare_convert_fusion, f32[17,129]{1,0:T(8,128)S(1)} %broadcast_multiply_fusion, f32[17]{0:T(128)S(1)} %compare_select_fusion.2, f32[18,130,130]{1,0,2:T(8,128)S(1)} %fusion.2, ...), kind=kLoop, calls=%fused_computation.146 | loop fusion | flops 9618498 | bytes 13892852 | tf_op jit(solution)/shard_map/mul | solution.py:55
  145.7 4.1 fusion.39
  149.8 8.3 %subtract_bitcast_fusion.1 = (f32[1,16,128,128]{2,1,3,0:T(8,128)S(1)}, f32[16,128,128]{1,0,2:T(8,128)}, f32[1,16,128,128]{2,1,3,0:T(8,128)S(1)}, f32[1,16,128,128]{2,1,3,0:T(8,128)S(1)}, f32[1,16,128,128]{2,1,3,0:T(8,128)S(1)}) fusion(f32[16,128,128]{1,0,2:T(8,128)S(1)} %copy-done.7, f32[17,129,129]{1,0,2:T(8,128)} %get-tuple-element.26, ...), kind=kLoop, calls=%fused_computation.101 | loop fusion | flops 2883584 | bytes 12582912 | tf_op jit(solution)/shard_map/broadcast_in_dim | solution.py:45
  159.4 4.9 %collective-permute-start.6 = (f32[4,16,128,1]{2,1,3,0:T(8,128)S(1)}, f32[4,16,128,1]{2,1,3,0:T(8,128)S(1)}, u32[]{:S(2)}, u32[]{:S(2)}) collective-permute-start(f32[4,16,128,1]{2,1,3,0:T(8,128)S(1)} %get-tuple-element.41), channel_id=1, source_target_pairs={{0,8},{8,16},{16,24},{1,9},{9,17},{17,25},{2,10},{10,18},{18,26},{... | collective-permute-start | bytes 98312 | tf_op jit(solution)/shard_map/ppermute | solution.py:22
  168.0 3.1 collective-permute-start.8
  172.9 4.1 pad_maximum_fusion.3
  177.0 11.0 %fusion.59 = (f32[4,18,1,130]{2,1,3,0:T(8,128)}, f32[4,18,1,130]{2,1,3,0:T(8,128)}) fusion(f32[4,18,128,130]{2,1,3,0:T(8,128)} %pad_maximum_fusion.3), kind=kLoop, calls=%fused_computation.154 | loop fusion | bytes 149760 | tf_op jit(solution)/shard_map/slice | solution.py:20
  188.0 6.3 %copy.16 = f32[4,18,1,130]{3,0,2,1:T(4,128)} copy(f32[4,18,1,130]{2,1,3,0:T(8,128)} %get-tuple-element.30) | data formatting | bytes 74880 | tf_op jit(solution)/shard_map/slice | solution.py:21
  195.6 6.3 %copy.14 = f32[4,18,1,130]{3,0,2,1:T(4,128)} copy(f32[4,18,1,130]{2,1,3,0:T(8,128)} %get-tuple-element.29) | data formatting | bytes 74880 | tf_op jit(solution)/shard_map/slice | solution.py:20
  201.9 5.3 %collective-permute-start.10 = (f32[4,18,1,130]{3,0,2,1:T(4,128)}, f32[4,18,1,130]{3,0,2,1:T(4,128)}, u32[]{:S(2)}, u32[]{:S(2)}) collective-permute-start(f32[4,18,1,130]{3,0,2,1:T(4,128)} %copy.14), channel_id=1, source_target_pairs={{0,1},{1,2},{2,3},{4,5},{5,6},{6,7},{8,9},{9,10},{10,11},{12,13},{... | collective-permute-start | bytes 112328 | tf_op jit(solution)/shard_map/ppermute | solution.py:22
  207.2 10.7 %pad_maximum_fusion = f32[4,18,130,130]{2,1,3,0:T(8,128)} fusion(f32[1,16,128,128]{2,1,3,0:T(8,128)} %copy-done.5, f32[1,16,128,128]{2,1,3,0:T(8,128)S(1)} %get-tuple-element.47, f32[1,16,128,128]{2,1,3,0:T(8,128)S(1)} %get-tuple-element.46, f32[1,16,128,128]{2,1,3,0:T(8,128)S(1)} %get-tuple-element.15), kind=kLoop, calls=%fused_computation.1 | loop fusion | flops 3650400 | bytes 9061504 | tf_op jit(solution)/shard_map/concatenate | solution.py:45
  217.9 6.1 %copy.18 = f32[4,18,1,130]{2,1,3,0:T(8,128)} copy(f32[4,18,1,130]{3,0,2,1:T(4,128)} %collective-permute-done.11) | data formatting | bytes 74880 | tf_op jit(solution)/shard_map/ppermute | solution.py:23
  224.1 6.2 %copy.15 = f32[4,18,1,130]{2,1,3,0:T(8,128)} copy(f32[4,18,1,130]{3,0,2,1:T(4,128)} %collective-permute-done.10) | data formatting | bytes 74880 | tf_op jit(solution)/shard_map/ppermute | solution.py:22
  230.2 16.3 %maximum_maximum_fusion = f32[4,18,129,130]{2,1,3,0:T(8,128)S(1)} fusion(f32[4,1,128,130]{2,1,3,0:T(1,128)S(1)} %collective-permute-done.9, f32[4,16,128,1]{2,1,3,0:T(8,128)S(1)} %collective-permute-done.7, f32[1,16,128,128]{2,1,3,0:T(8,128)} %copy-done.5, f32[1,16,128,128]{2,1,3,0:T(8,128)S(1)} %get-tuple-element.47, ...), kind=kLoop, calls=%fused_computation | loop fusion | flops 9659520 | bytes 9659520 | tf_op jit(solution)/shard_map/concatenate | solution.py:24
  246.6 3.0 fusion.1
  249.6 6.5 %fusion.43 = (f32[17,129,129]{1,0,2:T(8,128)}, f32[17,129,129]{1,0,2:T(8,128)}, f32[17,129,129]{1,0,2:T(8,128)}, f32[17,129,129]{1,0,2:T(8,128)}) fusion(f32[129]{0:T(256)S(1)} %compare_convert_fusion, f32[17,129]{1,0:T(8,128)S(1)} %broadcast_multiply_fusion, f32[17]{0:T(128)S(1)} %compare_select_fusion.2, f32[18,130,130]{1,0,2:T(8,128)S(1)} %fusion.1, ...), kind=kLoop, calls=%fused_computation.149 | loop fusion | flops 5375043 | bytes 12457856 | tf_op jit(solution)/shard_map/mul | solution.py:55
  256.1 7.0 %fusion.42 = (f32[17,129,129]{1,0,2:T(8,128)}, f32[17,129,129]{1,0,2:T(8,128)}) fusion(f32[17,129,129]{1,0,2:T(8,128)} %get-tuple-element.13, f32[17,129,129]{1,0,2:T(8,128)} %get-tuple-element.14, f32[17,129,129]{1,0,2:T(8,128)} %get-tuple-element.12, f32[129]{0:T(256)S(1)} %compare_convert_fusion, f32[17,129]{1,0:T(8,128)S(1)} %broadcast_multiply_fusion), kind=kLoop, calls=%fused_computation.148 | loop fusion | flops 3111867 | bytes 5667228 | tf_op jit(solution)/shard_map/mul | solution.py:55
  263.1 6.9 %subtract_bitcast_fusion = (f32[1,16,128,128]{2,1,3,0:T(8,128)S(1)}, f32[16,128,128]{1,0,2:T(8,128)}, f32[1,16,128,128]{2,1,3,0:T(8,128)S(1)}, f32[1,16,128,128]{2,1,3,0:T(8,128)S(1)}, f32[1,16,128,128]{2,1,3,0:T(8,128)S(1)}) fusion(f32[16,128,128]{1,0,2:T(8,128)S(1)} %copy-done.16, f32[16,128,128]{1,0,2:T(8,128)S(1)} %copy-done.8, ...), kind=kLoop, calls=%fused_computation.100 | loop fusion | flops 3145728 | bytes 13631488 | tf_op jit(solution)/shard_map/broadcast_in_dim | solution.py:45
  271.3 5.7 %collective-permute-start.12 = (f32[4,16,128,1]{2,1,3,0:T(8,128)S(1)}, f32[4,16,128,1]{2,1,3,0:T(8,128)S(1)}, u32[]{:S(2)}, u32[]{:S(2)}) collective-permute-start(f32[4,16,128,1]{2,1,3,0:T(8,128)S(1)} %get-tuple-element.39), channel_id=1, source_target_pairs={{0,8},{8,16},{16,24},{1,9},{9,17},{17,25},{2,10},{10,18},{18,26},{... | collective-permute-start | bytes 98312 | tf_op jit(solution)/shard_map/ppermute | solution.py:22
  280.7 3.1 collective-permute-start.14
  285.6 4.1 pad_maximum_fusion.4
  289.8 11.0 %fusion.58 = (f32[4,18,1,130]{2,1,3,0:T(8,128)}, f32[4,18,1,130]{2,1,3,0:T(8,128)}) fusion(f32[4,18,128,130]{2,1,3,0:T(8,128)} %pad_maximum_fusion.4), kind=kLoop, calls=%fused_computation.153 | loop fusion | bytes 149760 | tf_op jit(solution)/shard_map/slice | solution.py:20
  300.8 6.3 %copy.21 = f32[4,18,1,130]{3,0,2,1:T(4,128)} copy(f32[4,18,1,130]{2,1,3,0:T(8,128)} %get-tuple-element.28) | data formatting | bytes 74880 | tf_op jit(solution)/shard_map/slice | solution.py:21
  308.4 6.3 %copy.19 = f32[4,18,1,130]{3,0,2,1:T(4,128)} copy(f32[4,18,1,130]{2,1,3,0:T(8,128)} %get-tuple-element.27) | data formatting | bytes 74880 | tf_op jit(solution)/shard_map/slice | solution.py:20
  314.7 5.2 %collective-permute-start.16 = (f32[4,18,1,130]{3,0,2,1:T(4,128)}, f32[4,18,1,130]{3,0,2,1:T(4,128)}, u32[]{:S(2)}, u32[]{:S(2)}) collective-permute-start(f32[4,18,1,130]{3,0,2,1:T(4,128)} %copy.19), channel_id=1, source_target_pairs={{0,1},{1,2},{2,3},{4,5},{5,6},{6,7},{8,9},{9,10},{10,11},{12,13},{... | collective-permute-start | bytes 112328 | tf_op jit(solution)/shard_map/ppermute | solution.py:22
  319.9 11.0 %pad_maximum_fusion.1 = f32[4,18,130,130]{2,1,3,0:T(8,128)} fusion(f32[1,16,128,128]{2,1,3,0:T(8,128)} %copy-done.10, f32[1,16,128,128]{2,1,3,0:T(8,128)} %copy-done.9, f32[1,16,128,128]{2,1,3,0:T(8,128)S(1)} %get-tuple-element.43, f32[1,16,128,128]{2,1,3,0:T(8,128)S(1)} %get-tuple-element.9), kind=kLoop, calls=%fused_computation.3 | loop fusion | flops 3650400 | bytes 9061504 | tf_op jit(solution)/shard_map/concatenate | solution.py:45
  330.9 6.1 %copy.23 = f32[4,18,1,130]{2,1,3,0:T(8,128)} copy(f32[4,18,1,130]{3,0,2,1:T(4,128)} %collective-permute-done.17) | data formatting | bytes 74880 | tf_op jit(solution)/shard_map/ppermute | solution.py:23
  337.0 6.2 %copy.20 = f32[4,18,1,130]{2,1,3,0:T(8,128)} copy(f32[4,18,1,130]{3,0,2,1:T(4,128)} %collective-permute-done.16) | data formatting | bytes 74880 | tf_op jit(solution)/shard_map/ppermute | solution.py:22
  343.2 16.2 %maximum_maximum_fusion.1 = f32[4,18,129,130]{2,1,3,0:T(8,128)S(1)} fusion(f32[4,1,128,130]{2,1,3,0:T(1,128)S(1)} %collective-permute-done.15, f32[4,16,128,1]{2,1,3,0:T(8,128)S(1)} %collective-permute-done.13, f32[1,16,128,128]{2,1,3,0:T(8,128)} %copy-done.10, f32[1,16,128,128]{2,1,3,0:T(8,128)} %copy-done.9, f32[1,16,128,128]{2,1,3,0:T(8,128)S(1)} %get-tuple-element.43, ...), kind=kLoop, calls=%fused_computation.2 | loop fusion | flops 9659520 | bytes 9659520 | tf_op jit(solution)/shard_map/concatenate | solution.py:24
  359.4 3.0 fusion
  362.4 6.5 %fusion.46 = (f32[17,129,129]{1,0,2:T(8,128)}, f32[17,129,129]{1,0,2:T(8,128)}, f32[17,129,129]{1,0,2:T(8,128)}, f32[17,129,129]{1,0,2:T(8,128)}) fusion(f32[129]{0:T(256)S(1)} %compare_convert_fusion, f32[17,129]{1,0:T(8,128)S(1)} %broadcast_multiply_fusion, f32[17]{0:T(128)S(1)} %compare_select_fusion.2, f32[18,130,130]{1,0,2:T(8,128)S(1)} %fusion, ...), kind=kLoop, calls=%fused_computation.152 | loop fusion | flops 5375043 | bytes 12457856 | tf_op jit(solution)/shard_map/mul | solution.py:55
  368.9 5.1 %fusion.45 = (f32[17,129,129]{1,0,2:T(8,128)S(1)}, f32[17,129,129]{1,0,2:T(8,128)S(1)}) fusion(f32[17,129,129]{1,0,2:T(8,128)} %get-tuple-element.7, f32[17,129,129]{1,0,2:T(8,128)} %get-tuple-element.8, f32[17,129,129]{1,0,2:T(8,128)} %get-tuple-element.6, f32[129]{0:T(256)S(1)} %compare_convert_fusion, f32[17,129]{1,0:T(8,128)S(1)} %broadcast_multiply_fusion), kind=kLoop, calls=%fused_computation.151 | loop fusion | flops 3111867 | bytes 5667228 | tf_op jit(solution)/shard_map/mul | solution.py:55
  374.0 2.6 fusion.26
  376.6 56.0 %all-gather.2.cloned.1.call-done = f32[16,128,512]{1,0,2:T(8,128)} async-done(((f32[16,128,128]{1,0,2:T(8,128)}), f32[16,128,512]{1,0,2:T(8,128)}) %all-gather.2.cloned.1.call-update) | async-done | bytes 4194320 | tf_op jit(solution)/shard_map/all_gather | solution.py:89
  432.7 5.2 %copy.24 = f32[16,128,512]{2,1,0:T(8,128)} copy(f32[16,128,512]{1,0,2:T(8,128)} %all-gather.2.cloned.1.call-done) | data formatting | bytes 8388608 | tf_op jit(solution)/shard_map/all_gather | solution.py:89
  (92 shorter events, 27.6 us)
Async XLA Ops:
  6.5 5.4 %copy-start.21 = (s32[1,512]{1,0:T(1,128)S(1)}, s32[1,512]{1,0:T(1,128)}, u32[]{:S(2)}) copy-start(s32[1,512]{1,0:T(1,128)} %param.4) | copy-start | bytes 6148
  6.5 65.4 %reduce-scatter.2.cloned.1.call-start = ((), (), s32[]{:S(2)}) async-start(), calls=%async_computation.1 | async-start | bytes 5242880 | tf_op jit(solution)/shard_map/reduce_scatter | solution.py:77
  16.4 416.3 %all-gather.2.cloned.1.call-start = ((), (), s32[]{:S(2)}) async-start(), calls=%async_computation.2 | async-start | bytes 5242880 | tf_op jit(solution)/shard_map/all_gather | solution.py:89
  73.3 6.2 %copy-start.6 = (f32[16,128,128]{1,0,2:T(8,128)}, f32[16,128,128]{1,0,2:T(8,128)S(1)}, u32[]{:S(2)}) copy-start(f32[16,128,128]{1,0,2:T(8,128)S(1)} %multiply_subtract_fusion) | copy-start | bytes 3145732
  73.4 6.2 %collective-permute-start.1 = (f32[4,16,128,1]{2,1,3,0:T(8,128)S(1)}, f32[4,16,128,1]{2,1,3,0:T(8,128)S(1)}, u32[]{:S(2)}, u32[]{:S(2)}) collective-permute-start(f32[4,16,128,1]{2,1,3,0:T(8,128)S(1)} %get-tuple-element.50), channel_id=1, source_target_pairs={{8,0},{16,8},{24,16},{9,1},{17,9},{25,17},{10,2},{18,10},{26,18},{... | collective-permute-start | bytes 98312 | tf_op jit(solution)/shard_map/ppermute | solution.py:23
  74.7 6.1 %collective-permute-start = (f32[4,16,128,1]{2,1,3,0:T(8,128)S(1)}, f32[4,16,128,1]{2,1,3,0:T(8,128)S(1)}, u32[]{:S(2)}, u32[]{:S(2)}) collective-permute-start(f32[4,16,128,1]{2,1,3,0:T(8,128)S(1)} %get-tuple-element.49), channel_id=1, source_target_pairs={{0,8},{8,16},{16,24},{1,9},{9,17},{17,25},{2,10},{10,18},{18,26},{... | collective-permute-start | bytes 98312 | tf_op jit(solution)/shard_map/ppermute | solution.py:22
  79.6 7.1 %copy-start = (f32[4,16,128,128]{2,1,3,0:T(8,128)}, f32[4,16,128,128]{2,1,3,0:T(8,128)S(1)}, u32[]{:S(2)}) copy-start(f32[4,16,128,128]{2,1,3,0:T(8,128)S(1)} %concatenate.45) | copy-start | bytes 12582916
  81.2 4.5 %collective-permute-start.3 = (f32[4,1,128,130]{2,1,3,0:T(1,128)S(1)}, f32[4,1,128,130]{2,1,3,0:T(1,128)S(1)}, u32[]{:S(2)}, u32[]{:S(2)}) collective-permute-start(f32[4,1,128,130]{2,1,3,0:T(1,128)S(1)} %get-tuple-element.38), channel_id=1, source_target_pairs={{4,0},{5,1},{6,2},{7,3},{12,8},{13,9},{14,10},{15,11},{20,16},{21,... | collective-permute-start | bytes 798728 | tf_op jit(solution)/shard_map/ppermute | solution.py:23
  82.5 4.2 collective-permute-start.2
  106.6 12.1 %collective-permute-start.5 = (f32[4,18,1,130]{3,0,2,1:T(4,128)S(1)}, f32[4,18,1,130]{3,0,2,1:T(4,128)S(1)}, u32[]{:S(2)}, u32[]{:S(2)}) collective-permute-start(f32[4,18,1,130]{3,0,2,1:T(4,128)S(1)} %copy.11), channel_id=1, source_target_pairs={{1,0},{2,1},{3,2},{5,4},{6,5},{7,6},{9,8},{10,9},{11,10},{13,12},{... | collective-permute-start | bytes 112328 | tf_op jit(solution)/shard_map/ppermute | solution.py:23
  113.7 10.4 %collective-permute-start.4 = (f32[4,18,1,130]{3,0,2,1:T(4,128)S(1)}, f32[4,18,1,130]{3,0,2,1:T(4,128)S(1)}, u32[]{:S(2)}, u32[]{:S(2)}) collective-permute-start(f32[4,18,1,130]{3,0,2,1:T(4,128)S(1)} %copy.9), channel_id=1, source_target_pairs={{0,1},{1,2},{2,3},{4,5},{5,6},{6,7},{8,9},{9,10},{10,11},{12,13},{... | collective-permute-start | bytes 112328 | tf_op jit(solution)/shard_map/ppermute | solution.py:22
  129.5 4.2 copy-start.1
  129.5 5.4 %copy-start.2 = (f32[4,18,1,130]{2,1,3,0:T(8,128)S(1)}, f32[4,18,1,130]{2,1,3,0:T(8,128)}, u32[]{:S(2)}) copy-start(f32[4,18,1,130]{2,1,3,0:T(8,128)} %copy.10) | copy-start | bytes 112324
  145.7 4.1 copy-start.7
  158.1 14.1 %copy-start.5 = (f32[1,16,128,128]{2,1,3,0:T(8,128)}, f32[1,16,128,128]{2,1,3,0:T(8,128)S(1)}, u32[]{:S(2)}) copy-start(f32[1,16,128,128]{2,1,3,0:T(8,128)S(1)} %get-tuple-element.48) | copy-start | bytes 3145732
  158.1 6.2 %collective-permute-start.7 = (f32[4,16,128,1]{2,1,3,0:T(8,128)S(1)}, f32[4,16,128,1]{2,1,3,0:T(8,128)S(1)}, u32[]{:S(2)}, u32[]{:S(2)}) collective-permute-start(f32[4,16,128,1]{2,1,3,0:T(8,128)S(1)} %get-tuple-element.42), channel_id=1, source_target_pairs={{8,0},{16,8},{24,16},{9,1},{17,9},{25,17},{10,2},{18,10},{26,18},{... | collective-permute-start | bytes 98312 | tf_op jit(solution)/shard_map/ppermute | solution.py:23
  159.4 6.4 %collective-permute-start.6 = (f32[4,16,128,1]{2,1,3,0:T(8,128)S(1)}, f32[4,16,128,1]{2,1,3,0:T(8,128)S(1)}, u32[]{:S(2)}, u32[]{:S(2)}) collective-permute-start(f32[4,16,128,1]{2,1,3,0:T(8,128)S(1)} %get-tuple-element.41), channel_id=1, source_target_pairs={{0,8},{8,16},{16,24},{1,9},{9,17},{17,25},{2,10},{10,18},{18,26},{... | collective-permute-start | bytes 98312 | tf_op jit(solution)/shard_map/ppermute | solution.py:22
  166.7 4.4 collective-permute-start.9
  168.0 4.2 collective-permute-start.8
  172.2 0.7 copy-start.17
  194.3 23.6 %collective-permute-start.11 = (f32[4,18,1,130]{3,0,2,1:T(4,128)}, f32[4,18,1,130]{3,0,2,1:T(4,128)}, u32[]{:S(2)}, u32[]{:S(2)}) collective-permute-start(f32[4,18,1,130]{3,0,2,1:T(4,128)} %copy.16), channel_id=1, source_target_pairs={{1,0},{2,1},{3,2},{5,4},{6,5},{7,6},{9,8},{10,9},{11,10},{13,12},{... | collective-permute-start | bytes 112328 | tf_op jit(solution)/shard_map/ppermute | solution.py:23
  201.9 22.1 %collective-permute-start.10 = (f32[4,18,1,130]{3,0,2,1:T(4,128)}, f32[4,18,1,130]{3,0,2,1:T(4,128)}, u32[]{:S(2)}, u32[]{:S(2)}) collective-permute-start(f32[4,18,1,130]{3,0,2,1:T(4,128)} %copy.14), channel_id=1, source_target_pairs={{0,1},{1,2},{2,3},{4,5},{5,6},{6,7},{8,9},{9,10},{10,11},{12,13},{... | collective-permute-start | bytes 112328 | tf_op jit(solution)/shard_map/ppermute | solution.py:22
  230.2 16.3 %copy-start.3 = (f32[4,18,1,130]{2,1,3,0:T(8,128)S(1)}, f32[4,18,1,130]{2,1,3,0:T(8,128)}, u32[]{:S(2)}) copy-start(f32[4,18,1,130]{2,1,3,0:T(8,128)} %copy.15) | copy-start | bytes 112324
  230.2 16.3 %copy-start.11 = (f32[4,18,1,130]{2,1,3,0:T(8,128)S(1)}, f32[4,18,1,130]{2,1,3,0:T(8,128)}, u32[]{:S(2)}) copy-start(f32[4,18,1,130]{2,1,3,0:T(8,128)} %copy.18) | copy-start | bytes 112324
  230.2 16.3 %copy-start.18 = (f32[4,1,128,130]{2,1,3,0:T(1,128)S(1)}, f32[4,1,128,130]{2,1,3,0:T(1,128)}, u32[]{:S(2)}) copy-start(f32[4,1,128,130]{2,1,3,0:T(1,128)} %copy-done.17) | copy-start | bytes 798724
  256.1 7.0 %copy-start.8 = (f32[16,128,128]{1,0,2:T(8,128)S(1)}, f32[16,128,128]{1,0,2:T(8,128)}, u32[]{:S(2)}) copy-start(f32[16,128,128]{1,0,2:T(8,128)} %copy-done.6) | copy-start | bytes 3145732
  256.1 7.0 %copy-start.14 = (f32[17,129,129]{1,0,2:T(8,128)S(1)}, f32[17,129,129]{1,0,2:T(8,128)}, u32[]{:S(2)}) copy-start(f32[17,129,129]{1,0,2:T(8,128)} %get-tuple-element.11) | copy-start | bytes 3394768
  256.1 7.0 %copy-start.16 = (f32[16,128,128]{1,0,2:T(8,128)S(1)}, f32[16,128,128]{1,0,2:T(8,128)}, u32[]{:S(2)}) copy-start(f32[16,128,128]{1,0,2:T(8,128)} %get-tuple-element.16) | copy-start | bytes 3145732
  270.0 15.0 %copy-start.9 = (f32[1,16,128,128]{2,1,3,0:T(8,128)}, f32[1,16,128,128]{2,1,3,0:T(8,128)S(1)}, u32[]{:S(2)}) copy-start(f32[1,16,128,128]{2,1,3,0:T(8,128)S(1)} %get-tuple-element.44) | copy-start | bytes 3145732
  270.0 15.0 %copy-start.10 = (f32[1,16,128,128]{2,1,3,0:T(8,128)}, f32[1,16,128,128]{2,1,3,0:T(8,128)S(1)}, u32[]{:S(2)}) copy-start(f32[1,16,128,128]{2,1,3,0:T(8,128)S(1)} %get-tuple-element.45) | copy-start | bytes 3145732
  270.0 7.0 %collective-permute-start.13 = (f32[4,16,128,1]{2,1,3,0:T(8,128)S(1)}, f32[4,16,128,1]{2,1,3,0:T(8,128)S(1)}, u32[]{:S(2)}, u32[]{:S(2)}) collective-permute-start(f32[4,16,128,1]{2,1,3,0:T(8,128)S(1)} %get-tuple-element.40), channel_id=1, source_target_pairs={{8,0},{16,8},{24,16},{9,1},{17,9},{25,17},{10,2},{18,10},{26,18},{... | collective-permute-start | bytes 98312 | tf_op jit(solution)/shard_map/ppermute | solution.py:23
  271.3 7.3 %collective-permute-start.12 = (f32[4,16,128,1]{2,1,3,0:T(8,128)S(1)}, f32[4,16,128,1]{2,1,3,0:T(8,128)S(1)}, u32[]{:S(2)}, u32[]{:S(2)}) collective-permute-start(f32[4,16,128,1]{2,1,3,0:T(8,128)S(1)} %get-tuple-element.39), channel_id=1, source_target_pairs={{0,8},{8,16},{16,24},{1,9},{9,17},{17,25},{2,10},{10,18},{18,26},{... | collective-permute-start | bytes 98312 | tf_op jit(solution)/shard_map/ppermute | solution.py:22
  279.4 4.4 collective-permute-start.15
  280.7 4.2 collective-permute-start.14
  284.9 0.7 copy-start.19
  307.1 23.8 %collective-permute-start.17 = (f32[4,18,1,130]{3,0,2,1:T(4,128)}, f32[4,18,1,130]{3,0,2,1:T(4,128)}, u32[]{:S(2)}, u32[]{:S(2)}) collective-permute-start(f32[4,18,1,130]{3,0,2,1:T(4,128)} %copy.21), channel_id=1, source_target_pairs={{1,0},{2,1},{3,2},{5,4},{6,5},{7,6},{9,8},{10,9},{11,10},{13,12},{... | collective-permute-start | bytes 112328 | tf_op jit(solution)/shard_map/ppermute | solution.py:23
  314.7 22.3 %collective-permute-start.16 = (f32[4,18,1,130]{3,0,2,1:T(4,128)}, f32[4,18,1,130]{3,0,2,1:T(4,128)}, u32[]{:S(2)}, u32[]{:S(2)}) collective-permute-start(f32[4,18,1,130]{3,0,2,1:T(4,128)} %copy.19), channel_id=1, source_target_pairs={{0,1},{1,2},{2,3},{4,5},{5,6},{6,7},{8,9},{9,10},{10,11},{12,13},{... | collective-permute-start | bytes 112328 | tf_op jit(solution)/shard_map/ppermute | solution.py:22
  343.2 16.2 %copy-start.4 = (f32[4,18,1,130]{2,1,3,0:T(8,128)S(1)}, f32[4,18,1,130]{2,1,3,0:T(8,128)}, u32[]{:S(2)}) copy-start(f32[4,18,1,130]{2,1,3,0:T(8,128)} %copy.20) | copy-start | bytes 112324
  343.2 16.2 %copy-start.12 = (f32[4,18,1,130]{2,1,3,0:T(8,128)S(1)}, f32[4,18,1,130]{2,1,3,0:T(8,128)}, u32[]{:S(2)}) copy-start(f32[4,18,1,130]{2,1,3,0:T(8,128)} %copy.23) | copy-start | bytes 112324
  343.2 16.2 %copy-start.20 = (f32[4,1,128,130]{2,1,3,0:T(1,128)S(1)}, f32[4,1,128,130]{2,1,3,0:T(1,128)}, u32[]{:S(2)}) copy-start(f32[4,1,128,130]{2,1,3,0:T(1,128)} %copy-done.19) | copy-start | bytes 798724
  368.9 5.1 %copy-start.13 = (f32[17,129,129]{1,0,2:T(8,128)S(1)}, f32[17,129,129]{1,0,2:T(8,128)}, u32[]{:S(2)}) copy-start(f32[17,129,129]{1,0,2:T(8,128)} %get-tuple-element.5) | copy-start | bytes 3394768
  368.9 5.1 %copy-start.15 = (f32[16,128,128]{1,0,2:T(8,128)S(1)}, f32[16,128,128]{1,0,2:T(8,128)}, u32[]{:S(2)}) copy-start(f32[16,128,128]{1,0,2:T(8,128)} %get-tuple-element.10) | copy-start | bytes 3145732
Sparse Core Ops, SparseCore 0:
  16.5 55.3 reduce-scatter.1
  376.8 55.8 all-gather.1
where the time goes:
time: 452 us; the launch traced here: 445 us
  other arithmetic  141 us (31%)
  local copies, waits for them, and re-layouts  121 us (27%)
  waiting for transfers between devices  117 us (26%)
  starting transfers between devices  51.5 us (11%)
  between operations  14.4 us (3%)
    all_gather x1, waiting for transfers between devices, body(): return lax.all_gather(primal, 'shot', axis=2, tiled=True)  56 us
    reduce_scatter x1, waiting for transfers between devices, body(): summed = lax.psum_scatter(signed, 'shot', scatter_dimension=2, tiled=True)  53.6 us
    slice x7, local copies, waits for them, and re-layouts, padded_2(): last = lax.slice_in_dim(x, length - width, length, axis=dim)  51.4 us
    concatenate x5, other arithmetic, padded_2(): x = jnp.concatenate([before, x, after], axis=dim)  44 us
    mul x6, other arithmetic, iterate(): qz, qx, qy = (qz * scale, qx * scale, qy * scale)  39.8 us
    ppermute x9, starting transfers between devices, padded_2(): before = lax.ppermute(last, axis, up)  39.8 us
    concatenate x2, other arithmetic, iterate(): stacked = jnp.concatenate([extrapolated[None], dual], axis=0)  21.7 us
    slice x3, local copies, waits for them, and re-layouts, padded_2(): first = lax.slice_in_dim(x, 0, width, axis=dim)  18.3 us
  transfers between devices with their start and end apart: 20, of which 8 were waited for; matrix products, arithmetic and copies ran while one was open for 13% of the time, Pallas kernels for 0%

commit v1 on v0

v1 whole, which is shorter than its diff:
```python
import functools

import jax
import jax.numpy as jnp
from jax import lax
from jax.experimental import pallas as pl
from jax.experimental.pallas import tpu as pltpu
from jax.sharding import PartitionSpec as P

ITERS = 3
HALO = 3
SIDE = 8
VMEM_LIMIT = 32 * 1024 * 1024

step_tau = 0.28
step_sigma = 0.28
radius = 0.3
rate = 0.5

keep_old = 1.0 / (1.0 + step_tau)
take_new = step_tau / (1.0 + step_tau)

PAIRS_X = [(0, 1), (1, 0), (2, 3), (3, 2)]
PAIRS_Y = [(0, 2), (2, 0), (1, 3), (3, 1)]


def swap_x(array):
    return lax.ppermute(array, "shot", PAIRS_X)


def swap_y(array):
    return lax.ppermute(array, "shot", PAIRS_Y)


def params():
    return pltpu.CompilerParams(vmem_limit_bytes=VMEM_LIMIT)


def tile_rows(rows):
    return slice(rows * SIDE, rows * SIDE + SIDE)


def prepare_kernel(place, sign_a, sign_b, grad_a, grad_b, out_a, out_b):
    out_a[0] = grad_a[0] * sign_a[...][None]
    out_b[0] = grad_b[0] * sign_b[...][None]


def prepare(place, sign, gradient, shares):
    _, planes, rows, cols = gradient.shape
    share, half, steps = (rows // shares, cols // 2, 2)
    part = planes // steps
    spec = pltpu.PrefetchScalarGridSpec(
        num_scalar_prefetch=1,
        grid=(2, steps),
        in_specs=[
            pl.BlockSpec((1, half), lambda i, z, place: (0, 0)),
            pl.BlockSpec((1, half), lambda i, z, place: (0, 1)),
            pl.BlockSpec((1, part, share, half), lambda i, z, place: (0, z, place[1 + i], 0)),
            pl.BlockSpec((1, part, share, half), lambda i, z, place: (0, z, place[3 - i], 1)),
        ],
        out_specs=[pl.BlockSpec((1, part, share, half), lambda i, z, place: (i, z, 0, 0))] * 2,
    )
    shape = jax.ShapeDtypeStruct((2, planes, share, half), jnp.float32)
    return pl.pallas_call(prepare_kernel, grid_spec=spec, out_shape=[shape] * 2, compiler_params=params())(
        place, sign, sign, gradient, gradient
    )


def relay_kernel(place, sign, grad, came, out):
    out[...] = grad[0] * sign[...][None] + came[0]


def relay(place, sign, gradient, came, which, side):
    _, planes, share, half = came.shape
    steps = 2
    part = planes // steps
    spec = pltpu.PrefetchScalarGridSpec(
        num_scalar_prefetch=1,
        grid=(steps,),
        in_specs=[
            pl.BlockSpec((1, half), lambda z, place: (0, side)),
            pl.BlockSpec((1, part, share, half), lambda z, place: (0, z, place[which], side)),
            pl.BlockSpec((1, part, share, half), lambda z, place: (1, z, 0, 0)),
        ],
        out_specs=pl.BlockSpec((part, share, half), lambda z, place: (z, 0, 0)),
    )
    return pl.pallas_call(
        relay_kernel,
        grid_spec=spec,
        out_shape=jax.ShapeDtypeStruct((planes, share, half), jnp.float32),
        compiler_params=params(),
    )(place, sign, gradient, came)


def settle_kernel(place, sign, grad, model, near_a, far_a, near_b, far_b, out):
    half = near_a.shape[3]
    own = grad[0] * sign[...][None]
    out[:, :, :half] = model[:, :, :half] - rate * (own[:, :, :half] + near_a[0] + far_a[...])
    out[:, :, half:] = model[:, :, half:] - rate * (own[:, :, half:] + near_b[0] + far_b[...])


def settle(place, sign, gradient, model, near_a, far_a, near_b, far_b):
    _, planes, share, half = near_a.shape
    cols, steps = (2 * half, 2)
    part = planes // steps
    near = pl.BlockSpec((1, part, share, half), lambda z, place: (0, z, 0, 0))
    far = pl.BlockSpec((part, share, half), lambda z, place: (z, 0, 0))
    spec = pltpu.PrefetchScalarGridSpec(
        num_scalar_prefetch=1,
        grid=(steps,),
        in_specs=[
            pl.BlockSpec((1, cols), lambda z, place: (0, 0)),
            pl.BlockSpec((1, part, share, cols), lambda z, place: (0, z, place[0], 0)),
            pl.BlockSpec((part, share, cols), lambda z, place: (z, place[0], 0)),
            near,
            far,
            near,
            far,
        ],
        out_specs=pl.BlockSpec((part, share, cols), lambda z, place: (z, 0, 0)),
    )
    return pl.pallas_call(
        settle_kernel,
        grid_spec=spec,
        out_shape=jax.ShapeDtypeStruct((planes, share, cols), jnp.float32),
        compiler_params=params(),
    )(place, sign, gradient, model, near_a, far_a, near_b, far_b)


def vary_kernel(total_z, total_x, where, mid, low, high, before, after, out_a, out_b, target, primal, ahead, dual):
    planes, rows, cols = target.shape
    share = mid.shape[1]
    half = cols // 2
    tiles = rows // SIDE
    shape = (SIDE, cols)
    own = planes - 2 * HALO

    def fill(p, source):
        target[p, 0:SIDE] = jnp.zeros(shape, jnp.float32)
        target[p, SIDE + share : rows] = jnp.zeros(shape, jnp.float32)
        target[p, SIDE : SIDE + share] = source
        target[p, SIDE - HALO : SIDE] = before[pl.ds(p * HALO, HALO), :]
        target[p, SIDE + share : SIDE + share + HALO] = after[pl.ds(p * HALO, HALO), :]

    for p in range(HALO):
        fill(p, low[p])
        fill(HALO + own + p, high[p])
    for p in range(own):
        fill(HALO + p, mid[p])

    row = lax.broadcasted_iota(jnp.int32, shape, 0)
    col = lax.broadcasted_iota(jnp.int32, shape, 1)
    first_row, last_row = (row == 0, row == SIDE - 1)
    coef_y = jnp.where(col < cols - 1, jnp.float32(step_sigma), jnp.float32(0))
    start_z, start_x = (where[0], where[1])

    def coef_x(t):
        place = start_x - SIDE + t * SIDE + row
        return jnp.where((place >= 0) & (place <= total_x - 2), jnp.float32(step_sigma), jnp.float32(0))

    edge_x = {t: coef_x(t) for t in (0, (SIDE + share) // SIDE - 1)}

    for step in range(ITERS):
        source = target if step == 0 else ahead
        old = target if step == 0 else primal

        def plane(p, carry):
            place = start_z - HALO + p
            coef_z = jnp.where((place >= 0) & (place <= total_z - 2), jnp.float32(step_sigma), jnp.float32(0))
            tile = [source[p, tile_rows(t)] for t in range(tiles)]
            turned = [pltpu.roll(v, SIDE - 1, 0) for v in tile]
            turned.append(turned[0])
            last_x = None
            for t in range(tiles):
                here = tile_rows(t)
                v = tile[t]
                step_z = coef_z * (source[p + 1, here] - v)
                step_x = edge_x.get(t, jnp.float32(step_sigma)) * (jnp.where(last_row, turned[t + 1], turned[t]) - v)
                step_y = coef_y * (pltpu.roll(v, cols - 1, 1) - v)
                if step > 0:
                    step_z = step_z + dual[0, p, here]
                    step_x = step_x + dual[1, p, here]
                    step_y = step_y + dual[2, p, here]
                square = step_z * step_z + step_x * step_x + step_y * step_y
                scale = jnp.minimum(jnp.float32(1), jnp.float32(radius) * lax.rsqrt(square))
                step_z, step_x, step_y = (step_z * scale, step_x * scale, step_y * scale)
                dual[0, p, here] = step_z
                if step < ITERS - 1:
                    dual[1, p, here] = step_x
                    dual[2, p, here] = step_y
                moved = pltpu.roll(step_x, 1, 0)
                if last_x is None:
                    last_x = moved
                diverge = (
                    (step_z - dual[0, jnp.maximum(p - 1, 0), here])
                    + (step_x - jnp.where(first_row, last_x, moved))
                    + (step_y - pltpu.roll(step_y, 1, 1))
                )
                last_x = moved
                before_it = old[p, here]
                fresh = jnp.float32(keep_old) * before_it + jnp.float32(take_new) * (diverge + target[p, here])
                if step < ITERS - 1:
                    primal[p, here] = fresh
                    ahead[p, here] = 2.0 * fresh - before_it
                elif 1 <= t < tiles - 1:
                    spot = jnp.maximum(p - HALO, 0)
                    there = tile_rows(t - 1)
                    out_a[spot, there] = fresh[:, :half]
                    out_b[spot, there] = fresh[:, half:]
            return carry

        lax.fori_loop(step, planes - 1 - step, plane, 0)


def vary(where, mid, low, high, before, after, total_z, total_x):
    own, share, cols = mid.shape
    planes, rows = (own + 2 * HALO, share + 2 * SIDE)
    whole = pl.BlockSpec(memory_space=pltpu.VMEM)
    shape = jax.ShapeDtypeStruct((own, share, cols // 2), jnp.float32)
    field = pltpu.VMEM((planes, rows, cols), jnp.float32)
    return pl.pallas_call(
        functools.partial(vary_kernel, total_z, total_x),
        in_specs=[pl.BlockSpec(memory_space=pltpu.SMEM)] + [whole] * 5,
        out_specs=[whole] * 2,
        out_shape=[shape] * 2,
        scratch_shapes=[field, field, field, pltpu.VMEM((3, planes, rows, cols), jnp.float32)],
        compiler_params=params(),
    )(where, mid, low, high, before, after)


def gather_kernel(place, own_a, own_b, x_a, x_b, y_a, y_b, far_a, far_b, out, sems):
    share, half = own_a.shape[1:]
    copies = []
    for which, (left, right) in enumerate(((own_a, own_b), (x_a, x_b), (far_a, far_b), (y_a, y_b))):
        rows = pl.ds(pl.multiple_of(place[which] * share, share), share)
        copies.append(pltpu.make_async_copy(left, out.at[:, rows, pl.ds(0, half)], sems.at[2 * which]))
        copies.append(pltpu.make_async_copy(right, out.at[:, rows, pl.ds(half, half)], sems.at[2 * which + 1]))
    for copy in copies:
        copy.start()
    for copy in copies:
        copy.wait()


def gather(place, shares, *pieces):
    planes, share, half = pieces[0].shape
    anywhere = pl.BlockSpec(memory_space=pl.ANY)
    return pl.pallas_call(
        gather_kernel,
        in_specs=[pl.BlockSpec(memory_space=pltpu.SMEM)] + [anywhere] * 8,
        out_specs=anywhere,
        out_shape=jax.ShapeDtypeStruct((planes, shares * share, 2 * half), jnp.float32),
        scratch_shapes=[pltpu.SemaphoreType.DMA((8,))],
        compiler_params=params(),
    )(place, *pieces)


def gray(place):
    return place ^ (place >> 1)


def body(gradient, signs, model):
    shares, lines, layers = (lax.axis_size(name) for name in ("shot", "inline", "depth"))
    planes, rows, cols = model.shape
    share = rows // shares
    total_z, total_x = (planes * layers, rows * lines)
    shot = lax.axis_index("shot")
    at = gray(shot)
    place = jnp.stack([at, at ^ 1, at ^ 2, at ^ 3]).astype(jnp.int32)
    start_z = lax.axis_index("depth") * planes
    start_x = lax.axis_index("inline") * rows + at * share
    where = jnp.stack([start_z, start_x]).astype(jnp.int32)
    sign = (2 * signs - 1).astype(jnp.float32)

    order = [gray(spot) * lines + line for line in range(lines) for spot in range(shares)]
    ahead_x = list(zip(order[:-1], order[1:]))
    back_x = [(j, i) for i, j in ahead_x]
    ahead_z = [(i, i + 1) for i in range(layers - 1)]
    back_z = [(j, i) for i, j in ahead_z]

    send_a, send_b = prepare(place, sign, gradient, shares)
    near_a, near_b = (swap_x(send_a), swap_y(send_b))
    far_a = swap_y(relay(place, sign, gradient, near_a, 3, 0))
    far_b = swap_x(relay(place, sign, gradient, near_b, 1, 1))
    target = settle(place, sign, gradient, model, near_a, far_a, near_b, far_b)

    low = lax.ppermute(target[planes - HALO :], "depth", ahead_z)
    high = lax.ppermute(target[:HALO], "depth", back_z)
    tops = jnp.concatenate([part[:, share - HALO :].reshape(-1, cols) for part in (low, target, high)], axis=0)
    feet = jnp.concatenate([part[:, :HALO].reshape(-1, cols) for part in (low, target, high)], axis=0)
    before = lax.ppermute(tops, ("shot", "inline"), ahead_x)
    after = lax.ppermute(feet, ("shot", "inline"), back_x)
    own_a, own_b = vary(where, target, low, high, before, after, total_z, total_x)

    y_a, x_b = (swap_y(own_a), swap_x(own_b))
    y_b, x_a = (swap_y(own_b), swap_x(own_a))
    far_a, far_b = (swap_x(y_a), swap_y(x_b))
    return gather(place, shares, own_a, own_b, x_a, x_b, y_a, y_b, far_a, far_b)


def solution(mesh):
    placed = (P("shot", "depth", "inline", None), P("shot", None), P("depth", "inline", None))
    return jax.shard_map(
        body, mesh=mesh, in_specs=placed, out_specs=P("depth", "inline", None), check_vma=False
    )
```

time: 452 us -> 116 us (0.26); the launches traced: 445 us -> 116 us
  other arithmetic: 141 us -> 0.87 us
  local copies, waits for them, and re-layouts: 121 us -> 2.46 us
  waiting for transfers between devices: 117 us -> 73 us
  starting transfers between devices: 51.5 us -> 21.7 us
  Pallas kernels: 0 us -> 17.6 us
  between operations: 14.4 us -> 0.19 us
    slice x10 -> x4, local copies, waits for them, and re-layouts: 69.7 us -> 0.11 us  [the longest x3 0.08 us: body(): part[:, :HALO].reshape(-1, cols)]
    concatenate x7 -> x2, other arithmetic: 65.7 us -> 0.04 us  [the longest x1 0.02 us: body(): jnp.concatenate([part[:, share - HALO:].reshape(-1, cols) for part in (lo...]
    ppermute x18 -> x14, waiting for transfers between devices: 7.66 us -> 73 us  [the longest x5 45.8 us: swap_x(): return lax.ppermute(array, 'shot', PAIRS_X)]
    all_gather x1 -> x0, waiting for transfers between devices: 56 us -> none  [body(): return lax.all_gather(primal, 'shot', axis=2, tiled=True)]
    reduce_scatter x1 -> x0, waiting for transfers between devices: 53.6 us -> none  [body(): summed = lax.psum_scatter(signed, 'shot', scatter_dimension=2, tiled=True)]
    mul x10 -> x0, other arithmetic: 44.3 us -> none  [the longest x6 39.8 us: iterate(): qz, qx, qy = (qz * scale, qx * scale, qy * scale)]
    ppermute x6 -> x0, local copies, waits for them, and re-layouts: 35.4 us -> none  [the longest x3 17.8 us: padded_2(): before = lax.ppermute(last, axis, up)]
    ppermute x18 -> x14, starting transfers between devices: 51.4 us -> 21.7 us  [the longest x5 6.67 us: swap_x(): return lax.ppermute(array, 'shot', PAIRS_X)]
  transfers between devices with their start and end apart: 20 -> 14, of which waited for: 8 -> 10; matrix products, arithmetic and copies ran while one was open for 13% -> 0% of each run, Pallas kernels for 0% -> 1%
where the time goes in v1:
time: 116 us
  waiting for transfers between devices  73 us (63%)
  starting transfers between devices  21.7 us (19%)
  Pallas kernels  17.6 us (15%)
  local copies, waits for them, and re-layouts  2.46 us (2%)
    ppermute x5, waiting for transfers between devices, swap_x(): return lax.ppermute(array, 'shot', PAIRS_X)  45.8 us
    ppermute x5, waiting for transfers between devices, swap_y(): return lax.ppermute(array, 'shot', PAIRS_Y)  19.8 us
    pallas_call x1, Pallas kernels, vary(): pl.pallas_call(functools.partial(vary_kernel, total_z, total_x), in_specs...  11.6 us
    ppermute x5, starting transfers between devices, swap_x(): return lax.ppermute(array, 'shot', PAIRS_X)  6.67 us
    ppermute x5, starting transfers between devices, swap_y(): return lax.ppermute(array, 'shot', PAIRS_Y)  6.02 us
    ppermute x1, waiting for transfers between devices, body(): after = lax.ppermute(feet, ('shot', 'inline'), back_x)  4.15 us
    ppermute x1, starting transfers between devices, body(): before = lax.ppermute(tops, ('shot', 'inline'), ahead_x)  3.42 us
    ppermute x1, starting transfers between devices, body(): low = lax.ppermute(target[planes - HALO:], 'depth', ahead_z)  3.05 us
  transfers between devices with their start and end apart: 14, of which 10 were waited for; matrix products, arithmetic and copies ran while one was open for 0% of the time, Pallas kernels for 1%

profile of v1, /device:TPU:0, one launch (start us, length us, event | category | flops | bytes accessed | tf_op | source)
XLA Modules:
  0.0 115.9 jit_solution(17094606120892274238)
XLA Ops:
  0.0 0.7 add_convert_fusion.sign_a.sign_b.sign
  0.7 0.1 pad_add_fusion.place
  0.8 0.0 copy-start
  0.8 2.2 %copy-done = f32[1,16,128,512]{3,2,1,0:T(8,128)S(1)} copy-done((f32[1,16,128,512]{3,2,1,0:T(8,128)S(1)}, f32[1,16,128,512]{3,2,1,0:T(8,128)}, u32[]{:S(2)}) %copy-start) | copy-done | bytes 4194328
  3.0 1.0 shard_map.37
  4.0 3.0 %collective-permute-start = (f32[2,16,32,256]{3,2,1,0:T(8,128)S(1)}, f32[2,16,32,256]{3,2,1,0:T(8,128)S(1)}, u32[]{:S(2)}, u32[]{:S(2)}) collective-permute-start(f32[2,16,32,256]{3,2,1,0:T(8,128)S(1)} %get-tuple-element.9), channel_id=1, source_target_pairs={{0,8},{8,0},{16,24},{24,16},{1,9},{9,1},{17,25},{25,17},{2,10},{10... | collective-permute-start | bytes 3145736 | tf_op jit(solution)/shard_map/ppermute | solution.py:28
  7.0 1.5 %collective-permute-start.2 = (f32[2,16,32,256]{3,2,1,0:T(8,128)S(1)}, f32[2,16,32,256]{3,2,1,0:T(8,128)S(1)}, u32[]{:S(2)}, u32[]{:S(2)}) collective-permute-start(f32[2,16,32,256]{3,2,1,0:T(8,128)S(1)} %get-tuple-element.10), channel_id=1, source_target_pairs={{0,16},{16,0},{8,24},{24,8},{1,17},{17,1},{9,25},{25,9},{2,18},{18... | collective-permute-start | bytes 3145736 | tf_op jit(solution)/shard_map/ppermute | solution.py:32
  8.5 21.6 %collective-permute-done.came.near_a = f32[2,16,32,256]{3,2,1,0:T(8,128)S(1)} collective-permute-done((f32[2,16,32,256]{3,2,1,0:T(8,128)S(1)}, f32[2,16,32,256]{3,2,1,0:T(8,128)S(1)}, u32[]{:S(2)}, u32[]{:S(2)}) %collective-permute-start) | collective-permute-done | bytes 1048608 | tf_op jit(solution)/shard_map/ppermute | solution.py:28
  30.1 0.7 shard_map.38
  30.8 0.0 copy-start.1
  30.9 1.8 %collective-permute-start.1 = (f32[16,32,256]{2,1,0:T(8,128)S(1)}, f32[16,32,256]{2,1,0:T(8,128)S(1)}, u32[]{:S(2)}, u32[]{:S(2)}) collective-permute-start(f32[16,32,256]{2,1,0:T(8,128)S(1)} %shard_map.38), channel_id=1, source_target_pairs={{0,16},{16,0},{8,24},{24,8},{1,17},{17,1},{9,25},{25,9},{2,18},{18... | collective-permute-start | bytes 1572872 | tf_op jit(solution)/shard_map/ppermute | solution.py:32
  32.7 0.0 collective-permute-done.2.came.near_b
  32.7 0.7 shard_map.39
  33.4 1.6 %collective-permute-start.3 = (f32[16,32,256]{2,1,0:T(8,128)S(1)}, f32[16,32,256]{2,1,0:T(8,128)S(1)}, u32[]{:S(2)}, u32[]{:S(2)}) collective-permute-start(f32[16,32,256]{2,1,0:T(8,128)S(1)} %shard_map.39), channel_id=1, source_target_pairs={{0,8},{8,0},{16,24},{24,16},{1,9},{9,1},{17,25},{25,17},{2,10},{10... | collective-permute-start | bytes 1572872 | tf_op jit(solution)/shard_map/ppermute | solution.py:28
  35.0 9.1 %collective-permute-done.1.far_a = f32[16,32,256]{2,1,0:T(8,128)S(1)} collective-permute-done((f32[16,32,256]{2,1,0:T(8,128)S(1)}, f32[16,32,256]{2,1,0:T(8,128)S(1)}, u32[]{:S(2)}, u32[]{:S(2)}) %collective-permute-start.1) | collective-permute-done | bytes 524320 | tf_op jit(solution)/shard_map/ppermute | solution.py:32
  44.0 2.0 %collective-permute-done.3.far_b = f32[16,32,256]{2,1,0:T(8,128)S(1)} collective-permute-done((f32[16,32,256]{2,1,0:T(8,128)S(1)}, f32[16,32,256]{2,1,0:T(8,128)S(1)}, u32[]{:S(2)}, u32[]{:S(2)}) %collective-permute-start.3) | collective-permute-done | bytes 524320 | tf_op jit(solution)/shard_map/ppermute | solution.py:28
  46.0 0.0 copy-done.1
  46.0 1.1 shard_map.40.mid
  47.1 1.3 %collective-permute-start.5 = (f32[3,32,512]{2,1,0:T(8,128)S(1)}, f32[3,32,512]{2,1,0:T(8,128)S(1)}, u32[]{:S(2)}, u32[]{:S(2)}) collective-permute-start(f32[3,32,512]{2,1,0:T(8,128)S(1)} %get-tuple-element.15), channel_id=1, source_target_pairs={{4,0},{5,1},{6,2},{7,3},{12,8},{13,9},{14,10},{15,11},{20,16},{21,... | collective-permute-start | bytes 589832 | tf_op jit(solution)/shard_map/ppermute | solution.py:287
  48.4 0.1 fusion
  48.4 0.1 reshape.22
  48.5 0.1 reshape.19
  48.6 3.0 %collective-permute-start.4 = (f32[3,32,512]{2,1,0:T(8,128)S(1)}, f32[3,32,512]{2,1,0:T(8,128)S(1)}, u32[]{:S(2)}, u32[]{:S(2)}) collective-permute-start(f32[3,32,512]{2,1,0:T(8,128)S(1)} %get-tuple-element.16), channel_id=1, source_target_pairs={{0,4},{1,5},{2,6},{3,7},{8,12},{9,13},{10,14},{11,15},{16,20},{17,... | collective-permute-start | bytes 589832 | tf_op jit(solution)/shard_map/ppermute | solution.py:286
  51.6 0.0 collective-permute-done.5.high
  51.7 1.0 collective-permute-done.4.low
  52.7 3.4 %collective-permute-start.6 = (f32[66,512]{1,0:T(8,128)S(1)}, f32[66,512]{1,0:T(8,128)S(1)}, u32[]{:S(2)}, u32[]{:S(2)}) collective-permute-start(f32[66,512]{1,0:T(8,128)S(1)} %pad_maximum_fusion), channel_id=1, source_target_pairs={{0,8},{8,24},{24,16},{16,1},{1,9},{9,25},{25,17},{17,2},{2,10},{10... | collective-permute-start | bytes 405512 | tf_op jit(solution)/shard_map/ppermute | solution.py:290
  56.2 1.3 %collective-permute-start.7 = (f32[66,512]{1,0:T(8,128)S(1)}, f32[66,512]{1,0:T(8,128)S(1)}, u32[]{:S(2)}, u32[]{:S(2)}) collective-permute-start(f32[66,512]{1,0:T(8,128)S(1)} %pad_maximum_fusion.1), channel_id=1, source_target_pairs={{8,0},{24,8},{16,24},{1,16},{9,1},{25,9},{17,25},{2,17},{10,2},{26... | collective-permute-start | bytes 405512 | tf_op jit(solution)/shard_map/ppermute | solution.py:291
  57.5 0.1 pad_add_fusion.1.where
  57.6 2.2 %collective-permute-done.6.before = f32[66,512]{1,0:T(8,128)S(1)} collective-permute-done((f32[66,512]{1,0:T(8,128)S(1)}, f32[66,512]{1,0:T(8,128)S(1)}, u32[]{:S(2)}, u32[]{:S(2)}) %collective-permute-start.6) | collective-permute-done | bytes 135200 | tf_op jit(solution)/shard_map/ppermute | solution.py:290
  59.8 4.1 %collective-permute-done.7.after = f32[66,512]{1,0:T(8,128)S(1)} collective-permute-done((f32[66,512]{1,0:T(8,128)S(1)}, f32[66,512]{1,0:T(8,128)S(1)}, u32[]{:S(2)}, u32[]{:S(2)}) %collective-permute-start.7) | collective-permute-done | bytes 135200 | tf_op jit(solution)/shard_map/ppermute | solution.py:291
  63.9 11.6 %shard_map.41 = (f32[16,32,256]{2,1,0:T(8,128)S(1)}, f32[16,32,256]{2,1,0:T(8,128)S(1)}) custom-call(s32[2]{0:T(128)S(1)} %pad_add_fusion.1.where, f32[16,32,512]{2,1,0:T(8,128)S(1)} %shard_map.40.mid, f32[3,32,512]{2,1,0:T(8,128)S(1)} %collective-permute-done.4.low, f32[3,32,512]{2,1,0:T(8,128)S(1)} %collective-permute-done.5.high, ...), custom_call_target="tpu_custom_call" | custom-call | tf_op jit(solution)/shard_map/pallas_call | solution.py:221
  75.5 2.5 %collective-permute-start.10 = (f32[16,32,256]{2,1,0:T(8,128)S(1)}, f32[16,32,256]{2,1,0:T(8,128)S(1)}, u32[]{:S(2)}, u32[]{:S(2)}) collective-permute-start(f32[16,32,256]{2,1,0:T(8,128)S(1)} %get-tuple-element.11.own_a), channel_id=1, source_target_pairs={{0,16},{16,0},{8,24},{24,8},{1,17},{17,1},{9,25},{25,9},{2,18},{18... | collective-permute-start | bytes 1572872 | tf_op jit(solution)/shard_map/ppermute | solution.py:32
  78.0 0.0 collective-permute-start.9
  78.0 2.0 %collective-permute-start.8 = (f32[16,32,256]{2,1,0:T(8,128)S(1)}, f32[16,32,256]{2,1,0:T(8,128)S(1)}, u32[]{:S(2)}, u32[]{:S(2)}) collective-permute-start(f32[16,32,256]{2,1,0:T(8,128)S(1)} %get-tuple-element.11.own_a), channel_id=1, source_target_pairs={{0,8},{8,0},{16,24},{24,16},{1,9},{9,1},{17,25},{25,17},{2,10},{10... | collective-permute-start | bytes 1572872 | tf_op jit(solution)/shard_map/ppermute | solution.py:28
  80.0 0.1 collective-permute-start.11
  80.1 10.7 %collective-permute-done.10.y_a = f32[16,32,256]{2,1,0:T(8,128)S(1)} collective-permute-done((f32[16,32,256]{2,1,0:T(8,128)S(1)}, f32[16,32,256]{2,1,0:T(8,128)S(1)}, u32[]{:S(2)}, u32[]{:S(2)}) %collective-permute-start.10) | collective-permute-done | bytes 524320 | tf_op jit(solution)/shard_map/ppermute | solution.py:32
  90.8 0.1 collective-permute-start.12
  90.9 1.9 %collective-permute-done.9.x_b = f32[16,32,256]{2,1,0:T(8,128)S(1)} collective-permute-done((f32[16,32,256]{2,1,0:T(8,128)S(1)}, f32[16,32,256]{2,1,0:T(8,128)S(1)}, u32[]{:S(2)}, u32[]{:S(2)}) %collective-permute-start.9) | collective-permute-done | bytes 524320 | tf_op jit(solution)/shard_map/ppermute | solution.py:28
  92.8 0.1 collective-permute-start.13
  92.9 11.2 %collective-permute-done.8.x_a = f32[16,32,256]{2,1,0:T(8,128)S(1)} collective-permute-done((f32[16,32,256]{2,1,0:T(8,128)S(1)}, f32[16,32,256]{2,1,0:T(8,128)S(1)}, u32[]{:S(2)}, u32[]{:S(2)}) %collective-permute-start.8) | collective-permute-done | bytes 524320 | tf_op jit(solution)/shard_map/ppermute | solution.py:28
  104.1 0.0 collective-permute-done.11.y_b
  104.1 9.2 %collective-permute-done.12.far_a = f32[16,32,256]{2,1,0:T(8,128)S(1)} collective-permute-done((f32[16,32,256]{2,1,0:T(8,128)S(1)}, f32[16,32,256]{2,1,0:T(8,128)S(1)}, u32[]{:S(2)}, u32[]{:S(2)}) %collective-permute-start.12) | collective-permute-done | bytes 524320 | tf_op jit(solution)/shard_map/ppermute | solution.py:28
  113.2 0.0 collective-permute-done.13.far_b
  113.2 2.6 %shard_map.42 = f32[16,128,512]{2,1,0:T(8,128)} custom-call(s32[4]{0:T(128)S(1)} %pad_add_fusion.place, f32[16,32,256]{2,1,0:T(8,128)S(1)} %get-tuple-element.11.own_a, f32[16,32,256]{2,1,0:T(8,128)S(1)} %get-tuple-element.12.own_b, f32[16,32,256]{2,1,0:T(8,128)S(1)} %collective-permute-done.8.x_a, f32[16,32,256]{2,1,0:T(8,128)S(1)} %collective-permute-done.9.x_b, ...), custom_call_target="tpu_custom_call" | custom-call | tf_op jit(solution)/shard_map/pallas_call | solution.py:247
  (9 shorter events, 0.1 us)
Async XLA Ops:
  0.8 2.2 %copy-start = (f32[1,16,128,512]{3,2,1,0:T(8,128)S(1)}, f32[1,16,128,512]{3,2,1,0:T(8,128)}, u32[]{:S(2)}) copy-start(f32[1,16,128,512]{3,2,1,0:T(8,128)} %grad.5) | copy-start | bytes 12582916
  4.0 26.2 %collective-permute-start = (f32[2,16,32,256]{3,2,1,0:T(8,128)S(1)}, f32[2,16,32,256]{3,2,1,0:T(8,128)S(1)}, u32[]{:S(2)}, u32[]{:S(2)}) collective-permute-start(f32[2,16,32,256]{3,2,1,0:T(8,128)S(1)} %get-tuple-element.9), channel_id=1, source_target_pairs={{0,8},{8,0},{16,24},{24,16},{1,9},{9,1},{17,25},{25,17},{2,10},{10... | collective-permute-start | bytes 3145736 | tf_op jit(solution)/shard_map/ppermute | solution.py:28
  7.0 25.7 %collective-permute-start.2 = (f32[2,16,32,256]{3,2,1,0:T(8,128)S(1)}, f32[2,16,32,256]{3,2,1,0:T(8,128)S(1)}, u32[]{:S(2)}, u32[]{:S(2)}) collective-permute-start(f32[2,16,32,256]{3,2,1,0:T(8,128)S(1)} %get-tuple-element.10), channel_id=1, source_target_pairs={{0,16},{16,0},{8,24},{24,8},{1,17},{17,1},{9,25},{25,9},{2,18},{18... | collective-permute-start | bytes 3145736 | tf_op jit(solution)/shard_map/ppermute | solution.py:32
  30.8 15.1 %copy-start.1 = (f32[16,128,512]{2,1,0:T(8,128)S(1)}, f32[16,128,512]{2,1,0:T(8,128)}, u32[]{:S(2)}) copy-start(f32[16,128,512]{2,1,0:T(8,128)} %model.1) | copy-start | bytes 12582916
  30.9 13.2 %collective-permute-start.1 = (f32[16,32,256]{2,1,0:T(8,128)S(1)}, f32[16,32,256]{2,1,0:T(8,128)S(1)}, u32[]{:S(2)}, u32[]{:S(2)}) collective-permute-start(f32[16,32,256]{2,1,0:T(8,128)S(1)} %shard_map.38), channel_id=1, source_target_pairs={{0,16},{16,0},{8,24},{24,8},{1,17},{17,1},{9,25},{25,9},{2,18},{18... | collective-permute-start | bytes 1572872 | tf_op jit(solution)/shard_map/ppermute | solution.py:32
  33.4 12.6 %collective-permute-start.3 = (f32[16,32,256]{2,1,0:T(8,128)S(1)}, f32[16,32,256]{2,1,0:T(8,128)S(1)}, u32[]{:S(2)}, u32[]{:S(2)}) collective-permute-start(f32[16,32,256]{2,1,0:T(8,128)S(1)} %shard_map.39), channel_id=1, source_target_pairs={{0,8},{8,0},{16,24},{24,16},{1,9},{9,1},{17,25},{25,17},{2,10},{10... | collective-permute-start | bytes 1572872 | tf_op jit(solution)/shard_map/ppermute | solution.py:28
  47.1 4.5 %collective-permute-start.5 = (f32[3,32,512]{2,1,0:T(8,128)S(1)}, f32[3,32,512]{2,1,0:T(8,128)S(1)}, u32[]{:S(2)}, u32[]{:S(2)}) collective-permute-start(f32[3,32,512]{2,1,0:T(8,128)S(1)} %get-tuple-element.15), channel_id=1, source_target_pairs={{4,0},{5,1},{6,2},{7,3},{12,8},{13,9},{14,10},{15,11},{20,16},{21,... | collective-permute-start | bytes 589832 | tf_op jit(solution)/shard_map/ppermute | solution.py:287
  48.6 4.1 %collective-permute-start.4 = (f32[3,32,512]{2,1,0:T(8,128)S(1)}, f32[3,32,512]{2,1,0:T(8,128)S(1)}, u32[]{:S(2)}, u32[]{:S(2)}) collective-permute-start(f32[3,32,512]{2,1,0:T(8,128)S(1)} %get-tuple-element.16), channel_id=1, source_target_pairs={{0,4},{1,5},{2,6},{3,7},{8,12},{9,13},{10,14},{11,15},{16,20},{17,... | collective-permute-start | bytes 589832 | tf_op jit(solution)/shard_map/ppermute | solution.py:286
  52.7 7.0 %collective-permute-start.6 = (f32[66,512]{1,0:T(8,128)S(1)}, f32[66,512]{1,0:T(8,128)S(1)}, u32[]{:S(2)}, u32[]{:S(2)}) collective-permute-start(f32[66,512]{1,0:T(8,128)S(1)} %pad_maximum_fusion), channel_id=1, source_target_pairs={{0,8},{8,24},{24,16},{16,1},{1,9},{9,25},{25,17},{17,2},{2,10},{10... | collective-permute-start | bytes 405512 | tf_op jit(solution)/shard_map/ppermute | solution.py:290
  56.2 7.7 %collective-permute-start.7 = (f32[66,512]{1,0:T(8,128)S(1)}, f32[66,512]{1,0:T(8,128)S(1)}, u32[]{:S(2)}, u32[]{:S(2)}) collective-permute-start(f32[66,512]{1,0:T(8,128)S(1)} %pad_maximum_fusion.1), channel_id=1, source_target_pairs={{8,0},{24,8},{16,24},{1,16},{9,1},{25,9},{17,25},{2,17},{10,2},{26... | collective-permute-start | bytes 405512 | tf_op jit(solution)/shard_map/ppermute | solution.py:291
  75.5 15.3 %collective-permute-start.10 = (f32[16,32,256]{2,1,0:T(8,128)S(1)}, f32[16,32,256]{2,1,0:T(8,128)S(1)}, u32[]{:S(2)}, u32[]{:S(2)}) collective-permute-start(f32[16,32,256]{2,1,0:T(8,128)S(1)} %get-tuple-element.11.own_a), channel_id=1, source_target_pairs={{0,16},{16,0},{8,24},{24,8},{1,17},{17,1},{9,25},{25,9},{2,18},{18... | collective-permute-start | bytes 1572872 | tf_op jit(solution)/shard_map/ppermute | solution.py:32
  78.0 14.9 %collective-permute-start.9 = (f32[16,32,256]{2,1,0:T(8,128)S(1)}, f32[16,32,256]{2,1,0:T(8,128)S(1)}, u32[]{:S(2)}, u32[]{:S(2)}) collective-permute-start(f32[16,32,256]{2,1,0:T(8,128)S(1)} %get-tuple-element.12.own_b), channel_id=1, source_target_pairs={{0,8},{8,0},{16,24},{24,16},{1,9},{9,1},{17,25},{25,17},{2,10},{10... | collective-permute-start | bytes 1572872 | tf_op jit(solution)/shard_map/ppermute | solution.py:28
  78.0 26.1 %collective-permute-start.8 = (f32[16,32,256]{2,1,0:T(8,128)S(1)}, f32[16,32,256]{2,1,0:T(8,128)S(1)}, u32[]{:S(2)}, u32[]{:S(2)}) collective-permute-start(f32[16,32,256]{2,1,0:T(8,128)S(1)} %get-tuple-element.11.own_a), channel_id=1, source_target_pairs={{0,8},{8,0},{16,24},{24,16},{1,9},{9,1},{17,25},{25,17},{2,10},{10... | collective-permute-start | bytes 1572872 | tf_op jit(solution)/shard_map/ppermute | solution.py:28
  80.0 24.1 %collective-permute-start.11 = (f32[16,32,256]{2,1,0:T(8,128)S(1)}, f32[16,32,256]{2,1,0:T(8,128)S(1)}, u32[]{:S(2)}, u32[]{:S(2)}) collective-permute-start(f32[16,32,256]{2,1,0:T(8,128)S(1)} %get-tuple-element.12.own_b), channel_id=1, source_target_pairs={{0,16},{16,0},{8,24},{24,8},{1,17},{17,1},{9,25},{25,9},{2,18},{18... | collective-permute-start | bytes 1572872 | tf_op jit(solution)/shard_map/ppermute | solution.py:32
  90.8 22.4 %collective-permute-start.12 = (f32[16,32,256]{2,1,0:T(8,128)S(1)}, f32[16,32,256]{2,1,0:T(8,128)S(1)}, u32[]{:S(2)}, u32[]{:S(2)}) collective-permute-start(f32[16,32,256]{2,1,0:T(8,128)S(1)} %collective-permute-done.10.y_a), channel_id=1, source_target_pairs={{0,8},{8,0},{16,24},{24,16},{1,9},{9,1},{17,25},{25,17},{2,10},{10... | collective-permute-start | bytes 1572872 | tf_op jit(solution)/shard_map/ppermute | solution.py:28
  92.8 20.4 %collective-permute-start.13 = (f32[16,32,256]{2,1,0:T(8,128)S(1)}, f32[16,32,256]{2,1,0:T(8,128)S(1)}, u32[]{:S(2)}, u32[]{:S(2)}) collective-permute-start(f32[16,32,256]{2,1,0:T(8,128)S(1)} %collective-permute-done.9.x_b), channel_id=1, source_target_pairs={{0,16},{16,0},{8,24},{24,8},{1,17},{17,1},{9,25},{25,9},{2,18},{18... | collective-permute-start | bytes 1572872 | tf_op jit(solution)/shard_map/ppermute | solution.py:32

commit v2 on v0

v2 whole, which is shorter than its diff:
```python
import functools

import jax
import jax.numpy as jnp
from jax import lax
from jax.experimental import pallas as pl
from jax.experimental.pallas import tpu as pltpu
from jax.sharding import PartitionSpec as P

ITERS = 3
HALO = 3
SIDE = 8
VMEM_LIMIT = 16 * 1024 * 1024

step_tau = 0.28
step_sigma = 0.28
radius = 0.3
rate = 0.5

keep_old = 1.0 / (1.0 + step_tau)
take_new = step_tau / (1.0 + step_tau)

PAIRS_X = [(0, 1), (1, 0), (2, 3), (3, 2)]
PAIRS_Y = [(0, 2), (2, 0), (1, 3), (3, 1)]
PAIRS_FAR = [(0, 3), (3, 0), (1, 2), (2, 1)]


def swap_x(array):
    return lax.ppermute(array, "shot", PAIRS_X)


def swap_y(array):
    return lax.ppermute(array, "shot", PAIRS_Y)


def swap_far(array):
    return lax.ppermute(array, "shot", PAIRS_FAR)


def params():
    return pltpu.CompilerParams(vmem_limit_bytes=VMEM_LIMIT)


COST = pl.CostEstimate(flops=1, bytes_accessed=1, transcendentals=0)
HUGE = pl.CostEstimate(flops=1, bytes_accessed=1_000_000_000, transcendentals=0)
LONG = pl.CostEstimate(flops=1, bytes_accessed=100_000_000, transcendentals=0)


def tile_rows(rows):
    return slice(rows * SIDE, rows * SIDE + SIDE)


WHOLE = pl.BlockSpec(memory_space=pltpu.VMEM)
SCALARS = pl.BlockSpec(memory_space=pltpu.SMEM)
ANYWHERE = pl.BlockSpec(memory_space=pl.ANY)
FLIP, START_Z, START_X = (4, 5, 6)


def turn(flip, offset, count, total):
    return jnp.where(flip == 1, total - offset - count, offset)


def factor(signs):
    return (2 * signs[...] - 1).astype(jnp.float32)


def share_rows(spot, which, share):
    return pl.ds(pl.multiple_of(spot[which] * share, share), share)


def chunk_planes(spot, chunk, planes):
    offset, count = chunk
    return pl.ds(turn(spot[FLIP], offset, count, planes), count)


def fetch(source, spot, chunk, which, side, into, sem):
    planes, share, width = (source.shape[-3], into.shape[-2], into.shape[-1])
    place = (chunk_planes(spot, chunk, planes), share_rows(spot, which, share), pl.ds(side, width))
    if len(source.shape) == 4:
        place = (0,) + place
    copy = pltpu.make_async_copy(source.at[place], into, sem)
    copy.start()
    return copy


def prepare_kernel(chunk, after, spot, signs, gradient, *rest):
    out_a, out_b, held, held_signs, sems = rest[after:]
    half = out_a.shape[3]
    copy_signs = pltpu.make_async_copy(signs, held_signs, sems.at[4])
    copy_signs.start()
    todo = [(out_a, i, which, 0) for i, which in enumerate((1, 2))]
    todo += [(out_b, i, which, half) for i, which in enumerate((3, 2))]
    copies = [fetch(gradient, spot, chunk, which, side, held.at[n], sems.at[n]) for n, (_, _, which, side) in enumerate(todo)]
    copy_signs.wait()
    sign = factor(held_signs)[None]
    for n, (out, i, _, side) in enumerate(todo):
        copies[n].wait()
        out[i] = held[n] * sign[:, :, side : side + half]


def prepare(chunk, spot, signs, gradient, shares, after=()):
    rows, cols = gradient.shape[2:]
    shape = (2, chunk[1], rows // shares, cols // 2)
    return pl.pallas_call(
        functools.partial(prepare_kernel, chunk, len(after)),
        in_specs=[SCALARS] + [ANYWHERE] * (2 + len(after)),
        out_specs=[WHOLE] * 2,
        out_shape=[jax.ShapeDtypeStruct(shape, jnp.float32)] * 2,
        scratch_shapes=[
            pltpu.VMEM((4,) + shape[1:], jnp.float32),
            pltpu.VMEM(signs.shape, jnp.int32),
            pltpu.SemaphoreType.DMA((5,)),
        ],
        compiler_params=params(),
        cost_estimate=COST,
    )(spot, signs, gradient, *after)


def hold_kernel(chunks, after, spot, signs, gradient, model, *rest):
    fore_a, fore_b, base, held_a, held_b, held, held_signs, sems = rest[after:]
    half = fore_a.shape[2]
    copy_signs = pltpu.make_async_copy(signs, held_signs, sems.at[4 * len(chunks)])
    copy_signs.start()
    todo = []
    for chunk in chunks:
        here = pl.ds(*chunk)
        parts = ((gradient, 3, 0, held_a), (gradient, 1, half, held_b), (gradient, 0, 0, held.at[0]), (model, 0, 0, held.at[1]))
        copies = [
            fetch(source, spot, chunk, which, side, into.at[here], sems.at[len(todo) * 4 + n])
            for n, (source, which, side, into) in enumerate(parts)
        ]
        todo.append((copies, slice(chunk[0], chunk[0] + chunk[1])))
    copy_signs.wait()
    sign = factor(held_signs)[None]
    for copies, here in todo:
        for copy in copies:
            copy.wait()
        fore_a[here] = held_a[here] * sign[:, :, :half]
        fore_b[here] = held_b[here] * sign[:, :, half:]
        base[here] = held[1, here] - rate * (held[0, here] * sign)


def hold(chunks, spot, signs, gradient, model, shares, after=()):
    planes, rows, cols = model.shape
    whole = (planes, rows // shares, cols)
    part = (planes, rows // shares, cols // 2)
    return pl.pallas_call(
        functools.partial(hold_kernel, chunks, len(after)),
        in_specs=[SCALARS] + [ANYWHERE] * (3 + len(after)),
        out_specs=[WHOLE] * 3,
        out_shape=[pltpu.VMEM(shape, jnp.float32) for shape in (part, part, whole)],
        scratch_shapes=[
            pltpu.VMEM(part, jnp.float32),
            pltpu.VMEM(part, jnp.float32),
            pltpu.VMEM((2,) + whole, jnp.float32),
            pltpu.VMEM(signs.shape, jnp.int32),
            pltpu.SemaphoreType.DMA((4 * len(chunks) + 1,)),
        ],
        compiler_params=params(),
        cost_estimate=COST,
    )(spot, signs, gradient, model, *after)


def relay_kernel(chunk, ready, after, fore_a, fore_b, near_a, near_b, *rest):
    out_a, out_b = rest[ready + after :]
    at = 0
    if ready:
        at = rest[0].shape[0]
        out_a[:at] = rest[0][...]
        out_b[:at] = rest[1][...]
    here = slice(chunk[0], chunk[0] + chunk[1])
    out_a[at:] = fore_a[here] + near_a[1]
    out_b[at:] = fore_b[here] + near_b[1]


def relay(chunk, fores, near, ready=(), after=()):
    count = chunk[1] + sum(part.shape[0] for part in ready[:1])
    return pl.pallas_call(
        functools.partial(relay_kernel, chunk, len(ready), len(after)),
        in_specs=[WHOLE] * (4 + len(ready)) + [ANYWHERE] * len(after),
        out_specs=[WHOLE] * 2,
        out_shape=[jax.ShapeDtypeStruct((count,) + near[0].shape[2:], jnp.float32)] * 2,
        compiler_params=params(),
        cost_estimate=COST,
    )(*fores, *near, *ready, *after)


def settle_kernel(chunks, after, base, *refs):
    nears, (far_a, far_b) = (refs[: 2 * len(chunks)], refs[2 * len(chunks) : 2 * len(chunks) + 2])
    out = refs[-1]
    half = far_a.shape[2]
    at = 0
    for k, (start, count) in enumerate(chunks):
        here = slice(at, at + count)
        for side, near, far in ((slice(0, half), nears[2 * k], far_a), (slice(half, 2 * half), nears[2 * k + 1], far_b)):
            out[here, :, side] = base[start : start + count, :, side] - rate * (near[0] + far[here])
        at += count


def settle(chunks, base, nears, fars, after=()):
    count, share, half = fars[0].shape
    return pl.pallas_call(
        functools.partial(settle_kernel, chunks, len(after)),
        in_specs=[WHOLE] * (3 + len(nears)) + [ANYWHERE] * len(after),
        out_specs=WHOLE,
        out_shape=jax.ShapeDtypeStruct((count, share, 2 * half), jnp.float32),
        compiler_params=params(),
        cost_estimate=COST,
    )(base, *nears, *fars, *after)


def pack_kernel(count, *refs):
    parts, (tops, feet) = (refs[:count], refs[count:])
    at = 0
    for part in parts:
        for p in range(part.shape[0]):
            tops[at] = part[p, part.shape[1] - HALO :]
            feet[at] = part[p, :HALO]
            at += 1


def pack(parts):
    shape = (sum(part.shape[0] for part in parts), HALO, parts[0].shape[2])
    return pl.pallas_call(
        functools.partial(pack_kernel, len(parts)),
        in_specs=[WHOLE] * len(parts),
        out_specs=[WHOLE] * 2,
        out_shape=[jax.ShapeDtypeStruct(shape, jnp.float32)] * 2,
        compiler_params=params(),
        cost_estimate=COST,
    )(*parts)


def vary_kernel(span, pieces, sizes, counts, after, spot, *refs):
    fields, befores, afters = (refs[: counts[0]], refs[counts[0] : counts[0] + counts[1]], refs[counts[0] + counts[1] : counts[0] + 2 * counts[1]])
    out, target, primal, ahead, dual = refs[counts[0] + 2 * counts[1] + after :]
    planes, rows, cols = target.shape
    depth_planes, total_z, total_x = sizes
    share = rows - SIDE
    half = cols // 2
    tiles = share // SIDE
    shape = (SIDE, cols)
    flip = spot[FLIP]

    for field, held, offset, count, side, line, there, base in pieces:
        goes = turn(flip, there, count, planes)
        if field is None:
            for i in range(count):
                target[goes + i] = jnp.zeros((rows, cols), jnp.float32)
            continue
        comes = turn(flip, offset, count, held)
        for i in range(count):
            target[goes + i, :share] = fields[field][base + comes + i]
            target[goes + i, share:rows] = jnp.zeros(shape, jnp.float32)
            target[goes + i, share : share + HALO] = afters[side][line + comes + i]
            target[goes + i, rows - HALO : rows] = befores[side][line + comes + i]

    row = lax.broadcasted_iota(jnp.int32, shape, 0)
    col = lax.broadcasted_iota(jnp.int32, shape, 1)
    first_row, last_row = (row == 0, row == SIDE - 1)
    coef_y = jnp.where(col < cols - 1, jnp.float32(step_sigma), jnp.float32(0))
    start_x = spot[START_X]
    start_z = spot[START_Z] + turn(flip, span[0] - HALO, planes, depth_planes)

    def coef_x(place):
        return jnp.where((place >= 0) & (place <= total_x - 2), jnp.float32(step_sigma), jnp.float32(0))

    edge_x = {
        tiles - 1: coef_x(start_x + share - SIDE + row),
        tiles: coef_x(start_x + jnp.where(row < SIDE // 2, share + row, row - SIDE)),
    }

    for step in range(ITERS):
        source = target if step == 0 else ahead
        old = target if step == 0 else primal

        def plane(p, carry):
            place = start_z + p
            coef_z = jnp.where((place >= 0) & (place <= total_z - 2), jnp.float32(step_sigma), jnp.float32(0))
            tile = [source[p, tile_rows(t)] for t in range(tiles + 1)]
            turned = [pltpu.roll(v, SIDE - 1, 0) for v in tile]

            def steps_of(t):
                here = tile_rows(t)
                v = tile[t]
                beyond = turned[(t + 1) % (tiles + 1)]
                step_z = coef_z * (source[p + 1, here] - v)
                step_x = edge_x.get(t, jnp.float32(step_sigma)) * (jnp.where(last_row, beyond, turned[t]) - v)
                step_y = coef_y * (pltpu.roll(v, cols - 1, 1) - v)
                if step > 0:
                    step_z = step_z + dual[0, p, here]
                    step_x = step_x + dual[1, p, here]
                    step_y = step_y + dual[2, p, here]
                square = step_z * step_z + step_x * step_x + step_y * step_y
                scale = jnp.minimum(jnp.float32(1), jnp.float32(radius) * lax.rsqrt(square))
                step_z, step_x, step_y = (step_z * scale, step_x * scale, step_y * scale)
                dual[0, p, here] = step_z
                if step < ITERS - 1:
                    dual[1, p, here] = step_x
                    dual[2, p, here] = step_y
                return step_z, step_x, step_y, pltpu.roll(step_x, 1, 0)

            def renew(t, steps, last_x):
                here = tile_rows(t)
                step_z, step_x, step_y, moved = steps
                diverge = (
                    (step_z - dual[0, jnp.maximum(p - 1, 0), here])
                    + (step_x - jnp.where(first_row, last_x, moved))
                    + (step_y - pltpu.roll(step_y, 1, 1))
                )
                before_it = old[p, here]
                fresh = jnp.float32(keep_old) * before_it + jnp.float32(take_new) * (diverge + target[p, here])
                if step < ITERS - 1:
                    primal[p, here] = fresh
                    ahead[p, here] = 2.0 * fresh - before_it
                else:
                    place_out = jnp.maximum(p - HALO, 0)
                    out[0, place_out, here] = fresh[:, :half]
                    out[1, place_out, here] = fresh[:, half:]

            edge_steps = steps_of(tiles)
            last_x = edge_steps[3]
            for t in range(tiles):
                steps = steps_of(t)
                renew(t, steps, last_x)
                last_x = steps[3]
            if step < ITERS - 1:
                renew(tiles, edge_steps, last_x)
            return carry

        lax.fori_loop(step, planes - 1 - step, plane, 0)


def vary(span, pieces, sizes, spot, fields, befores, afters, after=()):
    _, share, cols = fields[0].shape
    planes, rows = (span[1] - span[0] + 2 * HALO, share + SIDE)
    field = pltpu.VMEM((planes, rows, cols), jnp.float32)
    counts = (len(fields), len(befores))
    return pl.pallas_call(
        functools.partial(vary_kernel, span, pieces, sizes, counts, len(after)),
        in_specs=[SCALARS] + [WHOLE] * (counts[0] + 2 * counts[1]) + [ANYWHERE] * len(after),
        out_specs=WHOLE,
        out_shape=jax.ShapeDtypeStruct((2, span[1] - span[0], share, cols // 2), jnp.float32),
        scratch_shapes=[field, field, field, pltpu.VMEM((3, planes, rows, cols), jnp.float32)],
        compiler_params=params(),
        cost_estimate=LONG,
    )(spot, *fields, *befores, *afters, *after)


def gather_kernel(span, parts, spot, *refs):
    out, sems = refs[-2:]
    layers = chunk_planes(spot, (span[0], span[1] - span[0]), out.shape[0])
    copies = []
    for ref, (which, sides) in zip(refs, parts):
        share, half = ref.shape[-2:]
        for n, side in enumerate(sides):
            there = out.at[layers, share_rows(spot, which, share), pl.ds(side * half, half)]
            source = ref.at[n] if len(ref.shape) == 4 else ref
            copies.append(pltpu.make_async_copy(source, there, sems.at[len(copies)]))
    for copy in copies:
        copy.start()
    for copy in copies:
        copy.wait()


def gather(span, spot, out_shape, pieces, so_far=None, cost=COST):
    before = [] if so_far is None else [so_far]
    arrays, parts = zip(*((array, (which, sides)) for array, which, sides in pieces))
    return pl.pallas_call(
        functools.partial(gather_kernel, span, parts),
        in_specs=[SCALARS] + [ANYWHERE] * (len(arrays) + len(before)),
        out_specs=pl.BlockSpec(memory_space=pltpu.HBM),
        out_shape=jax.ShapeDtypeStruct(out_shape, jnp.float32),
        input_output_aliases={1 + len(arrays): 0} if before else {},
        scratch_shapes=[pltpu.SemaphoreType.DMA((8,))],
        compiler_params=params(),
        cost_estimate=cost,
    )(spot, *arrays, *before)


def idle_kernel(*refs):
    pass


def idle(arrays, after):
    return pl.pallas_call(
        idle_kernel,
        in_specs=[ANYWHERE] * (len(arrays) + len(after)),
        out_specs=[ANYWHERE] * len(arrays),
        out_shape=[jax.ShapeDtypeStruct(array.shape, array.dtype) for array in arrays],
        input_output_aliases={i: i for i in range(len(arrays))},
        cost_estimate=COST,
    )(*arrays, *after)


def gray(place):
    return place ^ (place >> 1)


def spread(own):
    from_x, from_y = (swap_x(own), swap_y(own))
    far_a, far_b = (swap_x(from_y[0]), swap_y(from_x[1]))
    return ((own, 0, (0, 1)), (from_x, 1, (0, 1)), (far_a, 2, (0,)), (far_b, 2, (1,)), (from_y, 3, (0, 1)))


def spread_halves(own):
    y_a, x_b = (swap_y(own[0]), swap_x(own[1]))
    x_a, y_b = (swap_x(own[0]), swap_y(own[1]))
    far_a, far_b = (swap_x(y_a), swap_y(x_b))
    return (
        (own, 0, (0, 1)), (x_a, 1, (0,)), (x_b, 1, (1,)), (far_a, 2, (0,)), (far_b, 2, (1,)), (y_a, 3, (0,)), (y_b, 3, (1,))
    )


def spread_at_once(own):
    return ((own, 0, (0, 1)), (swap_x(own), 1, (0, 1)), (swap_far(own), 2, (0, 1)), (swap_y(own), 3, (0, 1)))


def body(gradient, signs, model):
    shares, lines, layers = (lax.axis_size(name) for name in ("shot", "inline", "depth"))
    planes, rows, cols = model.shape
    share = rows // shares
    sizes = (planes, planes * layers, rows * lines)
    paired = layers == 2
    at = gray(lax.axis_index("shot"))
    layer = lax.axis_index("depth")
    flip = (1 - layer) if paired else 0 * layer
    start_x = lax.axis_index("inline") * rows + at * share
    spot = jnp.stack([at, at ^ 1, at ^ 2, at ^ 3, flip, layer * planes, start_x]).astype(jnp.int32)

    order = [gray(place) * lines + line for line in range(lines) for place in range(shares)]
    ahead_x = list(zip(order[:-1], order[1:]))
    back_x = [(j, i) for i, j in ahead_x]
    ahead_z = [(i, i + 1) for i in range(layers - 1)]
    back_z = [(j, i) for i, j in ahead_z]

    def across(edges):
        tops, feet = edges
        group = ("shot", "inline")
        return lax.ppermute(tops, group, ahead_x), lax.ppermute(feet, group, back_x)

    gradient = pltpu.with_memory_space_constraint(gradient, pltpu.HBM)
    model = pltpu.with_memory_space_constraint(model, pltpu.HBM)
    signs = pltpu.with_memory_space_constraint(signs, pltpu.HBM)

    def both(a, b):
        return swap_x(a), swap_y(b)

    def crossed(a, b):
        return swap_y(a), swap_x(b)

    def prep(chunk, after=()):
        return prepare(chunk, spot, signs, gradient, shares, after)

    if not paired:
        c0 = (0, planes)
        sent = prep(c0)
        near = both(*sent)
        *fores, base = hold([c0], spot, signs, gradient, model, shares, sent)
        far = crossed(*relay(c0, fores, near))
        target = settle([c0], base, near, far)
        low = lax.ppermute(target[planes - HALO :], "depth", ahead_z)
        high = lax.ppermute(target[:HALO], "depth", back_z)
        before, after = across(pack((low, target, high)))
        pieces = [
            (0, HALO, 0, HALO, 0, 0, 0, 0),
            (1, planes, 0, planes, 0, HALO, HALO, 0),
            (2, HALO, 0, HALO, 0, HALO + planes, HALO + planes, 0),
        ]
        own = vary((0, planes), pieces, sizes, spot, (low, target, high), (before,), (after,))
        return gather((0, planes), spot, model.shape, spread(own))

    n0, n1 = ((7 * planes) // 16, planes // 4)
    n2 = planes - n0 - n1
    c0, c1, c2 = ((0, n0), (n0, n1), (n0 + n1, n2))
    sent_0 = prep(c0)
    near_0 = both(*sent_0)
    sent_1 = prep(c1, sent_0)
    near_1 = both(*sent_1)
    *fores, base = hold([c0, c1, c2], spot, signs, gradient, model, shares, sent_1)
    sent_2 = prep(c2, (base,))
    passed_0 = relay(c0, fores, near_0, after=sent_2)
    far_0 = crossed(*passed_0)
    passed_1 = relay(c1, fores, near_1, after=passed_0)
    near_2 = both(*idle(sent_2, passed_1))
    mid_0 = settle([c0], base, near_0, far_0, passed_1)
    edge = lax.dynamic_slice_in_dim(mid_0, turn(flip, 0, HALO, n0), HALO, 0)
    beside = lax.ppermute(edge, "depth", ahead_z + back_z)
    before_0, after_0 = across(pack((mid_0, beside)))
    passed_2 = relay(c2, fores, near_2, passed_1, (before_0, after_0))
    far_1 = crossed(*passed_2)
    mid_1 = settle([c1, c2], base, near_1 + near_2, far_1)
    before_1, after_1 = across(pack((mid_1,)))

    arrays = {"beside": beside, "mid_0": mid_0, "mid_1": mid_1}
    sides = [(before_0, after_0), (before_1, after_1)]
    held = [
        (-HALO, HALO, "beside", 0, 0, n0),
        (0, n0, "mid_0", 0, 0, 0),
        (n0, n1, "mid_1", 0, 1, 0),
        (n0 + n1, n2, "mid_1", n1, 1, n1),
        (planes, HALO, None, 0, 0, 0),
    ]

    def update(span, after=()):
        start, stop = (span[0] - HALO, span[1] + HALO)
        names, used, pieces = ([], [], [])
        for first, count, name, base, side, line in held:
            low, high = (max(first, start), min(first + count, stop))
            if low >= high:
                continue
            if name is not None:
                names += [name] if name not in names else []
                used += [side] if side not in used else []
            pieces.append((name, first, count, base, side, line, low, high))
        plan = []
        for name, first, count, base, side, line, low, high in pieces:
            if name is None:
                plan.append((None, 0, 0, high - low, 0, 0, low - start, 0))
            else:
                plan.append((names.index(name), count, low - first, high - low, used.index(side), line, low - start, base))
        return vary(
            span, plan, sizes, spot, [arrays[n] for n in names], [sides[i][0] for i in used], [sides[i][1] for i in used], after
        )

    m0 = n0 - HALO
    m1 = (m0 + planes) // 2
    spans = ((0, m0), (m0, m1), (m1, planes))
    own_0 = update(spans[0], passed_2)
    pieces_0 = spread(own_0)
    own_1 = update(spans[1], (own_0,))
    pieces_1 = spread(own_1)
    own_2 = update(spans[2], (own_1, pieces_0[1][0], pieces_0[4][0]))
    out = gather(spans[0], spot, model.shape, pieces_0)
    out = gather(spans[1], spot, model.shape, pieces_1, out)
    out = gather(spans[2], spot, model.shape, spread_halves(own_2), out)
    return out


def solution(mesh):
    placed = (P("shot", "depth", "inline", None), P("shot", None), P("depth", "inline", None))
    return jax.shard_map(
        body, mesh=mesh, in_specs=placed, out_specs=P("depth", "inline", None), check_vma=False
    )
```

time: 452 us -> 99.4 us (0.22); the launches traced: 445 us -> 99.1 us
  other arithmetic: 141 us -> 0 us
  local copies, waits for them, and re-layouts: 121 us -> 4.02 us
  waiting for transfers between devices: 117 us -> 16.9 us
  Pallas kernels: 0 us -> 34 us
  between operations: 14.4 us -> 0.28 us
  starting transfers between devices: 51.5 us -> 43.8 us
    slice x10 -> x0, local copies, waits for them, and re-layouts: 69.7 us -> none  [the longest x7 51.4 us: padded_2(): last = lax.slice_in_dim(x, length - width, length, axis=dim)]
    concatenate x7 -> x0, other arithmetic: 65.7 us -> none  [the longest x5 44 us: padded_2(): x = jnp.concatenate([before, x, after], axis=dim)]
    all_gather x1 -> x0, waiting for transfers between devices: 56 us -> none  [body(): return lax.all_gather(primal, 'shot', axis=2, tiled=True)]
    reduce_scatter x1 -> x0, waiting for transfers between devices: 53.6 us -> none  [body(): summed = lax.psum_scatter(signed, 'shot', scatter_dimension=2, tiled=True)]
    mul x10 -> x0, other arithmetic: 44.3 us -> none  [the longest x6 39.8 us: iterate(): qz, qx, qy = (qz * scale, qx * scale, qy * scale)]
    ppermute x6 -> x0, local copies, waits for them, and re-layouts: 35.4 us -> none  [the longest x3 17.8 us: padded_2(): before = lax.ppermute(last, axis, up)]
    pallas_call x0 -> x18, Pallas kernels: none -> 34 us  [the longest x3 15.9 us: vary(): pl.pallas_call(functools.partial(vary_kernel, span, pieces, sizes, counts...]
    broadcast_in_dim x2 -> x0, other arithmetic: 15.2 us -> none  [iterate(): stacked = jnp.concatenate([extrapolated[None], dual], axis=0)]
  transfers between devices with their start and end apart: 20 -> 29, of which waited for: 8 -> 14; matrix products, arithmetic and copies ran while one was open for 13% -> 0% of each run, Pallas kernels for 0% -> 31%
where the time goes in v2:
time: 99.4 us; the launch traced here: 99.1 us
  starting transfers between devices  43.8 us (44%)
  Pallas kernels  34 us (34%)
  waiting for transfers between devices  16.9 us (17%)
  local copies, waits for them, and re-layouts  4.02 us (4%)
    ppermute x12, starting transfers between devices, swap_y(): return lax.ppermute(array, 'shot', PAIRS_Y)  20.7 us
    pallas_call x3, Pallas kernels, vary(): pl.pallas_call(functools.partial(vary_kernel, span, pieces, sizes, counts...  15.9 us
    ppermute x12, starting transfers between devices, swap_x(): return lax.ppermute(array, 'shot', PAIRS_X)  11.5 us
    ppermute x2, starting transfers between devices, across(): lax.ppermute(tops, group, ahead_x)  8.94 us
    pallas_call x3, Pallas kernels, prepare(): pl.pallas_call(functools.partial(prepare_kernel, chunk, len(after)), in_s...  6.19 us
    ppermute x12, waiting for transfers between devices, swap_y(): return lax.ppermute(array, 'shot', PAIRS_Y)  5.78 us
    ppermute x12, waiting for transfers between devices, swap_x(): return lax.ppermute(array, 'shot', PAIRS_X)  5.49 us
    pallas_call x3, Pallas kernels, gather(): pl.pallas_call(functools.partial(gather_kernel, span, parts), in_specs=[S...  5.07 us
  transfers between devices with their start and end apart: 29, of which 14 were waited for; matrix products, arithmetic and copies ran while one was open for 0% of the time, Pallas kernels for 31%

profile of v2, /device:TPU:0, one launch (start us, length us, event | category | flops | bytes accessed | tf_op | source)
XLA Modules:
  0.0 99.1 jit_solution(1873207048302116702)
XLA Ops:
  0.1 1.9 %shard_map.37 = (f32[2,7,32,256]{3,2,1,0:T(8,128)S(1)}, f32[2,7,32,256]{3,2,1,0:T(8,128)S(1)}) custom-call(s32[7]{0:T(128)S(1)} %stack.31.spot, s32[1,512]{1,0:T(1,128)} %signs.7, f32[1,16,128,512]{3,2,1,0:T(8,128)} %gradient.7), custom_call_target="tpu_custom_call" | custom-call | flops 1 | bytes 1 | tf_op jit(solution)/shard_map/pallas_call | solution.py:104
  2.0 3.0 %collective-permute-start.2 = (f32[2,7,32,256]{3,2,1,0:T(8,128)S(1)}, f32[2,7,32,256]{3,2,1,0:T(8,128)S(1)}, u32[]{:S(2)}, u32[]{:S(2)}) collective-permute-start(f32[2,7,32,256]{3,2,1,0:T(8,128)S(1)} %get-tuple-element.26.rest_0_), channel_id=1, source_target_pairs={{0,8},{8,0},{16,24},{24,16},{1,9},{9,1},{17,25},{25,17},{2,10},{10... | collective-permute-start | bytes 1376264 | tf_op jit(solution)/shard_map/ppermute | solution.py:29
  5.0 1.5 %collective-permute-start.3 = (f32[2,7,32,256]{3,2,1,0:T(8,128)S(1)}, f32[2,7,32,256]{3,2,1,0:T(8,128)S(1)}, u32[]{:S(2)}, u32[]{:S(2)}) collective-permute-start(f32[2,7,32,256]{3,2,1,0:T(8,128)S(1)} %get-tuple-element.27.rest_1_), channel_id=1, source_target_pairs={{0,16},{16,0},{8,24},{24,8},{1,17},{17,1},{9,25},{25,9},{2,18},{18... | collective-permute-start | bytes 1376264 | tf_op jit(solution)/shard_map/ppermute | solution.py:33
  6.5 2.5 %shard_map.38 = (f32[2,4,32,256]{3,2,1,0:T(8,128)}, f32[2,4,32,256]{3,2,1,0:T(8,128)}) custom-call(s32[7]{0:T(128)S(1)} %stack.31.spot, s32[1,512]{1,0:T(1,128)} %signs.7, f32[1,16,128,512]{3,2,1,0:T(8,128)} %gradient.7, f32[2,7,32,256]{3,2,1,0:T(8,128)S(1)} %get-tuple-element.26.rest_0_, f32[2,7,32,256]{3,2,1,0:T(8,128)S(1)} %get-tuple-element.27.rest_1_), custom_call_target="tpu_custom_call" | custom-call | flops 1 | bytes 1 | tf_op jit(solution)/shard_map/pallas_call | solution.py:104
  9.0 0.6 collective-permute-start
  9.7 2.7 %shard_map.39 = (f32[16,32,256]{2,1,0:T(8,128)S(1)}, f32[16,32,256]{2,1,0:T(8,128)S(1)}, f32[16,32,512]{2,1,0:T(8,128)S(1)}) custom-call(s32[7]{0:T(128)S(1)} %stack.31.spot, s32[1,512]{1,0:T(1,128)} %signs.7, f32[1,16,128,512]{3,2,1,0:T(8,128)} %gradient.7, f32[16,128,512]{2,1,0:T(8,128)} %model.1, f32[2,4,32,256]{3,2,1,0:T(8,128)} %get-tuple-element.28.rest_0_, ...), custom_call_target="tpu_custom_call" | custom-call | flops 1 | bytes 1 | tf_op jit(solution)/shard_map/pallas_call | solution.py:147
  12.4 1.8 %shard_map.40 = (f32[2,5,32,256]{3,2,1,0:T(8,128)S(1)}, f32[2,5,32,256]{3,2,1,0:T(8,128)S(1)}) custom-call(s32[7]{0:T(128)S(1)} %stack.31.spot, s32[1,512]{1,0:T(1,128)} %signs.7, f32[1,16,128,512]{3,2,1,0:T(8,128)} %gradient.7, f32[16,32,512]{2,1,0:T(8,128)S(1)} %get-tuple-element.30.rest_0_.base), custom_call_target="tpu_custom_call" | custom-call | flops 1 | bytes 1 | tf_op jit(solution)/shard_map/pallas_call | solution.py:104
  14.2 2.2 %collective-permute-done.2.near_a.refs_0_ = f32[2,7,32,256]{3,2,1,0:T(8,128)S(1)} collective-permute-done((f32[2,7,32,256]{3,2,1,0:T(8,128)S(1)}, f32[2,7,32,256]{3,2,1,0:T(8,128)S(1)}, u32[]{:S(2)}, u32[]{:S(2)}) %collective-permute-start.2) | collective-permute-done | bytes 458784 | tf_op jit(solution)/shard_map/ppermute | solution.py:29
  16.4 2.1 %collective-permute-done.3.near_b.refs_1_ = f32[2,7,32,256]{3,2,1,0:T(8,128)S(1)} collective-permute-done((f32[2,7,32,256]{3,2,1,0:T(8,128)S(1)}, f32[2,7,32,256]{3,2,1,0:T(8,128)S(1)}, u32[]{:S(2)}, u32[]{:S(2)}) %collective-permute-start.3) | collective-permute-done | bytes 458784 | tf_op jit(solution)/shard_map/ppermute | solution.py:33
  18.4 0.8 shard_map.41
  19.3 0.7 copy-done.1
  20.0 1.5 %collective-permute-start.6 = (f32[7,32,256]{2,1,0:T(8,128)}, f32[7,32,256]{2,1,0:T(8,128)}, u32[]{:S(2)}, u32[]{:S(2)}) collective-permute-start(f32[7,32,256]{2,1,0:T(8,128)} %get-tuple-element.35.rest_0_), channel_id=1, source_target_pairs={{0,16},{16,0},{8,24},{24,8},{1,17},{17,1},{9,25},{25,9},{2,18},{18... | collective-permute-start | bytes 688136 | tf_op jit(solution)/shard_map/ppermute | solution.py:33
  22.1 2.1 %collective-permute-done.1.near_b.refs_1_ = f32[2,4,32,256]{3,2,1,0:T(8,128)} collective-permute-done((f32[2,4,32,256]{3,2,1,0:T(8,128)}, f32[2,4,32,256]{3,2,1,0:T(8,128)}, u32[]{:S(2)}, u32[]{:S(2)}) %collective-permute-start.1) | collective-permute-done | bytes 262176 | tf_op jit(solution)/shard_map/ppermute | solution.py:33
  24.2 1.1 %shard_map.42 = (f32[4,32,256]{2,1,0:T(8,128)S(1)}, f32[4,32,256]{2,1,0:T(8,128)S(1)}) custom-call(f32[16,32,256]{2,1,0:T(8,128)S(1)} %get-tuple-element.33.fore_a, f32[16,32,256]{2,1,0:T(8,128)S(1)} %get-tuple-element.34.fore_b, f32[2,4,32,256]{3,2,1,0:T(8,128)} %collective-permute-done.near_a.refs_0_, ...), custom_call_target="tpu_custom_call" | custom-call | flops 1 | bytes 1 | tf_op jit(solution)/shard_map/pallas_call | solution.py:178
  25.2 0.6 copy-done.2
  25.9 0.7 copy-done.4
  26.6 2.0 %collective-permute-start.5 = (f32[2,5,32,256]{3,2,1,0:T(8,128)}, f32[2,5,32,256]{3,2,1,0:T(8,128)S(1)}, u32[]{:S(2)}, u32[]{:S(2)}) collective-permute-start(f32[2,5,32,256]{3,2,1,0:T(8,128)} %get-tuple-element.40), channel_id=1, source_target_pairs={{0,16},{16,0},{8,24},{24,8},{1,17},{17,1},{9,25},{25,9},{2,18},{18... | collective-permute-start | bytes 983048 | tf_op jit(solution)/shard_map/ppermute | solution.py:33
  29.0 0.9 copy-done.3
  29.9 0.9 copy-done.5
  30.8 1.1 %shard_map.44.refs_0_.refs_1_ = f32[7,32,512]{2,1,0:T(8,128)S(1)} custom-call(f32[16,32,512]{2,1,0:T(8,128)S(1)} %get-tuple-element.30.rest_0_.base, f32[2,7,32,256]{3,2,1,0:T(8,128)S(1)} %collective-permute-done.2.near_a.refs_0_, f32[2,7,32,256]{3,2,1,0:T(8,128)S(1)} %collective-permute-done.3.near_b.refs_1_, f32[7,32,256]{2,1,0:T(8,128)} %collective-permute-done.6.refs_2_, ...), custom_call_target="tpu_custom_call" | custom-call | flops 1 | bytes 1 | tf_op jit(solution)/shard_map/pallas_call | solution.py:202
  32.1 1.4 %collective-permute-done.8.refs_1_.refs_0_ = f32[3,32,512]{2,1,0:T(8,128)S(1)} collective-permute-done((f32[3,32,512]{2,1,0:T(8,128)S(1)}, f32[3,32,512]{2,1,0:T(8,128)S(1)}, u32[]{:S(2)}, u32[]{:S(2)}) %collective-permute-start.8) | collective-permute-done | bytes 196640 | tf_op jit(solution)/shard_map/ppermute | solution.py:488
  33.5 1.3 %collective-permute-start.10 = (f32[10,3,512]{2,1,0:T(4,128)S(1)}, f32[10,3,512]{2,1,0:T(4,128)S(1)}, u32[]{:S(2)}, u32[]{:S(2)}) collective-permute-start(f32[10,3,512]{2,1,0:T(4,128)S(1)} %get-tuple-element.42), channel_id=1, source_target_pairs={{8,0},{24,8},{16,24},{1,16},{9,1},{25,9},{17,25},{2,17},{10,2},{26... | collective-permute-start | bytes 184328 | tf_op jit(solution)/shard_map/ppermute | solution.py:440
  34.8 4.6 %collective-permute-start.9 = (f32[10,3,512]{2,1,0:T(4,128)S(1)}, f32[10,3,512]{2,1,0:T(4,128)S(1)}, u32[]{:S(2)}, u32[]{:S(2)}) collective-permute-start(f32[10,3,512]{2,1,0:T(4,128)S(1)} %get-tuple-element.41), channel_id=1, source_target_pairs={{0,8},{8,24},{24,16},{16,1},{1,9},{9,25},{25,17},{17,2},{2,10},{10... | collective-permute-start | bytes 184328 | tf_op jit(solution)/shard_map/ppermute | solution.py:440
  39.9 1.5 %collective-permute-done.9.rest_2_.refs_2_ = f32[10,3,512]{2,1,0:T(4,128)S(1)} collective-permute-done((f32[10,3,512]{2,1,0:T(4,128)S(1)}, f32[10,3,512]{2,1,0:T(4,128)S(1)}, u32[]{:S(2)}, u32[]{:S(2)}) %collective-permute-start.9) | collective-permute-done | bytes 61472 | tf_op jit(solution)/shard_map/ppermute | solution.py:440
  41.5 2.0 %collective-permute-start.11 = (f32[9,32,256]{2,1,0:T(8,128)S(1)}, f32[9,32,256]{2,1,0:T(8,128)S(1)}, u32[]{:S(2)}, u32[]{:S(2)}) collective-permute-start(f32[9,32,256]{2,1,0:T(8,128)S(1)} %get-tuple-element.43.refs_4_), channel_id=1, source_target_pairs={{0,16},{16,0},{8,24},{24,8},{1,17},{17,1},{9,25},{25,9},{2,18},{18... | collective-permute-start | bytes 884744 | tf_op jit(solution)/shard_map/ppermute | solution.py:33
  43.5 1.5 %collective-permute-start.12 = (f32[9,32,256]{2,1,0:T(8,128)S(1)}, f32[9,32,256]{2,1,0:T(8,128)S(1)}, u32[]{:S(2)}, u32[]{:S(2)}) collective-permute-start(f32[9,32,256]{2,1,0:T(8,128)S(1)} %get-tuple-element.44.refs_5_), channel_id=1, source_target_pairs={{0,8},{8,0},{16,24},{24,16},{1,9},{9,1},{17,25},{25,17},{2,10},{10... | collective-permute-start | bytes 884744 | tf_op jit(solution)/shard_map/ppermute | solution.py:29
  45.0 4.5 %shard_map.49.refs_6_.refs_0_ = f32[2,4,32,256]{3,2,1,0:T(8,128)S(1)} custom-call(s32[7]{0:T(128)S(1)} %stack.31.spot, f32[3,32,512]{2,1,0:T(8,128)S(1)} %collective-permute-done.8.refs_1_.refs_0_, f32[7,32,512]{2,1,0:T(8,128)S(1)} %shard_map.44.refs_0_.refs_1_, f32[10,3,512]{2,1,0:T(4,128)S(1)} %collective-permute-done.9.rest_2_.refs_2_, ...), custom_call_target="tpu_custom_call" | custom-call | flops 1 | bytes 100000000 | tf_op jit(solution)/shard_map/pallas_call | solution.py:339
  49.5 1.0 %collective-permute-start.16 = (f32[2,4,32,256]{3,2,1,0:T(8,128)S(1)}, f32[2,4,32,256]{3,2,1,0:T(8,128)S(1)}, u32[]{:S(2)}, u32[]{:S(2)}) collective-permute-start(f32[2,4,32,256]{3,2,1,0:T(8,128)S(1)} %shard_map.49.refs_6_.refs_0_), channel_id=1, source_target_pairs={{0,16},{16,0},{8,24},{24,8},{1,17},{17,1},{9,25},{25,9},{2,18},{18... | collective-permute-start | bytes 786440 | tf_op jit(solution)/shard_map/ppermute | solution.py:33
  50.8 1.1 %shard_map.47.refs_0_.refs_1_ = f32[9,32,512]{2,1,0:T(8,128)S(1)} custom-call(f32[16,32,512]{2,1,0:T(8,128)S(1)} %get-tuple-element.30.rest_0_.base, f32[2,4,32,256]{3,2,1,0:T(8,128)} %collective-permute-done.near_a.refs_0_, f32[2,4,32,256]{3,2,1,0:T(8,128)} %collective-permute-done.1.near_b.refs_1_, ...), custom_call_target="tpu_custom_call" | custom-call | flops 1 | bytes 1 | tf_op jit(solution)/shard_map/pallas_call | solution.py:202
  52.0 4.4 %collective-permute-start.13 = (f32[9,3,512]{2,1,0:T(4,128)S(1)}, f32[9,3,512]{2,1,0:T(4,128)S(1)}, u32[]{:S(2)}, u32[]{:S(2)}) collective-permute-start(f32[9,3,512]{2,1,0:T(4,128)S(1)} %get-tuple-element.45), channel_id=1, source_target_pairs={{0,8},{8,24},{24,16},{16,1},{1,9},{9,25},{25,17},{17,2},{2,10},{10... | collective-permute-start | bytes 165896 | tf_op jit(solution)/shard_map/ppermute | solution.py:440
  56.4 1.3 %collective-permute-start.14 = (f32[9,3,512]{2,1,0:T(4,128)S(1)}, f32[9,3,512]{2,1,0:T(4,128)S(1)}, u32[]{:S(2)}, u32[]{:S(2)}) collective-permute-start(f32[9,3,512]{2,1,0:T(4,128)S(1)} %get-tuple-element.46), channel_id=1, source_target_pairs={{8,0},{24,8},{16,24},{1,16},{9,1},{25,9},{17,25},{2,17},{10,2},{26... | collective-permute-start | bytes 165896 | tf_op jit(solution)/shard_map/ppermute | solution.py:440
  57.7 2.7 %collective-permute-start.27 = (f32[4,32,256]{2,1,0:T(8,128)S(1)}, f32[4,32,256]{2,1,0:T(8,128)S(1)}, u32[]{:S(2)}, u32[]{:S(2)}) collective-permute-start(f32[4,32,256]{2,1,0:T(8,128)S(1)} %slice_bitcast_fusion.5), channel_id=1, source_target_pairs={{0,8},{8,0},{16,24},{24,16},{1,9},{9,1},{17,25},{25,17},{2,10},{10... | collective-permute-start | bytes 393224 | tf_op jit(solution)/shard_map/ppermute | solution.py:29
  60.4 2.2 %collective-permute-done.14.refs_5_.refs_2_ = f32[9,3,512]{2,1,0:T(4,128)S(1)} collective-permute-done((f32[9,3,512]{2,1,0:T(4,128)S(1)}, f32[9,3,512]{2,1,0:T(4,128)S(1)}, u32[]{:S(2)}, u32[]{:S(2)}) %collective-permute-start.14) | collective-permute-done | bytes 55328 | tf_op jit(solution)/shard_map/ppermute | solution.py:440
  62.6 5.7 %shard_map.50.refs_3_.refs_0_ = f32[2,6,32,256]{3,2,1,0:T(8,128)S(1)} custom-call(s32[7]{0:T(128)S(1)} %stack.31.spot, f32[7,32,512]{2,1,0:T(8,128)S(1)} %shard_map.44.refs_0_.refs_1_, f32[9,32,512]{2,1,0:T(8,128)S(1)} %shard_map.47.refs_0_.refs_1_, f32[10,3,512]{2,1,0:T(4,128)S(1)} %collective-permute-done.9.rest_2_.refs_2_, ...), custom_call_target="tpu_custom_call" | custom-call | flops 1 | bytes 100000000 | tf_op jit(solution)/shard_map/pallas_call | solution.py:339
  68.3 2.8 %collective-permute-start.24 = (f32[2,6,32,256]{3,2,1,0:T(8,128)S(1)}, f32[2,6,32,256]{3,2,1,0:T(8,128)S(1)}, u32[]{:S(2)}, u32[]{:S(2)}) collective-permute-start(f32[2,6,32,256]{3,2,1,0:T(8,128)S(1)} %shard_map.50.refs_3_.refs_0_), channel_id=1, source_target_pairs={{0,16},{16,0},{8,24},{24,8},{1,17},{17,1},{9,25},{25,9},{2,18},{18... | collective-permute-start | bytes 1179656 | tf_op jit(solution)/shard_map/ppermute | solution.py:33
  71.3 5.7 %shard_map.51.refs_0_ = f32[2,6,32,256]{3,2,1,0:T(8,128)S(1)} custom-call(s32[7]{0:T(128)S(1)} %stack.31.spot, f32[9,32,512]{2,1,0:T(8,128)S(1)} %shard_map.47.refs_0_.refs_1_, f32[9,3,512]{2,1,0:T(4,128)S(1)} %collective-permute-done.13.refs_3_.refs_1_, f32[9,3,512]{2,1,0:T(4,128)S(1)} %collective-permute-done.14.refs_5_.refs_2_, ...), custom_call_target="tpu_custom_call" | custom-call | flops 1 | bytes 100000000 | tf_op jit(solution)/shard_map/pallas_call | solution.py:339
  77.0 2.0 %collective-permute-start.19 = (f32[6,32,256]{2,1,0:T(8,128)S(1)}, f32[6,32,256]{2,1,0:T(8,128)S(1)}, u32[]{:S(2)}, u32[]{:S(2)}) collective-permute-start(f32[6,32,256]{2,1,0:T(8,128)S(1)} %get-tuple-element.48), channel_id=1, source_target_pairs={{0,16},{16,0},{8,24},{24,8},{1,17},{17,1},{9,25},{25,9},{2,18},{18... | collective-permute-start | bytes 589832 | tf_op jit(solution)/shard_map/ppermute | solution.py:33
  79.0 1.1 %collective-permute-done.24.refs_4_ = f32[2,6,32,256]{3,2,1,0:T(8,128)S(1)} collective-permute-done((f32[2,6,32,256]{3,2,1,0:T(8,128)S(1)}, f32[2,6,32,256]{3,2,1,0:T(8,128)S(1)}, u32[]{:S(2)}, u32[]{:S(2)}) %collective-permute-start.24) | collective-permute-done | bytes 393248 | tf_op jit(solution)/shard_map/ppermute | solution.py:33
  80.0 1.0 collective-permute-start.18
  81.1 1.1 %collective-permute-start.25 = (f32[6,32,256]{2,1,0:T(8,128)S(1)}, f32[6,32,256]{2,1,0:T(8,128)S(1)}, u32[]{:S(2)}, u32[]{:S(2)}) collective-permute-start(f32[6,32,256]{2,1,0:T(8,128)S(1)} %slice_bitcast_fusion.1), channel_id=1, source_target_pairs={{0,8},{8,0},{16,24},{24,16},{1,9},{9,1},{17,25},{25,17},{2,10},{10... | collective-permute-start | bytes 589832 | tf_op jit(solution)/shard_map/ppermute | solution.py:29
  82.2 1.0 %collective-permute-start.17 = (f32[6,32,256]{2,1,0:T(8,128)S(1)}, f32[6,32,256]{2,1,0:T(8,128)S(1)}, u32[]{:S(2)}, u32[]{:S(2)}) collective-permute-start(f32[6,32,256]{2,1,0:T(8,128)S(1)} %get-tuple-element.48), channel_id=1, source_target_pairs={{0,8},{8,0},{16,24},{24,16},{1,9},{9,1},{17,25},{25,17},{2,10},{10... | collective-permute-start | bytes 589832 | tf_op jit(solution)/shard_map/ppermute | solution.py:29
  83.2 3.6 %collective-permute-start.26 = (f32[6,32,256]{2,1,0:T(8,128)S(1)}, f32[6,32,256]{2,1,0:T(8,128)S(1)}, u32[]{:S(2)}, u32[]{:S(2)}) collective-permute-start(f32[6,32,256]{2,1,0:T(8,128)S(1)} %slice_bitcast_fusion), channel_id=1, source_target_pairs={{0,16},{16,0},{8,24},{24,8},{1,17},{17,1},{9,25},{25,9},{2,18},{18... | collective-permute-start | bytes 589832 | tf_op jit(solution)/shard_map/ppermute | solution.py:33
  87.0 2.1 %collective-permute-start.22 = (f32[6,32,256]{2,1,0:T(8,128)S(1)}, f32[6,32,256]{2,1,0:T(8,128)S(1)}, u32[]{:S(2)}, u32[]{:S(2)}) collective-permute-start(f32[6,32,256]{2,1,0:T(8,128)S(1)} %get-tuple-element.47), channel_id=1, source_target_pairs={{0,16},{16,0},{8,24},{24,8},{1,17},{17,1},{9,25},{25,9},{2,18},{18... | collective-permute-start | bytes 589832 | tf_op jit(solution)/shard_map/ppermute | solution.py:33
  89.1 2.5 %collective-permute-done.25.refs_2_ = f32[6,32,256]{2,1,0:T(8,128)S(1)} collective-permute-done((f32[6,32,256]{2,1,0:T(8,128)S(1)}, f32[6,32,256]{2,1,0:T(8,128)S(1)}, u32[]{:S(2)}, u32[]{:S(2)}) %collective-permute-start.25) | collective-permute-done | bytes 196640 | tf_op jit(solution)/shard_map/ppermute | solution.py:29
  91.7 1.9 %collective-permute-start.21 = (f32[6,32,256]{2,1,0:T(8,128)S(1)}, f32[6,32,256]{2,1,0:T(8,128)S(1)}, u32[]{:S(2)}, u32[]{:S(2)}) collective-permute-start(f32[6,32,256]{2,1,0:T(8,128)S(1)} %collective-permute-done.18.refs_2_), channel_id=1, source_target_pairs={{0,16},{16,0},{8,24},{24,8},{1,17},{17,1},{9,25},{25,9},{2,18},{18... | collective-permute-start | bytes 589832 | tf_op jit(solution)/shard_map/ppermute | solution.py:33
  93.6 1.6 %shard_map.52.refs_5_ = f32[16,128,512]{2,1,0:T(8,128)} custom-call(s32[7]{0:T(128)S(1)} %stack.31.spot, f32[2,4,32,256]{3,2,1,0:T(8,128)S(1)} %shard_map.49.refs_6_.refs_0_, f32[2,4,32,256]{3,2,1,0:T(8,128)S(1)} %collective-permute-done.15.refs_4_.refs_1_, f32[4,32,256]{2,1,0:T(8,128)S(1)} %collective-permute-done.27.refs_2_, ...), custom_call_target="tpu_custom_call" | custom-call | flops 1 | bytes 1 | tf_op jit(solution)/shard_map/pallas_call | solution.py:369
  95.2 1.8 %shard_map.53.refs_7_ = f32[16,128,512]{2,1,0:T(8,128)} custom-call(s32[7]{0:T(128)S(1)} %stack.31.spot, f32[2,6,32,256]{3,2,1,0:T(8,128)S(1)} %shard_map.50.refs_3_.refs_0_, f32[2,6,32,256]{3,2,1,0:T(8,128)S(1)} %collective-permute-done.23.refs_1_, f32[6,32,256]{2,1,0:T(8,128)S(1)} %collective-permute-done.25.refs_2_, ...), custom_call_target="tpu_custom_call", output_to_operand_aliasing={{}: (6, {})} | custom-call | flops 1 | bytes 1 | tf_op jit(solution)/shard_map/pallas_call | solution.py:369
  97.3 1.7 %shard_map.54 = f32[16,128,512]{2,1,0:T(8,128)} custom-call(s32[7]{0:T(128)S(1)} %stack.31.spot, f32[2,6,32,256]{3,2,1,0:T(8,128)S(1)} %shard_map.51.refs_0_, f32[6,32,256]{2,1,0:T(8,128)S(1)} %collective-permute-done.17.refs_1_, f32[6,32,256]{2,1,0:T(8,128)S(1)} %collective-permute-done.18.refs_2_, ...), custom_call_target="tpu_custom_call", output_to_operand_aliasing={{}: (8, {})} | custom-call | flops 1 | bytes 1 | tf_op jit(solution)/shard_map/pallas_call | solution.py:369
  (47 shorter events, 2.9 us)
Async XLA Ops:
  2.0 14.4 %collective-permute-start.2 = (f32[2,7,32,256]{3,2,1,0:T(8,128)S(1)}, f32[2,7,32,256]{3,2,1,0:T(8,128)S(1)}, u32[]{:S(2)}, u32[]{:S(2)}) collective-permute-start(f32[2,7,32,256]{3,2,1,0:T(8,128)S(1)} %get-tuple-element.26.rest_0_), channel_id=1, source_target_pairs={{0,8},{8,0},{16,24},{24,16},{1,9},{9,1},{17,25},{25,17},{2,10},{10... | collective-permute-start | bytes 1376264 | tf_op jit(solution)/shard_map/ppermute | solution.py:29
  5.0 13.4 %collective-permute-start.3 = (f32[2,7,32,256]{3,2,1,0:T(8,128)S(1)}, f32[2,7,32,256]{3,2,1,0:T(8,128)S(1)}, u32[]{:S(2)}, u32[]{:S(2)}) collective-permute-start(f32[2,7,32,256]{3,2,1,0:T(8,128)S(1)} %get-tuple-element.27.rest_1_), channel_id=1, source_target_pairs={{0,16},{16,0},{8,24},{24,8},{1,17},{17,1},{9,25},{25,9},{2,18},{18... | collective-permute-start | bytes 1376264 | tf_op jit(solution)/shard_map/ppermute | solution.py:33
  9.0 13.0 %collective-permute-start = (f32[2,4,32,256]{3,2,1,0:T(8,128)}, f32[2,4,32,256]{3,2,1,0:T(8,128)}, u32[]{:S(2)}, u32[]{:S(2)}) collective-permute-start(f32[2,4,32,256]{3,2,1,0:T(8,128)} %get-tuple-element.28.rest_0_), channel_id=1, source_target_pairs={{0,8},{8,0},{16,24},{24,16},{1,9},{9,1},{17,25},{25,17},{2,10},{10... | collective-permute-start | bytes 786440 | tf_op jit(solution)/shard_map/ppermute | solution.py:29
  9.6 14.5 %collective-permute-start.1 = (f32[2,4,32,256]{3,2,1,0:T(8,128)}, f32[2,4,32,256]{3,2,1,0:T(8,128)}, u32[]{:S(2)}, u32[]{:S(2)}) collective-permute-start(f32[2,4,32,256]{3,2,1,0:T(8,128)} %get-tuple-element.29.rest_1_), channel_id=1, source_target_pairs={{0,16},{16,0},{8,24},{24,8},{1,17},{17,1},{9,25},{25,9},{2,18},{18... | collective-permute-start | bytes 786440 | tf_op jit(solution)/shard_map/ppermute | solution.py:33
  14.1 12.4 %copy-start = (f32[2,5,32,256]{3,2,1,0:T(8,128)}, f32[2,5,32,256]{3,2,1,0:T(8,128)S(1)}, u32[]{:S(2)}) copy-start(f32[2,5,32,256]{3,2,1,0:T(8,128)S(1)} %get-tuple-element.31.rest_0_.refs_0_) | copy-start | bytes 983044
  19.3 0.7 copy-start.1
  20.0 8.6 %collective-permute-start.6 = (f32[7,32,256]{2,1,0:T(8,128)}, f32[7,32,256]{2,1,0:T(8,128)}, u32[]{:S(2)}, u32[]{:S(2)}) collective-permute-start(f32[7,32,256]{2,1,0:T(8,128)} %get-tuple-element.35.rest_0_), channel_id=1, source_target_pairs={{0,16},{16,0},{8,24},{24,8},{1,17},{17,1},{9,25},{25,9},{2,18},{18... | collective-permute-start | bytes 688136 | tf_op jit(solution)/shard_map/ppermute | solution.py:33
  21.5 7.5 %collective-permute-start.7 = (f32[7,32,256]{2,1,0:T(8,128)}, f32[7,32,256]{2,1,0:T(8,128)}, u32[]{:S(2)}, u32[]{:S(2)}) collective-permute-start(f32[7,32,256]{2,1,0:T(8,128)} %get-tuple-element.36.rest_1_), channel_id=1, source_target_pairs={{0,8},{8,0},{16,24},{24,16},{1,9},{9,1},{17,25},{25,17},{2,10},{10... | collective-permute-start | bytes 688136 | tf_op jit(solution)/shard_map/ppermute | solution.py:29
  25.2 0.7 copy-start.2
  25.9 0.7 copy-start.4
  26.5 12.8 %collective-permute-start.4 = (f32[2,5,32,256]{3,2,1,0:T(8,128)}, f32[2,5,32,256]{3,2,1,0:T(8,128)S(1)}, u32[]{:S(2)}, u32[]{:S(2)}) collective-permute-start(f32[2,5,32,256]{3,2,1,0:T(8,128)} %get-tuple-element.39), channel_id=1, source_target_pairs={{0,8},{8,0},{16,24},{24,16},{1,9},{9,1},{17,25},{25,17},{2,10},{10... | collective-permute-start | bytes 983048 | tf_op jit(solution)/shard_map/ppermute | solution.py:29
  26.6 12.8 %collective-permute-start.5 = (f32[2,5,32,256]{3,2,1,0:T(8,128)}, f32[2,5,32,256]{3,2,1,0:T(8,128)S(1)}, u32[]{:S(2)}, u32[]{:S(2)}) collective-permute-start(f32[2,5,32,256]{3,2,1,0:T(8,128)} %get-tuple-element.40), channel_id=1, source_target_pairs={{0,16},{16,0},{8,24},{24,8},{1,17},{17,1},{9,25},{25,9},{2,18},{18... | collective-permute-start | bytes 983048 | tf_op jit(solution)/shard_map/ppermute | solution.py:33
  29.0 0.9 copy-start.3
  29.9 0.9 copy-start.5
  32.0 1.5 %collective-permute-start.8 = (f32[3,32,512]{2,1,0:T(8,128)S(1)}, f32[3,32,512]{2,1,0:T(8,128)S(1)}, u32[]{:S(2)}, u32[]{:S(2)}) collective-permute-start(f32[3,32,512]{2,1,0:T(8,128)S(1)} %constant_dynamic-slice_fusion), channel_id=1, source_target_pairs={{0,4},{4,0},{1,5},{5,1},{2,6},{6,2},{3,7},{7,3},{8,12},{12,8},{9,1... | collective-permute-start | bytes 589832 | tf_op jit(solution)/shard_map/ppermute | solution.py:488
  33.5 6.4 %collective-permute-start.10 = (f32[10,3,512]{2,1,0:T(4,128)S(1)}, f32[10,3,512]{2,1,0:T(4,128)S(1)}, u32[]{:S(2)}, u32[]{:S(2)}) collective-permute-start(f32[10,3,512]{2,1,0:T(4,128)S(1)} %get-tuple-element.42), channel_id=1, source_target_pairs={{8,0},{24,8},{16,24},{1,16},{9,1},{25,9},{17,25},{2,17},{10,2},{26... | collective-permute-start | bytes 184328 | tf_op jit(solution)/shard_map/ppermute | solution.py:440
  34.8 6.6 %collective-permute-start.9 = (f32[10,3,512]{2,1,0:T(4,128)S(1)}, f32[10,3,512]{2,1,0:T(4,128)S(1)}, u32[]{:S(2)}, u32[]{:S(2)}) collective-permute-start(f32[10,3,512]{2,1,0:T(4,128)S(1)} %get-tuple-element.41), channel_id=1, source_target_pairs={{0,8},{8,24},{24,16},{16,1},{1,9},{9,25},{25,17},{17,2},{2,10},{10... | collective-permute-start | bytes 184328 | tf_op jit(solution)/shard_map/ppermute | solution.py:440
  41.5 9.1 %collective-permute-start.11 = (f32[9,32,256]{2,1,0:T(8,128)S(1)}, f32[9,32,256]{2,1,0:T(8,128)S(1)}, u32[]{:S(2)}, u32[]{:S(2)}) collective-permute-start(f32[9,32,256]{2,1,0:T(8,128)S(1)} %get-tuple-element.43.refs_4_), channel_id=1, source_target_pairs={{0,16},{16,0},{8,24},{24,8},{1,17},{17,1},{9,25},{25,9},{2,18},{18... | collective-permute-start | bytes 884744 | tf_op jit(solution)/shard_map/ppermute | solution.py:33
  43.5 7.3 %collective-permute-start.12 = (f32[9,32,256]{2,1,0:T(8,128)S(1)}, f32[9,32,256]{2,1,0:T(8,128)S(1)}, u32[]{:S(2)}, u32[]{:S(2)}) collective-permute-start(f32[9,32,256]{2,1,0:T(8,128)S(1)} %get-tuple-element.44.refs_5_), channel_id=1, source_target_pairs={{0,8},{8,0},{16,24},{24,16},{1,9},{9,1},{17,25},{25,17},{2,10},{10... | collective-permute-start | bytes 884744 | tf_op jit(solution)/shard_map/ppermute | solution.py:29
  49.5 8.1 %collective-permute-start.16 = (f32[2,4,32,256]{3,2,1,0:T(8,128)S(1)}, f32[2,4,32,256]{3,2,1,0:T(8,128)S(1)}, u32[]{:S(2)}, u32[]{:S(2)}) collective-permute-start(f32[2,4,32,256]{3,2,1,0:T(8,128)S(1)} %shard_map.49.refs_6_.refs_0_), channel_id=1, source_target_pairs={{0,16},{16,0},{8,24},{24,8},{1,17},{17,1},{9,25},{25,9},{2,18},{18... | collective-permute-start | bytes 786440 | tf_op jit(solution)/shard_map/ppermute | solution.py:33
  50.6 20.5 %collective-permute-start.15 = (f32[2,4,32,256]{3,2,1,0:T(8,128)S(1)}, f32[2,4,32,256]{3,2,1,0:T(8,128)S(1)}, u32[]{:S(2)}, u32[]{:S(2)}) collective-permute-start(f32[2,4,32,256]{3,2,1,0:T(8,128)S(1)} %shard_map.49.refs_6_.refs_0_), channel_id=1, source_target_pairs={{0,8},{8,0},{16,24},{24,16},{1,9},{9,1},{17,25},{25,17},{2,10},{10... | collective-permute-start | bytes 786440 | tf_op jit(solution)/shard_map/ppermute | solution.py:29
  52.0 8.4 %collective-permute-start.13 = (f32[9,3,512]{2,1,0:T(4,128)S(1)}, f32[9,3,512]{2,1,0:T(4,128)S(1)}, u32[]{:S(2)}, u32[]{:S(2)}) collective-permute-start(f32[9,3,512]{2,1,0:T(4,128)S(1)} %get-tuple-element.45), channel_id=1, source_target_pairs={{0,8},{8,24},{24,16},{16,1},{1,9},{9,25},{25,17},{17,2},{2,10},{10... | collective-permute-start | bytes 165896 | tf_op jit(solution)/shard_map/ppermute | solution.py:440
  56.4 6.2 %collective-permute-start.14 = (f32[9,3,512]{2,1,0:T(4,128)S(1)}, f32[9,3,512]{2,1,0:T(4,128)S(1)}, u32[]{:S(2)}, u32[]{:S(2)}) collective-permute-start(f32[9,3,512]{2,1,0:T(4,128)S(1)} %get-tuple-element.46), channel_id=1, source_target_pairs={{8,0},{24,8},{16,24},{1,16},{9,1},{25,9},{17,25},{2,17},{10,2},{26... | collective-permute-start | bytes 165896 | tf_op jit(solution)/shard_map/ppermute | solution.py:440
  57.7 24.5 %collective-permute-start.27 = (f32[4,32,256]{2,1,0:T(8,128)S(1)}, f32[4,32,256]{2,1,0:T(8,128)S(1)}, u32[]{:S(2)}, u32[]{:S(2)}) collective-permute-start(f32[4,32,256]{2,1,0:T(8,128)S(1)} %slice_bitcast_fusion.5), channel_id=1, source_target_pairs={{0,8},{8,0},{16,24},{24,16},{1,9},{9,1},{17,25},{25,17},{2,10},{10... | collective-permute-start | bytes 393224 | tf_op jit(solution)/shard_map/ppermute | solution.py:29
  68.3 11.7 %collective-permute-start.24 = (f32[2,6,32,256]{3,2,1,0:T(8,128)S(1)}, f32[2,6,32,256]{3,2,1,0:T(8,128)S(1)}, u32[]{:S(2)}, u32[]{:S(2)}) collective-permute-start(f32[2,6,32,256]{3,2,1,0:T(8,128)S(1)} %shard_map.50.refs_3_.refs_0_), channel_id=1, source_target_pairs={{0,16},{16,0},{8,24},{24,8},{1,17},{17,1},{9,25},{25,9},{2,18},{18... | collective-permute-start | bytes 1179656 | tf_op jit(solution)/shard_map/ppermute | solution.py:33
  71.1 12.1 %collective-permute-start.28 = (f32[4,32,256]{2,1,0:T(8,128)S(1)}, f32[4,32,256]{2,1,0:T(8,128)S(1)}, u32[]{:S(2)}, u32[]{:S(2)}) collective-permute-start(f32[4,32,256]{2,1,0:T(8,128)S(1)} %slice_bitcast_fusion.4), channel_id=1, source_target_pairs={{0,16},{16,0},{8,24},{24,8},{1,17},{17,1},{9,25},{25,9},{2,18},{18... | collective-permute-start | bytes 393224 | tf_op jit(solution)/shard_map/ppermute | solution.py:33
  71.2 9.9 %collective-permute-start.23 = (f32[2,6,32,256]{3,2,1,0:T(8,128)S(1)}, f32[2,6,32,256]{3,2,1,0:T(8,128)S(1)}, u32[]{:S(2)}, u32[]{:S(2)}) collective-permute-start(f32[2,6,32,256]{3,2,1,0:T(8,128)S(1)} %shard_map.50.refs_3_.refs_0_), channel_id=1, source_target_pairs={{0,8},{8,0},{16,24},{24,16},{1,9},{9,1},{17,25},{25,17},{2,10},{10... | collective-permute-start | bytes 1179656 | tf_op jit(solution)/shard_map/ppermute | solution.py:29
  77.0 10.0 %collective-permute-start.19 = (f32[6,32,256]{2,1,0:T(8,128)S(1)}, f32[6,32,256]{2,1,0:T(8,128)S(1)}, u32[]{:S(2)}, u32[]{:S(2)}) collective-permute-start(f32[6,32,256]{2,1,0:T(8,128)S(1)} %get-tuple-element.48), channel_id=1, source_target_pairs={{0,16},{16,0},{8,24},{24,8},{1,17},{17,1},{9,25},{25,9},{2,18},{18... | collective-permute-start | bytes 589832 | tf_op jit(solution)/shard_map/ppermute | solution.py:33
  80.0 9.1 %collective-permute-start.18 = (f32[6,32,256]{2,1,0:T(8,128)S(1)}, f32[6,32,256]{2,1,0:T(8,128)S(1)}, u32[]{:S(2)}, u32[]{:S(2)}) collective-permute-start(f32[6,32,256]{2,1,0:T(8,128)S(1)} %get-tuple-element.47), channel_id=1, source_target_pairs={{0,8},{8,0},{16,24},{24,16},{1,9},{9,1},{17,25},{25,17},{2,10},{10... | collective-permute-start | bytes 589832 | tf_op jit(solution)/shard_map/ppermute | solution.py:29
  81.1 10.6 %collective-permute-start.25 = (f32[6,32,256]{2,1,0:T(8,128)S(1)}, f32[6,32,256]{2,1,0:T(8,128)S(1)}, u32[]{:S(2)}, u32[]{:S(2)}) collective-permute-start(f32[6,32,256]{2,1,0:T(8,128)S(1)} %slice_bitcast_fusion.1), channel_id=1, source_target_pairs={{0,8},{8,0},{16,24},{24,16},{1,9},{9,1},{17,25},{25,17},{2,10},{10... | collective-permute-start | bytes 589832 | tf_op jit(solution)/shard_map/ppermute | solution.py:29
  82.2 14.8 %collective-permute-start.17 = (f32[6,32,256]{2,1,0:T(8,128)S(1)}, f32[6,32,256]{2,1,0:T(8,128)S(1)}, u32[]{:S(2)}, u32[]{:S(2)}) collective-permute-start(f32[6,32,256]{2,1,0:T(8,128)S(1)} %get-tuple-element.48), channel_id=1, source_target_pairs={{0,8},{8,0},{16,24},{24,16},{1,9},{9,1},{17,25},{25,17},{2,10},{10... | collective-permute-start | bytes 589832 | tf_op jit(solution)/shard_map/ppermute | solution.py:29
  83.2 12.0 %collective-permute-start.26 = (f32[6,32,256]{2,1,0:T(8,128)S(1)}, f32[6,32,256]{2,1,0:T(8,128)S(1)}, u32[]{:S(2)}, u32[]{:S(2)}) collective-permute-start(f32[6,32,256]{2,1,0:T(8,128)S(1)} %slice_bitcast_fusion), channel_id=1, source_target_pairs={{0,16},{16,0},{8,24},{24,8},{1,17},{17,1},{9,25},{25,9},{2,18},{18... | collective-permute-start | bytes 589832 | tf_op jit(solution)/shard_map/ppermute | solution.py:33
  87.0 10.0 %collective-permute-start.22 = (f32[6,32,256]{2,1,0:T(8,128)S(1)}, f32[6,32,256]{2,1,0:T(8,128)S(1)}, u32[]{:S(2)}, u32[]{:S(2)}) collective-permute-start(f32[6,32,256]{2,1,0:T(8,128)S(1)} %get-tuple-element.47), channel_id=1, source_target_pairs={{0,16},{16,0},{8,24},{24,8},{1,17},{17,1},{9,25},{25,9},{2,18},{18... | collective-permute-start | bytes 589832 | tf_op jit(solution)/shard_map/ppermute | solution.py:33
  89.1 7.9 %collective-permute-start.20 = (f32[6,32,256]{2,1,0:T(8,128)S(1)}, f32[6,32,256]{2,1,0:T(8,128)S(1)}, u32[]{:S(2)}, u32[]{:S(2)}) collective-permute-start(f32[6,32,256]{2,1,0:T(8,128)S(1)} %collective-permute-done.19.refs_5_), channel_id=1, source_target_pairs={{0,8},{8,0},{16,24},{24,16},{1,9},{9,1},{17,25},{25,17},{2,10},{10... | collective-permute-start | bytes 589832 | tf_op jit(solution)/shard_map/ppermute | solution.py:29
  91.7 5.7 %collective-permute-start.21 = (f32[6,32,256]{2,1,0:T(8,128)S(1)}, f32[6,32,256]{2,1,0:T(8,128)S(1)}, u32[]{:S(2)}, u32[]{:S(2)}) collective-permute-start(f32[6,32,256]{2,1,0:T(8,128)S(1)} %collective-permute-done.18.refs_2_), channel_id=1, source_target_pairs={{0,16},{16,0},{8,24},{24,8},{1,17},{17,1},{9,25},{25,9},{2,18},{18... | collective-permute-start | bytes 589832 | tf_op jit(solution)/shard_map/ppermute | solution.py:33

commit v3 on v2

--- a/solution.py
+++ b/solution.py
@@ -23,6 +23,10 @@
 PAIRS_X = [(0, 1), (1, 0), (2, 3), (3, 2)]
 PAIRS_Y = [(0, 2), (2, 0), (1, 3), (3, 1)]
 PAIRS_FAR = [(0, 3), (3, 0), (1, 2), (2, 1)]
+
+
+def near_core(arrays):
+    return [pltpu.with_memory_space_constraint(array, pltpu.VMEM) for array in arrays]
 
 
 def swap_x(array):
@@ -98,14 +102,14 @@
         out[i] = held[n] * sign[:, :, side : side + half]
 
 
-def prepare(chunk, spot, signs, gradient, shares, after=()):
+def prepare(chunk, spot, signs, gradient, shares, after=(), keep=False):
     rows, cols = gradient.shape[2:]
     shape = (2, chunk[1], rows // shares, cols // 2)
     return pl.pallas_call(
         functools.partial(prepare_kernel, chunk, len(after)),
-        in_specs=[SCALARS] + [ANYWHERE] * (2 + len(after)),
+        in_specs=[SCALARS] + [ANYWHERE] * 2 + [WHOLE] * len(after),
         out_specs=[WHOLE] * 2,
-        out_shape=[jax.ShapeDtypeStruct(shape, jnp.float32)] * 2,
+        out_shape=[pltpu.VMEM(shape, jnp.float32) if keep else jax.ShapeDtypeStruct(shape, jnp.float32)] * 2,
         scratch_shapes=[
             pltpu.VMEM((4,) + shape[1:], jnp.float32),
             pltpu.VMEM(signs.shape, jnp.int32),
@@ -113,7 +117,7 @@
         ],
         compiler_params=params(),
         cost_estimate=COST,
-    )(spot, signs, gradient, *after)
+    )(spot, signs, gradient, *near_core(after))
 
 
 def hold_kernel(chunks, after, spot, signs, gradient, model, *rest):
@@ -146,7 +150,7 @@
     part = (planes, rows // shares, cols // 2)
     return pl.pallas_call(
         functools.partial(hold_kernel, chunks, len(after)),
-        in_specs=[SCALARS] + [ANYWHERE] * (3 + len(after)),
+        in_specs=[SCALARS] + [ANYWHERE] * 3 + [WHOLE] * len(after),
         out_specs=[WHOLE] * 3,
         out_shape=[pltpu.VMEM(shape, jnp.float32) for shape in (part, part, whole)],
         scratch_shapes=[
@@ -158,31 +162,35 @@
         ],
         compiler_params=params(),
         cost_estimate=COST,
-    )(spot, signs, gradient, model, *after)
-
-
-def relay_kernel(chunk, ready, after, fore_a, fore_b, near_a, near_b, *rest):
-    out_a, out_b = rest[ready + after :]
+    )(spot, signs, gradient, model, *near_core(after))
+
+
+def relay_kernel(chunk, carried, ready, after, fore_a, fore_b, near_a, near_b, *rest):
+    outs = rest[carried + ready + after :]
+    here = slice(chunk[0], chunk[0] + chunk[1])
     at = 0
     if ready:
-        at = rest[0].shape[0]
-        out_a[:at] = rest[0][...]
-        out_b[:at] = rest[1][...]
-    here = slice(chunk[0], chunk[0] + chunk[1])
-    out_a[at:] = fore_a[here] + near_a[1]
-    out_b[at:] = fore_b[here] + near_b[1]
-
-
-def relay(chunk, fores, near, ready=(), after=()):
-    count = chunk[1] + sum(part.shape[0] for part in ready[:1])
-    return pl.pallas_call(
-        functools.partial(relay_kernel, chunk, len(ready), len(after)),
-        in_specs=[WHOLE] * (4 + len(ready)) + [ANYWHERE] * len(after),
-        out_specs=[WHOLE] * 2,
-        out_shape=[jax.ShapeDtypeStruct((count,) + near[0].shape[2:], jnp.float32)] * 2,
+        at = rest[carried].shape[0]
+        outs[0][:at] = rest[carried][...]
+        outs[1][:at] = rest[carried + 1][...]
+    outs[0][at:] = fore_a[here] + near_a[1]
+    outs[1][at:] = fore_b[here] + near_b[1]
+    for source, out in zip(rest[:carried], outs[2:]):
+        out[...] = source[...]
+
+
+def relay(chunk, fores, near, carried=(), after=(), ready=()):
+    count = chunk[1] + sum(array.shape[0] for array in ready[:1])
+    shapes = [(count,) + near[0].shape[2:]] * 2 + [array.shape for array in carried]
+    outs = pl.pallas_call(
+        functools.partial(relay_kernel, chunk, len(carried), len(ready), len(after)),
+        in_specs=[WHOLE] * (4 + len(carried) + len(ready) + len(after)),
+        out_specs=[WHOLE] * len(shapes),
+        out_shape=[jax.ShapeDtypeStruct(shape, jnp.float32) for shape in shapes],
         compiler_params=params(),
         cost_estimate=COST,
-    )(*fores, *near, *ready, *after)
+    )(*fores, *near_core((*near, *carried, *ready, *after)))
+    return outs[:2], outs[2:]
 
 
 def settle_kernel(chunks, after, base, *refs):
@@ -201,34 +209,37 @@
     count, share, half = fars[0].shape
     return pl.pallas_call(
         functools.partial(settle_kernel, chunks, len(after)),
-        in_specs=[WHOLE] * (3 + len(nears)) + [ANYWHERE] * len(after),
+        in_specs=[WHOLE] * (3 + len(nears)) + [WHOLE] * len(after),
         out_specs=WHOLE,
         out_shape=jax.ShapeDtypeStruct((count, share, 2 * half), jnp.float32),
         compiler_params=params(),
         cost_estimate=COST,
-    )(base, *nears, *fars, *after)
-
-
-def pack_kernel(count, *refs):
-    parts, (tops, feet) = (refs[:count], refs[count:])
+    )(base, *near_core((*nears, *fars, *after)))
+
+
+def pack_kernel(count, spot, *refs):
+    parts, (one, two) = (refs[:count], refs[count:])
+    odd = spot[0] % 2 == 1
     at = 0
     for part in parts:
         for p in range(part.shape[0]):
-            tops[at] = part[p, part.shape[1] - HALO :]
-            feet[at] = part[p, :HALO]
+            last = part[p, part.shape[1] - HALO :]
+            first = part[p, :HALO]
+            one[at] = jnp.where(odd, first, last)
+            two[at] = jnp.where(odd, last, first)
             at += 1
 
 
-def pack(parts):
+def pack(spot, parts):
     shape = (sum(part.shape[0] for part in parts), HALO, parts[0].shape[2])
     return pl.pallas_call(
         functools.partial(pack_kernel, len(parts)),
-        in_specs=[WHOLE] * len(parts),
+        in_specs=[SCALARS] + [WHOLE] * len(parts),
         out_specs=[WHOLE] * 2,
         out_shape=[jax.ShapeDtypeStruct(shape, jnp.float32)] * 2,
         compiler_params=params(),
         cost_estimate=COST,
-    )(*parts)
+    )(spot, *near_core(parts))
 
 
 def vary_kernel(span, pieces, sizes, counts, after, spot, *refs):
@@ -241,6 +252,7 @@
     tiles = share // SIDE
     shape = (SIDE, cols)
     flip = spot[FLIP]
+    odd = spot[0] % 2 == 1
 
     for field, held, offset, count, side, line, there, base in pieces:
         goes = turn(flip, there, count, planes)
@@ -252,8 +264,10 @@
         for i in range(count):
             target[goes + i, :share] = fields[field][base + comes + i]
             target[goes + i, share:rows] = jnp.zeros(shape, jnp.float32)
-            target[goes + i, share : share + HALO] = afters[side][line + comes + i]
-            target[goes + i, rows - HALO : rows] = befores[side][line + comes + i]
+            one = befores[side][line + comes + i]
+            two = afters[side][line + comes + i]
+            target[goes + i, share : share + HALO] = jnp.where(odd, two, one)
+            target[goes + i, rows - HALO : rows] = jnp.where(odd, one, two)
 
     row = lax.broadcasted_iota(jnp.int32, shape, 0)
     col = lax.broadcasted_iota(jnp.int32, shape, 1)
@@ -338,13 +352,13 @@
     counts = (len(fields), len(befores))
     return pl.pallas_call(
         functools.partial(vary_kernel, span, pieces, sizes, counts, len(after)),
-        in_specs=[SCALARS] + [WHOLE] * (counts[0] + 2 * counts[1]) + [ANYWHERE] * len(after),
+        in_specs=[SCALARS] + [WHOLE] * (counts[0] + 2 * counts[1]) + [WHOLE] * len(after),
         out_specs=WHOLE,
         out_shape=jax.ShapeDtypeStruct((2, span[1] - span[0], share, cols // 2), jnp.float32),
         scratch_shapes=[field, field, field, pltpu.VMEM((3, planes, rows, cols), jnp.float32)],
         compiler_params=params(),
         cost_estimate=LONG,
-    )(spot, *fields, *befores, *afters, *after)
+    )(spot, *near_core((*fields, *befores, *afters, *after)))
 
 
 def gather_kernel(span, parts, spot, *refs):
@@ -378,19 +392,20 @@
     )(spot, *arrays, *before)
 
 
-def idle_kernel(*refs):
-    pass
-
-
-def idle(arrays, after):
-    return pl.pallas_call(
-        idle_kernel,
-        in_specs=[ANYWHERE] * (len(arrays) + len(after)),
-        out_specs=[ANYWHERE] * len(arrays),
+def carry_kernel(count, after, *refs):
+    for source, out in zip(refs[:count], refs[count + after :]):
+        out[...] = source[...]
+
+
+def carry(arrays, after):
+    return pl.pallas_call(
+        functools.partial(carry_kernel, len(arrays), len(after)),
+        in_specs=[WHOLE] * (len(arrays) + len(after)),
+        out_specs=[WHOLE] * len(arrays),
         out_shape=[jax.ShapeDtypeStruct(array.shape, array.dtype) for array in arrays],
-        input_output_aliases={i: i for i in range(len(arrays))},
+        compiler_params=params(),
         cost_estimate=COST,
-    )(*arrays, *after)
+    )(*near_core((*arrays, *after)))
 
 
 def gray(place):
@@ -429,15 +444,14 @@
     spot = jnp.stack([at, at ^ 1, at ^ 2, at ^ 3, flip, layer * planes, start_x]).astype(jnp.int32)
 
     order = [gray(place) * lines + line for line in range(lines) for place in range(shares)]
-    ahead_x = list(zip(order[:-1], order[1:]))
-    back_x = [(j, i) for i, j in ahead_x]
+    pairs_one = [pair for i, j in zip(order[::2], order[1::2]) for pair in ((i, j), (j, i))]
+    pairs_two = [pair for i, j in zip(order[1:-1:2], order[2::2]) for pair in ((i, j), (j, i))]
     ahead_z = [(i, i + 1) for i in range(layers - 1)]
     back_z = [(j, i) for i, j in ahead_z]
 
     def across(edges):
-        tops, feet = edges
         group = ("shot", "inline")
-        return lax.ppermute(tops, group, ahead_x), lax.ppermute(feet, group, back_x)
+        return [lax.ppermute(edge, group, pairs) for edge, pairs in zip(edges, (pairs_one, pairs_two))]
 
     gradient = pltpu.with_memory_space_constraint(gradient, pltpu.HBM)
     model = pltpu.with_memory_space_constraint(model, pltpu.HBM)
@@ -457,11 +471,11 @@
         sent = prep(c0)
         near = both(*sent)
         *fores, base = hold([c0], spot, signs, gradient, model, shares, sent)
-        far = crossed(*relay(c0, fores, near))
+        far = crossed(*relay(c0, fores, near)[0])
         target = settle([c0], base, near, far)
         low = lax.ppermute(target[planes - HALO :], "depth", ahead_z)
         high = lax.ppermute(target[:HALO], "depth", back_z)
-        before, after = across(pack((low, target, high)))
+        before, after = across(pack(spot, (low, target, high)))
         pieces = [
             (0, HALO, 0, HALO, 0, 0, 0, 0),
             (1, planes, 0, planes, 0, HALO, HALO, 0),
@@ -478,22 +492,20 @@
     sent_1 = prep(c1, sent_0)
     near_1 = both(*sent_1)
     *fores, base = hold([c0, c1, c2], spot, signs, gradient, model, shares, sent_1)
-    sent_2 = prep(c2, (base,))
-    passed_0 = relay(c0, fores, near_0, after=sent_2)
+    sent_2 = prepare(c2, spot, signs, gradient, shares, (base,), True)
+    passed_0, _ = relay(c0, fores, near_0, after=sent_2)
     far_0 = crossed(*passed_0)
-    passed_1 = relay(c1, fores, near_1, after=passed_0)
-    near_2 = both(*idle(sent_2, passed_1))
+    passed_1, sent_2 = relay(c1, fores, near_1, sent_2, passed_0)
+    near_2 = both(*sent_2)
     mid_0 = settle([c0], base, near_0, far_0, passed_1)
     edge = lax.dynamic_slice_in_dim(mid_0, turn(flip, 0, HALO, n0), HALO, 0)
     beside = lax.ppermute(edge, "depth", ahead_z + back_z)
-    before_0, after_0 = across(pack((mid_0, beside)))
-    passed_2 = relay(c2, fores, near_2, passed_1, (before_0, after_0))
+    edges_0 = pack(spot, (mid_0, beside))
+    before_0, after_0 = across(edges_0)
+    passed_2, _ = relay(c2, fores, near_2, after=edges_0, ready=passed_1)
     far_1 = crossed(*passed_2)
-    mid_1 = settle([c1, c2], base, near_1 + near_2, far_1)
-    before_1, after_1 = across(pack((mid_1,)))
-
-    arrays = {"beside": beside, "mid_0": mid_0, "mid_1": mid_1}
-    sides = [(before_0, after_0), (before_1, after_1)]
+    arrays = {"beside": beside, "mid_0": mid_0, }
+    sides = [(before_0, after_0)]
     held = [
         (-HALO, HALO, "beside", 0, 0, n0),
         (0, n0, "mid_0", 0, 0, 0),
@@ -527,6 +539,11 @@
     m1 = (m0 + planes) // 2
     spans = ((0, m0), (m0, m1), (m1, planes))
     own_0 = update(spans[0], passed_2)
+    mid_1 = settle([c1, c2], base, near_1 + near_2, far_1, (own_0,))
+    edges_1 = pack(spot, (mid_1,))
+    before_1, after_1 = across(edges_1)
+    arrays["mid_1"] = mid_1
+    sides.append((before_1, after_1))
     pieces_0 = spread(own_0)
     own_1 = update(spans[1], (own_0,))
     pieces_1 = spread(own_1)

time: 99.4 us -> 92.5 us (0.931)
  starting transfers between devices: 43.8 us -> 39.4 us
  local copies, waits for them, and re-layouts: 4.02 us -> 1.88 us
  waiting for transfers between devices: 16.9 us -> 14.9 us
  Pallas kernels: 34 us -> 35.8 us
    ppermute x4, starting transfers between devices: 11.5 us -> 3.48 us  [across(): lax.ppermute(edge, group, pairs)]
    ppermute x4, waiting for transfers between devices: 4.23 us -> 1.31 us  [across(): lax.ppermute(edge, group, pairs)]
    ppermute x12, starting transfers between devices: 11.5 us -> 14.3 us  [swap_x(): return lax.ppermute(array, 'shot', PAIRS_X)]
    unnamed x12 -> x4, local copies, waits for them, and re-layouts: 3.83 us -> 1.7 us
    pallas_call x6 -> x5, Pallas kernels: 1.98 us -> 3.25 us  [the longest x3 2.09 us: relay(): pl.pallas_call(functools.partial(relay_kernel, chunk, len(carried), len(r...]
  transfers between devices with their start and end apart: 29 -> 29, of which waited for: 14 -> 12; matrix products, arithmetic and copies ran while one was open for 0% -> 0% of each run, Pallas kernels for 31% -> 35%
where the time goes in v3:
time: 92.5 us; the launch traced here: 92.2 us
  starting transfers between devices  39.4 us (43%)
  Pallas kernels  35.8 us (39%)
  waiting for transfers between devices  14.9 us (16%)
  local copies, waits for them, and re-layouts  1.88 us (2%)
    ppermute x12, starting transfers between devices, swap_y(): return lax.ppermute(array, 'shot', PAIRS_Y)  21.5 us
    pallas_call x3, Pallas kernels, vary(): pl.pallas_call(functools.partial(vary_kernel, span, pieces, sizes, counts...  15.9 us
    ppermute x12, starting transfers between devices, swap_x(): return lax.ppermute(array, 'shot', PAIRS_X)  14.3 us
    ppermute x12, waiting for transfers between devices, swap_y(): return lax.ppermute(array, 'shot', PAIRS_Y)  6.2 us
    pallas_call x3, Pallas kernels, prepare(): pl.pallas_call(functools.partial(prepare_kernel, chunk, len(after)), in_s...  6.19 us
    ppermute x12, waiting for transfers between devices, swap_x(): return lax.ppermute(array, 'shot', PAIRS_X)  5.94 us
    pallas_call x3, Pallas kernels, gather(): pl.pallas_call(functools.partial(gather_kernel, span, parts), in_specs=[S...  5.07 us
    ppermute x4, starting transfers between devices, across(): lax.ppermute(edge, group, pairs)  3.48 us
  transfers between devices with their start and end apart: 29, of which 12 were waited for; matrix products, arithmetic and copies ran while one was open for 0% of the time, Pallas kernels for 35%

profile of v3, /device:TPU:0, one launch (start us, length us, event | category | flops | bytes accessed | tf_op | source)
XLA Modules:
  0.0 92.2 jit_solution(17300981283602413804)
XLA Ops:
  0.1 1.9 %shard_map.37 = (f32[2,7,32,256]{3,2,1,0:T(8,128)S(1)}, f32[2,7,32,256]{3,2,1,0:T(8,128)S(1)}) custom-call(s32[7]{0:T(128)S(1)} %stack.31.spot, s32[1,512]{1,0:T(1,128)} %signs.7, f32[1,16,128,512]{3,2,1,0:T(8,128)} %gradient.7), custom_call_target="tpu_custom_call" | custom-call | flops 1 | bytes 1 | tf_op jit(solution)/shard_map/pallas_call | solution.py:108
  2.0 3.0 %collective-permute-start.2 = (f32[2,7,32,256]{3,2,1,0:T(8,128)S(1)}, f32[2,7,32,256]{3,2,1,0:T(8,128)S(1)}, u32[]{:S(2)}, u32[]{:S(2)}) collective-permute-start(f32[2,7,32,256]{3,2,1,0:T(8,128)S(1)} %get-tuple-element.26.rest_0_), channel_id=1, source_target_pairs={{0,8},{8,0},{16,24},{24,16},{1,9},{9,1},{17,25},{25,17},{2,10},{10... | collective-permute-start | bytes 1376264 | tf_op jit(solution)/shard_map/ppermute | solution.py:33
  5.0 1.5 %collective-permute-start.3 = (f32[2,7,32,256]{3,2,1,0:T(8,128)S(1)}, f32[2,7,32,256]{3,2,1,0:T(8,128)S(1)}, u32[]{:S(2)}, u32[]{:S(2)}) collective-permute-start(f32[2,7,32,256]{3,2,1,0:T(8,128)S(1)} %get-tuple-element.27.rest_1_), channel_id=1, source_target_pairs={{0,16},{16,0},{8,24},{24,8},{1,17},{17,1},{9,25},{25,9},{2,18},{18... | collective-permute-start | bytes 1376264 | tf_op jit(solution)/shard_map/ppermute | solution.py:37
  6.5 2.5 %shard_map.38 = (f32[2,4,32,256]{3,2,1,0:T(8,128)}, f32[2,4,32,256]{3,2,1,0:T(8,128)}) custom-call(s32[7]{0:T(128)S(1)} %stack.31.spot, s32[1,512]{1,0:T(1,128)} %signs.7, f32[1,16,128,512]{3,2,1,0:T(8,128)} %gradient.7, f32[2,7,32,256]{3,2,1,0:T(8,128)S(1)} %get-tuple-element.26.rest_0_, f32[2,7,32,256]{3,2,1,0:T(8,128)S(1)} %get-tuple-element.27.rest_1_), custom_call_target="tpu_custom_call" | custom-call | flops 1 | bytes 1 | tf_op jit(solution)/shard_map/pallas_call | solution.py:108
  9.0 0.6 collective-permute-start
  9.7 3.2 %shard_map.39 = (f32[16,32,256]{2,1,0:T(8,128)S(1)}, f32[16,32,256]{2,1,0:T(8,128)S(1)}, f32[16,32,512]{2,1,0:T(8,128)S(1)}) custom-call(s32[7]{0:T(128)S(1)} %stack.31.spot, s32[1,512]{1,0:T(1,128)} %signs.7, f32[1,16,128,512]{3,2,1,0:T(8,128)} %gradient.7, f32[16,128,512]{2,1,0:T(8,128)} %model.1, f32[2,4,32,256]{3,2,1,0:T(8,128)} %get-tuple-element.28.rest_0_, ...), custom_call_target="tpu_custom_call" | custom-call | flops 1 | bytes 1 | tf_op jit(solution)/shard_map/pallas_call | solution.py:151
  12.9 1.8 %shard_map.40 = (f32[2,5,32,256]{3,2,1,0:T(8,128)S(1)}, f32[2,5,32,256]{3,2,1,0:T(8,128)S(1)}) custom-call(s32[7]{0:T(128)S(1)} %stack.31.spot, s32[1,512]{1,0:T(1,128)} %signs.7, f32[1,16,128,512]{3,2,1,0:T(8,128)} %gradient.7, f32[16,32,512]{2,1,0:T(8,128)S(1)} %get-tuple-element.30.rest_0_.base), custom_call_target="tpu_custom_call" | custom-call | flops 1 | bytes 1 | tf_op jit(solution)/shard_map/pallas_call | solution.py:108
  14.6 1.7 %collective-permute-done.2.near_a.refs_0_ = f32[2,7,32,256]{3,2,1,0:T(8,128)S(1)} collective-permute-done((f32[2,7,32,256]{3,2,1,0:T(8,128)S(1)}, f32[2,7,32,256]{3,2,1,0:T(8,128)S(1)}, u32[]{:S(2)}, u32[]{:S(2)}) %collective-permute-start.2) | collective-permute-done | bytes 458784 | tf_op jit(solution)/shard_map/ppermute | solution.py:33
  16.4 2.1 %collective-permute-done.3.near_b.refs_1_ = f32[2,7,32,256]{3,2,1,0:T(8,128)S(1)} collective-permute-done((f32[2,7,32,256]{3,2,1,0:T(8,128)S(1)}, f32[2,7,32,256]{3,2,1,0:T(8,128)S(1)}, u32[]{:S(2)}, u32[]{:S(2)}) %collective-permute-start.3) | collective-permute-done | bytes 458784 | tf_op jit(solution)/shard_map/ppermute | solution.py:37
  18.4 0.8 shard_map.41
  19.3 0.7 copy-done
  20.0 1.5 %collective-permute-start.6 = (f32[7,32,256]{2,1,0:T(8,128)}, f32[7,32,256]{2,1,0:T(8,128)}, u32[]{:S(2)}, u32[]{:S(2)}) collective-permute-start(f32[7,32,256]{2,1,0:T(8,128)} %get-tuple-element.35.rest_2_), channel_id=1, source_target_pairs={{0,16},{16,0},{8,24},{24,8},{1,17},{17,1},{9,25},{25,9},{2,18},{18... | collective-permute-start | bytes 688136 | tf_op jit(solution)/shard_map/ppermute | solution.py:37
  22.0 2.1 %collective-permute-done.1.near_b.refs_1_ = f32[2,4,32,256]{3,2,1,0:T(8,128)} collective-permute-done((f32[2,4,32,256]{3,2,1,0:T(8,128)}, f32[2,4,32,256]{3,2,1,0:T(8,128)}, u32[]{:S(2)}, u32[]{:S(2)}) %collective-permute-start.1) | collective-permute-done | bytes 262176 | tf_op jit(solution)/shard_map/ppermute | solution.py:37
  24.2 1.0 %copy-done.1 = f32[2,5,32,256]{3,2,1,0:T(8,128)S(1)} copy-done((f32[2,5,32,256]{3,2,1,0:T(8,128)S(1)}, f32[2,5,32,256]{3,2,1,0:T(8,128)}, u32[]{:S(2)}) %copy-start.1) | copy-done | bytes 327704
  25.1 1.2 %shard_map.42 = (f32[4,32,256]{2,1,0:T(8,128)S(1)}, f32[4,32,256]{2,1,0:T(8,128)S(1)}, f32[2,5,32,256]{3,2,1,0:T(8,128)S(1)}, f32[2,5,32,256]{3,2,1,0:T(8,128)S(1)}) custom-call(f32[16,32,256]{2,1,0:T(8,128)S(1)} %get-tuple-element.31.fore_a, f32[16,32,256]{2,1,0:T(8,128)S(1)} %get-tuple-element.32.fore_b, ...), custom_call_target="tpu_custom_call" | custom-call | flops 1 | bytes 1 | tf_op jit(solution)/shard_map/pallas_call | solution.py:185
  26.5 2.0 %collective-permute-start.5 = (f32[2,5,32,256]{3,2,1,0:T(8,128)S(1)}, f32[2,5,32,256]{3,2,1,0:T(8,128)S(1)}, u32[]{:S(2)}, u32[]{:S(2)}) collective-permute-start(f32[2,5,32,256]{3,2,1,0:T(8,128)S(1)} %get-tuple-element.38), channel_id=1, source_target_pairs={{0,16},{16,0},{8,24},{24,8},{1,17},{17,1},{9,25},{25,9},{2,18},{18... | collective-permute-start | bytes 983048 | tf_op jit(solution)/shard_map/ppermute | solution.py:37
  28.5 0.8 collective-permute-done.7.refs_3_
  29.4 1.1 %shard_map.43.refs_0_.refs_1_ = f32[7,32,512]{2,1,0:T(8,128)S(1)} custom-call(f32[16,32,512]{2,1,0:T(8,128)S(1)} %get-tuple-element.30.rest_0_.base, f32[2,7,32,256]{3,2,1,0:T(8,128)S(1)} %collective-permute-done.2.near_a.refs_0_, f32[2,7,32,256]{3,2,1,0:T(8,128)S(1)} %collective-permute-done.3.near_b.refs_1_, f32[7,32,256]{2,1,0:T(8,128)} %collective-permute-done.6.refs_2_, ...), custom_call_target="tpu_custom_call" | custom-call | flops 1 | bytes 1 | tf_op jit(solution)/shard_map/pallas_call | solution.py:210
  30.6 1.4 %collective-permute-done.8.refs_1_.refs_0_ = f32[3,32,512]{2,1,0:T(8,128)S(1)} collective-permute-done((f32[3,32,512]{2,1,0:T(8,128)S(1)}, f32[3,32,512]{2,1,0:T(8,128)S(1)}, u32[]{:S(2)}, u32[]{:S(2)}) %collective-permute-start.8) | collective-permute-done | bytes 196640 | tf_op jit(solution)/shard_map/ppermute | solution.py:502
  32.0 0.6 shard_map.44
  32.6 0.7 collective-permute-start.11
  33.3 0.7 collective-permute-start.12
  34.0 0.8 collective-permute-done.4.near_a.refs_2_
  34.8 2.6 %collective-permute-start.10 = (f32[9,32,256]{2,1,0:T(8,128)S(1)}, f32[9,32,256]{2,1,0:T(8,128)S(1)}, u32[]{:S(2)}, u32[]{:S(2)}) collective-permute-start(f32[9,32,256]{2,1,0:T(8,128)S(1)} %get-tuple-element.44.refs_5_), channel_id=1, source_target_pairs={{0,8},{8,0},{16,24},{24,16},{1,9},{9,1},{17,25},{25,17},{2,10},{10... | collective-permute-start | bytes 884744 | tf_op jit(solution)/shard_map/ppermute | solution.py:33
  37.4 1.3 %collective-permute-start.9 = (f32[9,32,256]{2,1,0:T(8,128)S(1)}, f32[9,32,256]{2,1,0:T(8,128)S(1)}, u32[]{:S(2)}, u32[]{:S(2)}) collective-permute-start(f32[9,32,256]{2,1,0:T(8,128)S(1)} %get-tuple-element.43.refs_4_), channel_id=1, source_target_pairs={{0,16},{16,0},{8,24},{24,8},{1,17},{17,1},{9,25},{25,9},{2,18},{18... | collective-permute-start | bytes 884744 | tf_op jit(solution)/shard_map/ppermute | solution.py:37
  38.8 4.5 %shard_map.46.refs_6_.refs_0_ = f32[2,4,32,256]{3,2,1,0:T(8,128)S(1)} custom-call(s32[7]{0:T(128)S(1)} %stack.31.spot, f32[3,32,512]{2,1,0:T(8,128)S(1)} %collective-permute-done.8.refs_1_.refs_0_, f32[7,32,512]{2,1,0:T(8,128)S(1)} %shard_map.43.refs_0_.refs_1_, f32[10,3,512]{2,1,0:T(4,128)S(1)} %collective-permute-done.11.refs_2_, ...), custom_call_target="tpu_custom_call" | custom-call | flops 1 | bytes 100000000 | tf_op jit(solution)/shard_map/pallas_call | solution.py:353
  43.3 2.4 %collective-permute-start.16 = (f32[2,4,32,256]{3,2,1,0:T(8,128)S(1)}, f32[2,4,32,256]{3,2,1,0:T(8,128)S(1)}, u32[]{:S(2)}, u32[]{:S(2)}) collective-permute-start(f32[2,4,32,256]{3,2,1,0:T(8,128)S(1)} %shard_map.46.refs_6_.refs_0_), channel_id=1, source_target_pairs={{0,16},{16,0},{8,24},{24,8},{1,17},{17,1},{9,25},{25,9},{2,18},{18... | collective-permute-start | bytes 786440 | tf_op jit(solution)/shard_map/ppermute | solution.py:37
  45.7 0.6 collective-permute-start.15
  46.3 1.1 %shard_map.47.refs_0_.refs_1_ = f32[9,32,512]{2,1,0:T(8,128)S(1)} custom-call(f32[16,32,512]{2,1,0:T(8,128)S(1)} %get-tuple-element.30.rest_0_.base, f32[2,4,32,256]{3,2,1,0:T(8,128)} %collective-permute-done.near_a.refs_0_, f32[2,4,32,256]{3,2,1,0:T(8,128)} %collective-permute-done.1.near_b.refs_1_, ...), custom_call_target="tpu_custom_call" | custom-call | flops 1 | bytes 1 | tf_op jit(solution)/shard_map/pallas_call | solution.py:210
  47.5 0.6 shard_map.48
  48.0 1.5 %collective-permute-start.13 = (f32[9,3,512]{2,1,0:T(4,128)S(1)}, f32[9,3,512]{2,1,0:T(4,128)S(1)}, u32[]{:S(2)}, u32[]{:S(2)}) collective-permute-start(f32[9,3,512]{2,1,0:T(4,128)S(1)} %get-tuple-element.45), channel_id=1, source_target_pairs={{0,8},{8,0},{24,16},{16,24},{1,9},{9,1},{25,17},{17,25},{2,10},{10... | collective-permute-start | bytes 165896 | tf_op jit(solution)/shard_map/ppermute | solution.py:454
  49.5 0.7 collective-permute-start.14
  50.2 1.1 %collective-permute-done.16.refs_5_.refs_4_ = f32[2,4,32,256]{3,2,1,0:T(8,128)S(1)} collective-permute-done((f32[2,4,32,256]{3,2,1,0:T(8,128)S(1)}, f32[2,4,32,256]{3,2,1,0:T(8,128)S(1)}, u32[]{:S(2)}, u32[]{:S(2)}) %collective-permute-start.16) | collective-permute-done | bytes 262176 | tf_op jit(solution)/shard_map/ppermute | solution.py:37
  51.3 2.7 %collective-permute-start.27 = (f32[4,32,256]{2,1,0:T(8,128)S(1)}, f32[4,32,256]{2,1,0:T(8,128)S(1)}, u32[]{:S(2)}, u32[]{:S(2)}) collective-permute-start(f32[4,32,256]{2,1,0:T(8,128)S(1)} %slice_bitcast_fusion.5), channel_id=1, source_target_pairs={{0,8},{8,0},{16,24},{24,16},{1,9},{9,1},{17,25},{25,17},{2,10},{10... | collective-permute-start | bytes 393224 | tf_op jit(solution)/shard_map/ppermute | solution.py:33
  54.0 1.3 %collective-permute-done.13.refs_3_.refs_1_ = f32[9,3,512]{2,1,0:T(4,128)S(1)} collective-permute-done((f32[9,3,512]{2,1,0:T(4,128)S(1)}, f32[9,3,512]{2,1,0:T(4,128)S(1)}, u32[]{:S(2)}, u32[]{:S(2)}) %collective-permute-start.13) | collective-permute-done | bytes 55328 | tf_op jit(solution)/shard_map/ppermute | solution.py:454
  55.3 5.7 %shard_map.49.refs_3_.refs_0_ = f32[2,6,32,256]{3,2,1,0:T(8,128)S(1)} custom-call(s32[7]{0:T(128)S(1)} %stack.31.spot, f32[7,32,512]{2,1,0:T(8,128)S(1)} %shard_map.43.refs_0_.refs_1_, f32[9,32,512]{2,1,0:T(8,128)S(1)} %shard_map.47.refs_0_.refs_1_, f32[10,3,512]{2,1,0:T(4,128)S(1)} %collective-permute-done.11.refs_2_, ...), custom_call_target="tpu_custom_call" | custom-call | flops 1 | bytes 100000000 | tf_op jit(solution)/shard_map/pallas_call | solution.py:353
  61.0 3.3 %collective-permute-start.24 = (f32[2,6,32,256]{3,2,1,0:T(8,128)S(1)}, f32[2,6,32,256]{3,2,1,0:T(8,128)S(1)}, u32[]{:S(2)}, u32[]{:S(2)}) collective-permute-start(f32[2,6,32,256]{3,2,1,0:T(8,128)S(1)} %shard_map.49.refs_3_.refs_0_), channel_id=1, source_target_pairs={{0,16},{16,0},{8,24},{24,8},{1,17},{17,1},{9,25},{25,9},{2,18},{18... | collective-permute-start | bytes 1179656 | tf_op jit(solution)/shard_map/ppermute | solution.py:37
  64.4 5.7 %shard_map.50.refs_0_ = f32[2,6,32,256]{3,2,1,0:T(8,128)S(1)} custom-call(s32[7]{0:T(128)S(1)} %stack.31.spot, f32[9,32,512]{2,1,0:T(8,128)S(1)} %shard_map.47.refs_0_.refs_1_, f32[9,3,512]{2,1,0:T(4,128)S(1)} %collective-permute-done.13.refs_3_.refs_1_, f32[9,3,512]{2,1,0:T(4,128)S(1)} %collective-permute-done.14.refs_5_.refs_2_, ...), custom_call_target="tpu_custom_call" | custom-call | flops 1 | bytes 100000000 | tf_op jit(solution)/shard_map/pallas_call | solution.py:353
  70.1 2.0 %collective-permute-start.19 = (f32[6,32,256]{2,1,0:T(8,128)S(1)}, f32[6,32,256]{2,1,0:T(8,128)S(1)}, u32[]{:S(2)}, u32[]{:S(2)}) collective-permute-start(f32[6,32,256]{2,1,0:T(8,128)S(1)} %get-tuple-element.48), channel_id=1, source_target_pairs={{0,16},{16,0},{8,24},{24,8},{1,17},{17,1},{9,25},{25,9},{2,18},{18... | collective-permute-start | bytes 589832 | tf_op jit(solution)/shard_map/ppermute | solution.py:37
  72.5 1.6 %collective-permute-start.18 = (f32[6,32,256]{2,1,0:T(8,128)S(1)}, f32[6,32,256]{2,1,0:T(8,128)S(1)}, u32[]{:S(2)}, u32[]{:S(2)}) collective-permute-start(f32[6,32,256]{2,1,0:T(8,128)S(1)} %get-tuple-element.47), channel_id=1, source_target_pairs={{0,8},{8,0},{16,24},{24,16},{1,9},{9,1},{17,25},{25,17},{2,10},{10... | collective-permute-start | bytes 589832 | tf_op jit(solution)/shard_map/ppermute | solution.py:33
  74.7 1.7 %collective-permute-start.17 = (f32[6,32,256]{2,1,0:T(8,128)S(1)}, f32[6,32,256]{2,1,0:T(8,128)S(1)}, u32[]{:S(2)}, u32[]{:S(2)}) collective-permute-start(f32[6,32,256]{2,1,0:T(8,128)S(1)} %get-tuple-element.48), channel_id=1, source_target_pairs={{0,8},{8,0},{16,24},{24,16},{1,9},{9,1},{17,25},{25,17},{2,10},{10... | collective-permute-start | bytes 589832 | tf_op jit(solution)/shard_map/ppermute | solution.py:33
  76.4 3.0 %collective-permute-start.26 = (f32[6,32,256]{2,1,0:T(8,128)S(1)}, f32[6,32,256]{2,1,0:T(8,128)S(1)}, u32[]{:S(2)}, u32[]{:S(2)}) collective-permute-start(f32[6,32,256]{2,1,0:T(8,128)S(1)} %slice_bitcast_fusion), channel_id=1, source_target_pairs={{0,16},{16,0},{8,24},{24,8},{1,17},{17,1},{9,25},{25,9},{2,18},{18... | collective-permute-start | bytes 589832 | tf_op jit(solution)/shard_map/ppermute | solution.py:37
  79.6 2.2 %collective-permute-start.22 = (f32[6,32,256]{2,1,0:T(8,128)S(1)}, f32[6,32,256]{2,1,0:T(8,128)S(1)}, u32[]{:S(2)}, u32[]{:S(2)}) collective-permute-start(f32[6,32,256]{2,1,0:T(8,128)S(1)} %get-tuple-element.47), channel_id=1, source_target_pairs={{0,16},{16,0},{8,24},{24,8},{1,17},{17,1},{9,25},{25,9},{2,18},{18... | collective-permute-start | bytes 589832 | tf_op jit(solution)/shard_map/ppermute | solution.py:37
  82.0 2.6 %collective-permute-done.25.refs_2_ = f32[6,32,256]{2,1,0:T(8,128)S(1)} collective-permute-done((f32[6,32,256]{2,1,0:T(8,128)S(1)}, f32[6,32,256]{2,1,0:T(8,128)S(1)}, u32[]{:S(2)}, u32[]{:S(2)}) %collective-permute-start.25) | collective-permute-done | bytes 196640 | tf_op jit(solution)/shard_map/ppermute | solution.py:33
  84.6 2.2 %collective-permute-start.21 = (f32[6,32,256]{2,1,0:T(8,128)S(1)}, f32[6,32,256]{2,1,0:T(8,128)S(1)}, u32[]{:S(2)}, u32[]{:S(2)}) collective-permute-start(f32[6,32,256]{2,1,0:T(8,128)S(1)} %collective-permute-done.18.refs_2_), channel_id=1, source_target_pairs={{0,16},{16,0},{8,24},{24,8},{1,17},{17,1},{9,25},{25,9},{2,18},{18... | collective-permute-start | bytes 589832 | tf_op jit(solution)/shard_map/ppermute | solution.py:37
  86.8 1.6 %shard_map.51.refs_5_ = f32[16,128,512]{2,1,0:T(8,128)} custom-call(s32[7]{0:T(128)S(1)} %stack.31.spot, f32[2,4,32,256]{3,2,1,0:T(8,128)S(1)} %shard_map.46.refs_6_.refs_0_, f32[2,4,32,256]{3,2,1,0:T(8,128)S(1)} %collective-permute-done.15.refs_4_.refs_1_, f32[4,32,256]{2,1,0:T(8,128)S(1)} %collective-permute-done.27.refs_2_, ...), custom_call_target="tpu_custom_call" | custom-call | flops 1 | bytes 1 | tf_op jit(solution)/shard_map/pallas_call | solution.py:383
  88.4 1.8 %shard_map.52.refs_7_ = f32[16,128,512]{2,1,0:T(8,128)} custom-call(s32[7]{0:T(128)S(1)} %stack.31.spot, f32[2,6,32,256]{3,2,1,0:T(8,128)S(1)} %shard_map.49.refs_3_.refs_0_, f32[2,6,32,256]{3,2,1,0:T(8,128)S(1)} %collective-permute-done.23.refs_1_, f32[6,32,256]{2,1,0:T(8,128)S(1)} %collective-permute-done.25.refs_2_, ...), custom_call_target="tpu_custom_call", output_to_operand_aliasing={{}: (6, {})} | custom-call | flops 1 | bytes 1 | tf_op jit(solution)/shard_map/pallas_call | solution.py:383
  90.4 1.7 %shard_map.53 = f32[16,128,512]{2,1,0:T(8,128)} custom-call(s32[7]{0:T(128)S(1)} %stack.31.spot, f32[2,6,32,256]{3,2,1,0:T(8,128)S(1)} %shard_map.50.refs_0_, f32[6,32,256]{2,1,0:T(8,128)S(1)} %collective-permute-done.17.refs_1_, f32[6,32,256]{2,1,0:T(8,128)S(1)} %collective-permute-done.18.refs_2_, ...), custom_call_target="tpu_custom_call", output_to_operand_aliasing={{}: (8, {})} | custom-call | flops 1 | bytes 1 | tf_op jit(solution)/shard_map/pallas_call | solution.py:383
  (38 shorter events, 2.8 us)
Async XLA Ops:
  2.0 14.4 %collective-permute-start.2 = (f32[2,7,32,256]{3,2,1,0:T(8,128)S(1)}, f32[2,7,32,256]{3,2,1,0:T(8,128)S(1)}, u32[]{:S(2)}, u32[]{:S(2)}) collective-permute-start(f32[2,7,32,256]{3,2,1,0:T(8,128)S(1)} %get-tuple-element.26.rest_0_), channel_id=1, source_target_pairs={{0,8},{8,0},{16,24},{24,16},{1,9},{9,1},{17,25},{25,17},{2,10},{10... | collective-permute-start | bytes 1376264 | tf_op jit(solution)/shard_map/ppermute | solution.py:33
  5.0 13.4 %collective-permute-start.3 = (f32[2,7,32,256]{3,2,1,0:T(8,128)S(1)}, f32[2,7,32,256]{3,2,1,0:T(8,128)S(1)}, u32[]{:S(2)}, u32[]{:S(2)}) collective-permute-start(f32[2,7,32,256]{3,2,1,0:T(8,128)S(1)} %get-tuple-element.27.rest_1_), channel_id=1, source_target_pairs={{0,16},{16,0},{8,24},{24,8},{1,17},{17,1},{9,25},{25,9},{2,18},{18... | collective-permute-start | bytes 1376264 | tf_op jit(solution)/shard_map/ppermute | solution.py:37
  9.0 13.0 %collective-permute-start = (f32[2,4,32,256]{3,2,1,0:T(8,128)}, f32[2,4,32,256]{3,2,1,0:T(8,128)}, u32[]{:S(2)}, u32[]{:S(2)}) collective-permute-start(f32[2,4,32,256]{3,2,1,0:T(8,128)} %get-tuple-element.28.rest_0_), channel_id=1, source_target_pairs={{0,8},{8,0},{16,24},{24,16},{1,9},{9,1},{17,25},{25,17},{2,10},{10... | collective-permute-start | bytes 786440 | tf_op jit(solution)/shard_map/ppermute | solution.py:33
  9.6 14.5 %collective-permute-start.1 = (f32[2,4,32,256]{3,2,1,0:T(8,128)}, f32[2,4,32,256]{3,2,1,0:T(8,128)}, u32[]{:S(2)}, u32[]{:S(2)}) collective-permute-start(f32[2,4,32,256]{3,2,1,0:T(8,128)} %get-tuple-element.29.rest_1_), channel_id=1, source_target_pairs={{0,16},{16,0},{8,24},{24,8},{1,17},{17,1},{9,25},{25,9},{2,18},{18... | collective-permute-start | bytes 786440 | tf_op jit(solution)/shard_map/ppermute | solution.py:37
  19.3 0.7 copy-start
  20.0 8.5 %collective-permute-start.6 = (f32[7,32,256]{2,1,0:T(8,128)}, f32[7,32,256]{2,1,0:T(8,128)}, u32[]{:S(2)}, u32[]{:S(2)}) collective-permute-start(f32[7,32,256]{2,1,0:T(8,128)} %get-tuple-element.35.rest_2_), channel_id=1, source_target_pairs={{0,16},{16,0},{8,24},{24,8},{1,17},{17,1},{9,25},{25,9},{2,18},{18... | collective-permute-start | bytes 688136 | tf_op jit(solution)/shard_map/ppermute | solution.py:37
  21.5 7.9 %collective-permute-start.7 = (f32[7,32,256]{2,1,0:T(8,128)}, f32[7,32,256]{2,1,0:T(8,128)}, u32[]{:S(2)}, u32[]{:S(2)}) collective-permute-start(f32[7,32,256]{2,1,0:T(8,128)} %get-tuple-element.36.rest_3_), channel_id=1, source_target_pairs={{0,8},{8,0},{16,24},{24,16},{1,9},{9,1},{17,25},{25,17},{2,10},{10... | collective-permute-start | bytes 688136 | tf_op jit(solution)/shard_map/ppermute | solution.py:33
  24.2 1.0 %copy-start.1 = (f32[2,5,32,256]{3,2,1,0:T(8,128)S(1)}, f32[2,5,32,256]{3,2,1,0:T(8,128)}, u32[]{:S(2)}) copy-start(f32[2,5,32,256]{3,2,1,0:T(8,128)} %copy-done) | copy-start | bytes 983044
  26.4 8.4 %collective-permute-start.4 = (f32[2,5,32,256]{3,2,1,0:T(8,128)S(1)}, f32[2,5,32,256]{3,2,1,0:T(8,128)S(1)}, u32[]{:S(2)}, u32[]{:S(2)}) collective-permute-start(f32[2,5,32,256]{3,2,1,0:T(8,128)S(1)} %get-tuple-element.37), channel_id=1, source_target_pairs={{0,8},{8,0},{16,24},{24,16},{1,9},{9,1},{17,25},{25,17},{2,10},{10... | collective-permute-start | bytes 983048 | tf_op jit(solution)/shard_map/ppermute | solution.py:33
  26.5 8.3 %collective-permute-start.5 = (f32[2,5,32,256]{3,2,1,0:T(8,128)S(1)}, f32[2,5,32,256]{3,2,1,0:T(8,128)S(1)}, u32[]{:S(2)}, u32[]{:S(2)}) collective-permute-start(f32[2,5,32,256]{3,2,1,0:T(8,128)S(1)} %get-tuple-element.38), channel_id=1, source_target_pairs={{0,16},{16,0},{8,24},{24,8},{1,17},{17,1},{9,25},{25,9},{2,18},{18... | collective-permute-start | bytes 983048 | tf_op jit(solution)/shard_map/ppermute | solution.py:37
  30.5 1.5 %collective-permute-start.8 = (f32[3,32,512]{2,1,0:T(8,128)S(1)}, f32[3,32,512]{2,1,0:T(8,128)S(1)}, u32[]{:S(2)}, u32[]{:S(2)}) collective-permute-start(f32[3,32,512]{2,1,0:T(8,128)S(1)} %constant_dynamic-slice_fusion), channel_id=1, source_target_pairs={{0,4},{4,0},{1,5},{5,1},{2,6},{6,2},{3,7},{7,3},{8,12},{12,8},{9,1... | collective-permute-start | bytes 589832 | tf_op jit(solution)/shard_map/ppermute | solution.py:502
  32.6 6.2 %collective-permute-start.11 = (f32[10,3,512]{2,1,0:T(4,128)S(1)}, f32[10,3,512]{2,1,0:T(4,128)S(1)}, u32[]{:S(2)}, u32[]{:S(2)}) collective-permute-start(f32[10,3,512]{2,1,0:T(4,128)S(1)} %get-tuple-element.41.rest_2_), channel_id=1, source_target_pairs={{0,8},{8,0},{24,16},{16,24},{1,9},{9,1},{25,17},{17,25},{2,10},{10... | collective-permute-start | bytes 184328 | tf_op jit(solution)/shard_map/ppermute | solution.py:454
  33.3 5.5 %collective-permute-start.12 = (f32[10,3,512]{2,1,0:T(4,128)S(1)}, f32[10,3,512]{2,1,0:T(4,128)S(1)}, u32[]{:S(2)}, u32[]{:S(2)}) collective-permute-start(f32[10,3,512]{2,1,0:T(4,128)S(1)} %get-tuple-element.42.rest_3_), channel_id=1, source_target_pairs={{8,24},{24,8},{16,1},{1,16},{9,25},{25,9},{17,2},{2,17},{10,26},{2... | collective-permute-start | bytes 184328 | tf_op jit(solution)/shard_map/ppermute | solution.py:454
  34.8 11.5 %collective-permute-start.10 = (f32[9,32,256]{2,1,0:T(8,128)S(1)}, f32[9,32,256]{2,1,0:T(8,128)S(1)}, u32[]{:S(2)}, u32[]{:S(2)}) collective-permute-start(f32[9,32,256]{2,1,0:T(8,128)S(1)} %get-tuple-element.44.refs_5_), channel_id=1, source_target_pairs={{0,8},{8,0},{16,24},{24,16},{1,9},{9,1},{17,25},{25,17},{2,10},{10... | collective-permute-start | bytes 884744 | tf_op jit(solution)/shard_map/ppermute | solution.py:33
  37.4 8.9 %collective-permute-start.9 = (f32[9,32,256]{2,1,0:T(8,128)S(1)}, f32[9,32,256]{2,1,0:T(8,128)S(1)}, u32[]{:S(2)}, u32[]{:S(2)}) collective-permute-start(f32[9,32,256]{2,1,0:T(8,128)S(1)} %get-tuple-element.43.refs_4_), channel_id=1, source_target_pairs={{0,16},{16,0},{8,24},{24,8},{1,17},{17,1},{9,25},{25,9},{2,18},{18... | collective-permute-start | bytes 884744 | tf_op jit(solution)/shard_map/ppermute | solution.py:37
  43.3 7.9 %collective-permute-start.16 = (f32[2,4,32,256]{3,2,1,0:T(8,128)S(1)}, f32[2,4,32,256]{3,2,1,0:T(8,128)S(1)}, u32[]{:S(2)}, u32[]{:S(2)}) collective-permute-start(f32[2,4,32,256]{3,2,1,0:T(8,128)S(1)} %shard_map.46.refs_6_.refs_0_), channel_id=1, source_target_pairs={{0,16},{16,0},{8,24},{24,8},{1,17},{17,1},{9,25},{25,9},{2,18},{18... | collective-permute-start | bytes 786440 | tf_op jit(solution)/shard_map/ppermute | solution.py:37
  45.7 18.6 %collective-permute-start.15 = (f32[2,4,32,256]{3,2,1,0:T(8,128)S(1)}, f32[2,4,32,256]{3,2,1,0:T(8,128)S(1)}, u32[]{:S(2)}, u32[]{:S(2)}) collective-permute-start(f32[2,4,32,256]{3,2,1,0:T(8,128)S(1)} %shard_map.46.refs_6_.refs_0_), channel_id=1, source_target_pairs={{0,8},{8,0},{16,24},{24,16},{1,9},{9,1},{17,25},{25,17},{2,10},{10... | collective-permute-start | bytes 786440 | tf_op jit(solution)/shard_map/ppermute | solution.py:33
  48.0 7.2 %collective-permute-start.13 = (f32[9,3,512]{2,1,0:T(4,128)S(1)}, f32[9,3,512]{2,1,0:T(4,128)S(1)}, u32[]{:S(2)}, u32[]{:S(2)}) collective-permute-start(f32[9,3,512]{2,1,0:T(4,128)S(1)} %get-tuple-element.45), channel_id=1, source_target_pairs={{0,8},{8,0},{24,16},{16,24},{1,9},{9,1},{25,17},{17,25},{2,10},{10... | collective-permute-start | bytes 165896 | tf_op jit(solution)/shard_map/ppermute | solution.py:454
  49.5 5.8 %collective-permute-start.14 = (f32[9,3,512]{2,1,0:T(4,128)S(1)}, f32[9,3,512]{2,1,0:T(4,128)S(1)}, u32[]{:S(2)}, u32[]{:S(2)}) collective-permute-start(f32[9,3,512]{2,1,0:T(4,128)S(1)} %get-tuple-element.46), channel_id=1, source_target_pairs={{8,24},{24,8},{16,1},{1,16},{9,25},{25,9},{17,2},{2,17},{10,26},{2... | collective-permute-start | bytes 165896 | tf_op jit(solution)/shard_map/ppermute | solution.py:454
  51.3 23.4 %collective-permute-start.27 = (f32[4,32,256]{2,1,0:T(8,128)S(1)}, f32[4,32,256]{2,1,0:T(8,128)S(1)}, u32[]{:S(2)}, u32[]{:S(2)}) collective-permute-start(f32[4,32,256]{2,1,0:T(8,128)S(1)} %slice_bitcast_fusion.5), channel_id=1, source_target_pairs={{0,8},{8,0},{16,24},{24,16},{1,9},{9,1},{17,25},{25,17},{2,10},{10... | collective-permute-start | bytes 393224 | tf_op jit(solution)/shard_map/ppermute | solution.py:33
  61.0 11.6 %collective-permute-start.24 = (f32[2,6,32,256]{3,2,1,0:T(8,128)S(1)}, f32[2,6,32,256]{3,2,1,0:T(8,128)S(1)}, u32[]{:S(2)}, u32[]{:S(2)}) collective-permute-start(f32[2,6,32,256]{3,2,1,0:T(8,128)S(1)} %shard_map.49.refs_3_.refs_0_), channel_id=1, source_target_pairs={{0,16},{16,0},{8,24},{24,8},{1,17},{17,1},{9,25},{25,9},{2,18},{18... | collective-permute-start | bytes 1179656 | tf_op jit(solution)/shard_map/ppermute | solution.py:37
  64.3 12.1 %collective-permute-start.28 = (f32[4,32,256]{2,1,0:T(8,128)S(1)}, f32[4,32,256]{2,1,0:T(8,128)S(1)}, u32[]{:S(2)}, u32[]{:S(2)}) collective-permute-start(f32[4,32,256]{2,1,0:T(8,128)S(1)} %slice_bitcast_fusion.4), channel_id=1, source_target_pairs={{0,16},{16,0},{8,24},{24,8},{1,17},{17,1},{9,25},{25,9},{2,18},{18... | collective-permute-start | bytes 393224 | tf_op jit(solution)/shard_map/ppermute | solution.py:37
  64.4 9.8 %collective-permute-start.23 = (f32[2,6,32,256]{3,2,1,0:T(8,128)S(1)}, f32[2,6,32,256]{3,2,1,0:T(8,128)S(1)}, u32[]{:S(2)}, u32[]{:S(2)}) collective-permute-start(f32[2,6,32,256]{3,2,1,0:T(8,128)S(1)} %shard_map.49.refs_3_.refs_0_), channel_id=1, source_target_pairs={{0,8},{8,0},{16,24},{24,16},{1,9},{9,1},{17,25},{25,17},{2,10},{10... | collective-permute-start | bytes 1179656 | tf_op jit(solution)/shard_map/ppermute | solution.py:33
  70.1 9.4 %collective-permute-start.19 = (f32[6,32,256]{2,1,0:T(8,128)S(1)}, f32[6,32,256]{2,1,0:T(8,128)S(1)}, u32[]{:S(2)}, u32[]{:S(2)}) collective-permute-start(f32[6,32,256]{2,1,0:T(8,128)S(1)} %get-tuple-element.48), channel_id=1, source_target_pairs={{0,16},{16,0},{8,24},{24,8},{1,17},{17,1},{9,25},{25,9},{2,18},{18... | collective-permute-start | bytes 589832 | tf_op jit(solution)/shard_map/ppermute | solution.py:37
  72.5 9.2 %collective-permute-start.18 = (f32[6,32,256]{2,1,0:T(8,128)S(1)}, f32[6,32,256]{2,1,0:T(8,128)S(1)}, u32[]{:S(2)}, u32[]{:S(2)}) collective-permute-start(f32[6,32,256]{2,1,0:T(8,128)S(1)} %get-tuple-element.47), channel_id=1, source_target_pairs={{0,8},{8,0},{16,24},{24,16},{1,9},{9,1},{17,25},{25,17},{2,10},{10... | collective-permute-start | bytes 589832 | tf_op jit(solution)/shard_map/ppermute | solution.py:33
  74.2 10.4 %collective-permute-start.25 = (f32[6,32,256]{2,1,0:T(8,128)S(1)}, f32[6,32,256]{2,1,0:T(8,128)S(1)}, u32[]{:S(2)}, u32[]{:S(2)}) collective-permute-start(f32[6,32,256]{2,1,0:T(8,128)S(1)} %slice_bitcast_fusion.1), channel_id=1, source_target_pairs={{0,8},{8,0},{16,24},{24,16},{1,9},{9,1},{17,25},{25,17},{2,10},{10... | collective-permute-start | bytes 589832 | tf_op jit(solution)/shard_map/ppermute | solution.py:33
  74.7 15.4 %collective-permute-start.17 = (f32[6,32,256]{2,1,0:T(8,128)S(1)}, f32[6,32,256]{2,1,0:T(8,128)S(1)}, u32[]{:S(2)}, u32[]{:S(2)}) collective-permute-start(f32[6,32,256]{2,1,0:T(8,128)S(1)} %get-tuple-element.48), channel_id=1, source_target_pairs={{0,8},{8,0},{16,24},{24,16},{1,9},{9,1},{17,25},{25,17},{2,10},{10... | collective-permute-start | bytes 589832 | tf_op jit(solution)/shard_map/ppermute | solution.py:33
  76.4 12.0 %collective-permute-start.26 = (f32[6,32,256]{2,1,0:T(8,128)S(1)}, f32[6,32,256]{2,1,0:T(8,128)S(1)}, u32[]{:S(2)}, u32[]{:S(2)}) collective-permute-start(f32[6,32,256]{2,1,0:T(8,128)S(1)} %slice_bitcast_fusion), channel_id=1, source_target_pairs={{0,16},{16,0},{8,24},{24,8},{1,17},{17,1},{9,25},{25,9},{2,18},{18... | collective-permute-start | bytes 589832 | tf_op jit(solution)/shard_map/ppermute | solution.py:37
  79.6 10.6 %collective-permute-start.22 = (f32[6,32,256]{2,1,0:T(8,128)S(1)}, f32[6,32,256]{2,1,0:T(8,128)S(1)}, u32[]{:S(2)}, u32[]{:S(2)}) collective-permute-start(f32[6,32,256]{2,1,0:T(8,128)S(1)} %get-tuple-element.47), channel_id=1, source_target_pairs={{0,16},{16,0},{8,24},{24,8},{1,17},{17,1},{9,25},{25,9},{2,18},{18... | collective-permute-start | bytes 589832 | tf_op jit(solution)/shard_map/ppermute | solution.py:37
  81.7 8.4 %collective-permute-start.20 = (f32[6,32,256]{2,1,0:T(8,128)S(1)}, f32[6,32,256]{2,1,0:T(8,128)S(1)}, u32[]{:S(2)}, u32[]{:S(2)}) collective-permute-start(f32[6,32,256]{2,1,0:T(8,128)S(1)} %collective-permute-done.19.refs_5_), channel_id=1, source_target_pairs={{0,8},{8,0},{16,24},{24,16},{1,9},{9,1},{17,25},{25,17},{2,10},{10... | collective-permute-start | bytes 589832 | tf_op jit(solution)/shard_map/ppermute | solution.py:33
  84.6 5.8 %collective-permute-start.21 = (f32[6,32,256]{2,1,0:T(8,128)S(1)}, f32[6,32,256]{2,1,0:T(8,128)S(1)}, u32[]{:S(2)}, u32[]{:S(2)}) collective-permute-start(f32[6,32,256]{2,1,0:T(8,128)S(1)} %collective-permute-done.18.refs_2_), channel_id=1, source_target_pairs={{0,16},{16,0},{8,24},{24,8},{1,17},{17,1},{9,25},{25,9},{2,18},{18... | collective-permute-start | bytes 589832 | tf_op jit(solution)/shard_map/ppermute | solution.py:37

commit v4 on v3

--- a/solution.py
+++ b/solution.py
@@ -193,9 +193,9 @@
     return outs[:2], outs[2:]
 
 
-def settle_kernel(chunks, after, base, *refs):
+def settle_kernel(chunks, edges, after, spot, base, *refs):
     nears, (far_a, far_b) = (refs[: 2 * len(chunks)], refs[2 * len(chunks) : 2 * len(chunks) + 2])
-    out = refs[-1]
+    out, *sides = refs[2 * len(chunks) + 2 + after :]
     half = far_a.shape[2]
     at = 0
     for k, (start, count) in enumerate(chunks):
@@ -203,18 +203,26 @@
         for side, near, far in ((slice(0, half), nears[2 * k], far_a), (slice(half, 2 * half), nears[2 * k + 1], far_b)):
             out[here, :, side] = base[start : start + count, :, side] - rate * (near[0] + far[here])
         at += count
-
-
-def settle(chunks, base, nears, fars, after=()):
+    if edges:
+        odd = spot[0] % 2 == 1
+        for p in range(out.shape[0]):
+            last = out[p, out.shape[1] - HALO :]
+            first = out[p, :HALO]
+            sides[0][p] = jnp.where(odd, first, last)
+            sides[1][p] = jnp.where(odd, last, first)
+
+
+def settle(chunks, spot, base, nears, fars, after=(), edges=False):
     count, share, half = fars[0].shape
-    return pl.pallas_call(
-        functools.partial(settle_kernel, chunks, len(after)),
-        in_specs=[WHOLE] * (3 + len(nears)) + [WHOLE] * len(after),
-        out_specs=WHOLE,
-        out_shape=jax.ShapeDtypeStruct((count, share, 2 * half), jnp.float32),
+    shapes = [(count, share, 2 * half)] + ([(count, HALO, 2 * half)] * 2 if edges else [])
+    return pl.pallas_call(
+        functools.partial(settle_kernel, chunks, edges, len(after)),
+        in_specs=[SCALARS] + [WHOLE] * (3 + len(nears) + len(after)),
+        out_specs=[WHOLE] * len(shapes),
+        out_shape=[jax.ShapeDtypeStruct(shape, jnp.float32) for shape in shapes],
         compiler_params=params(),
         cost_estimate=COST,
-    )(base, *near_core((*nears, *fars, *after)))
+    )(spot, base, *near_core((*nears, *fars, *after)))
 
 
 def pack_kernel(count, spot, *refs):
@@ -291,58 +299,58 @@
         def plane(p, carry):
             place = start_z + p
             coef_z = jnp.where((place >= 0) & (place <= total_z - 2), jnp.float32(step_sigma), jnp.float32(0))
-            tile = [source[p, tile_rows(t)] for t in range(tiles + 1)]
+            rows_of = [tile_rows(t) for t in range(tiles + 1)]
+            tile = [source[p, here] for here in rows_of]
+            below = [source[p + 1, here] for here in rows_of]
+            before_z = [dual[0, max(p - 1, 0), here] for here in rows_of]
+            if step > 0:
+                olds = [[dual[i, p, here] for here in rows_of] for i in range(3)]
+                old_value = [old[p, here] for here in rows_of]
+                goal = [target[p, here] for here in rows_of]
+            else:
+                old_value, goal = (tile, tile)
             turned = [pltpu.roll(v, SIDE - 1, 0) for v in tile]
-
-            def steps_of(t):
-                here = tile_rows(t)
+            aside = [pltpu.roll(v, cols - 1, 1) for v in tile]
+            all_steps = []
+            for t in range(tiles + 1):
                 v = tile[t]
                 beyond = turned[(t + 1) % (tiles + 1)]
-                step_z = coef_z * (source[p + 1, here] - v)
+                step_z = coef_z * (below[t] - v)
                 step_x = edge_x.get(t, jnp.float32(step_sigma)) * (jnp.where(last_row, beyond, turned[t]) - v)
-                step_y = coef_y * (pltpu.roll(v, cols - 1, 1) - v)
+                step_y = coef_y * (aside[t] - v)
                 if step > 0:
-                    step_z = step_z + dual[0, p, here]
-                    step_x = step_x + dual[1, p, here]
-                    step_y = step_y + dual[2, p, here]
+                    step_z = step_z + olds[0][t]
+                    step_x = step_x + olds[1][t]
+                    step_y = step_y + olds[2][t]
                 square = step_z * step_z + step_x * step_x + step_y * step_y
                 scale = jnp.minimum(jnp.float32(1), jnp.float32(radius) * lax.rsqrt(square))
-                step_z, step_x, step_y = (step_z * scale, step_x * scale, step_y * scale)
-                dual[0, p, here] = step_z
+                all_steps.append((step_z * scale, step_x * scale, step_y * scale))
+            moved = [pltpu.roll(steps[1], 1, 0) for steps in all_steps]
+            aside = [pltpu.roll(steps[2], 1, 1) for steps in all_steps]
+            news = []
+            needed = 0 if p == step else tiles + 1 if step < ITERS - 1 else tiles
+            for t in range(needed):
+                step_z, step_x, step_y = all_steps[t]
+                last_x = moved[t - 1 if t else tiles]
+                diverge = (step_z - before_z[t]) + (step_x - jnp.where(first_row, last_x, moved[t])) + (step_y - aside[t])
+                news.append(jnp.float32(keep_old) * old_value[t] + jnp.float32(take_new) * (diverge + goal[t]))
+            for t, here in enumerate(rows_of):
+                dual[0, p, here] = all_steps[t][0]
+                if p == step:
+                    continue
                 if step < ITERS - 1:
-                    dual[1, p, here] = step_x
-                    dual[2, p, here] = step_y
-                return step_z, step_x, step_y, pltpu.roll(step_x, 1, 0)
-
-            def renew(t, steps, last_x):
-                here = tile_rows(t)
-                step_z, step_x, step_y, moved = steps
-                diverge = (
-                    (step_z - dual[0, jnp.maximum(p - 1, 0), here])
-                    + (step_x - jnp.where(first_row, last_x, moved))
-                    + (step_y - pltpu.roll(step_y, 1, 1))
-                )
-                before_it = old[p, here]
-                fresh = jnp.float32(keep_old) * before_it + jnp.float32(take_new) * (diverge + target[p, here])
-                if step < ITERS - 1:
-                    primal[p, here] = fresh
-                    ahead[p, here] = 2.0 * fresh - before_it
-                else:
-                    place_out = jnp.maximum(p - HALO, 0)
-                    out[0, place_out, here] = fresh[:, :half]
-                    out[1, place_out, here] = fresh[:, half:]
-
-            edge_steps = steps_of(tiles)
-            last_x = edge_steps[3]
-            for t in range(tiles):
-                steps = steps_of(t)
-                renew(t, steps, last_x)
-                last_x = steps[3]
-            if step < ITERS - 1:
-                renew(tiles, edge_steps, last_x)
+                    dual[1, p, here] = all_steps[t][1]
+                    dual[2, p, here] = all_steps[t][2]
+                    primal[p, here] = news[t]
+                    ahead[p, here] = 2.0 * news[t] - old_value[t]
+                elif t < tiles:
+                    place_out = max(p - HALO, 0)
+                    out[0, place_out, here] = news[t][:, :half]
+                    out[1, place_out, here] = news[t][:, half:]
             return carry
 
-        lax.fori_loop(step, planes - 1 - step, plane, 0)
+        for p in range(step, planes - 1 - step):
+            plane(p, 0)
 
 
 def vary(span, pieces, sizes, spot, fields, befores, afters, after=()):
@@ -472,7 +480,7 @@
         near = both(*sent)
         *fores, base = hold([c0], spot, signs, gradient, model, shares, sent)
         far = crossed(*relay(c0, fores, near)[0])
-        target = settle([c0], base, near, far)
+        (target,) = settle([c0], spot, base, near, far)
         low = lax.ppermute(target[planes - HALO :], "depth", ahead_z)
         high = lax.ppermute(target[:HALO], "depth", back_z)
         before, after = across(pack(spot, (low, target, high)))
@@ -497,7 +505,7 @@
     far_0 = crossed(*passed_0)
     passed_1, sent_2 = relay(c1, fores, near_1, sent_2, passed_0)
     near_2 = both(*sent_2)
-    mid_0 = settle([c0], base, near_0, far_0, passed_1)
+    (mid_0,) = settle([c0], spot, base, near_0, far_0, passed_1)
     edge = lax.dynamic_slice_in_dim(mid_0, turn(flip, 0, HALO, n0), HALO, 0)
     beside = lax.ppermute(edge, "depth", ahead_z + back_z)
     edges_0 = pack(spot, (mid_0, beside))
@@ -539,8 +547,7 @@
     m1 = (m0 + planes) // 2
     spans = ((0, m0), (m0, m1), (m1, planes))
     own_0 = update(spans[0], passed_2)
-    mid_1 = settle([c1, c2], base, near_1 + near_2, far_1, (own_0,))
-    edges_1 = pack(spot, (mid_1,))
+    mid_1, *edges_1 = settle([c1, c2], spot, base, near_1 + near_2, far_1, (own_0,), True)
     before_1, after_1 = across(edges_1)
     arrays["mid_1"] = mid_1
     sides.append((before_1, after_1))

time: 92.5 us -> 90.5 us (0.978)
  Pallas kernels: 35.8 us -> 29.1 us
  waiting for transfers between devices: 14.9 us -> 21.1 us
  starting transfers between devices: 39.4 us -> 37.7 us
    ppermute x12, waiting for transfers between devices: 6.2 us -> 13 us  [swap_y(): return lax.ppermute(array, 'shot', PAIRS_Y)]
    pallas_call x3, Pallas kernels: 15.9 us -> 9.72 us  [vary(): pl.pallas_call(functools.partial(vary_kernel, span, pieces, sizes, counts...]
    ppermute x4, waiting for transfers between devices: 1.31 us -> 0.01 us  [across(): lax.ppermute(edge, group, pairs)]
  transfers between devices with their start and end apart: 29 -> 29, of which waited for: 12 -> 13; matrix products, arithmetic and copies ran while one was open for 0% -> 0% of each run, Pallas kernels for 35% -> 28%
where the time goes in v4:
time: 90.5 us; the launch traced here: 90.1 us
  starting transfers between devices  37.7 us (42%)
  Pallas kernels  29.1 us (32%)
  waiting for transfers between devices  21.1 us (23%)
  local copies, waits for them, and re-layouts  1.88 us (2%)
    ppermute x12, starting transfers between devices, swap_y(): return lax.ppermute(array, 'shot', PAIRS_Y)  20.9 us
    ppermute x12, starting transfers between devices, swap_x(): return lax.ppermute(array, 'shot', PAIRS_X)  13.4 us
    ppermute x12, waiting for transfers between devices, swap_y(): return lax.ppermute(array, 'shot', PAIRS_Y)  13 us
    pallas_call x3, Pallas kernels, vary(): pl.pallas_call(functools.partial(vary_kernel, span, pieces, sizes, counts...  9.72 us
    ppermute x12, waiting for transfers between devices, swap_x(): return lax.ppermute(array, 'shot', PAIRS_X)  6.67 us
    pallas_call x3, Pallas kernels, prepare(): pl.pallas_call(functools.partial(prepare_kernel, chunk, len(after)), in_s...  6.19 us
    pallas_call x3, Pallas kernels, gather(): pl.pallas_call(functools.partial(gather_kernel, span, parts), in_specs=[S...  5.07 us
    ppermute x4, starting transfers between devices, across(): lax.ppermute(edge, group, pairs)  3.22 us
  transfers between devices with their start and end apart: 29, of which 13 were waited for; matrix products, arithmetic and copies ran while one was open for 0% of the time, Pallas kernels for 28%

profile of v4, /device:TPU:0, one launch (start us, length us, event | category | flops | bytes accessed | tf_op | source)
XLA Modules:
  0.0 90.1 jit_solution(9419766008670913267)
XLA Ops:
  0.1 1.9 %shard_map.37 = (f32[2,7,32,256]{3,2,1,0:T(8,128)S(1)}, f32[2,7,32,256]{3,2,1,0:T(8,128)S(1)}) custom-call(s32[7]{0:T(128)S(1)} %stack.31.spot, s32[1,512]{1,0:T(1,128)} %signs.7, f32[1,16,128,512]{3,2,1,0:T(8,128)} %gradient.7), custom_call_target="tpu_custom_call" | custom-call | flops 1 | bytes 1 | tf_op jit(solution)/shard_map/pallas_call | solution.py:108
  2.0 3.0 %collective-permute-start.2 = (f32[2,7,32,256]{3,2,1,0:T(8,128)S(1)}, f32[2,7,32,256]{3,2,1,0:T(8,128)S(1)}, u32[]{:S(2)}, u32[]{:S(2)}) collective-permute-start(f32[2,7,32,256]{3,2,1,0:T(8,128)S(1)} %get-tuple-element.27.rest_0_), channel_id=1, source_target_pairs={{0,8},{8,0},{16,24},{24,16},{1,9},{9,1},{17,25},{25,17},{2,10},{10... | collective-permute-start | bytes 1376264 | tf_op jit(solution)/shard_map/ppermute | solution.py:33
  5.0 1.5 %collective-permute-start.3 = (f32[2,7,32,256]{3,2,1,0:T(8,128)S(1)}, f32[2,7,32,256]{3,2,1,0:T(8,128)S(1)}, u32[]{:S(2)}, u32[]{:S(2)}) collective-permute-start(f32[2,7,32,256]{3,2,1,0:T(8,128)S(1)} %get-tuple-element.28.rest_1_), channel_id=1, source_target_pairs={{0,16},{16,0},{8,24},{24,8},{1,17},{17,1},{9,25},{25,9},{2,18},{18... | collective-permute-start | bytes 1376264 | tf_op jit(solution)/shard_map/ppermute | solution.py:37
  6.5 2.5 %shard_map.38 = (f32[2,4,32,256]{3,2,1,0:T(8,128)}, f32[2,4,32,256]{3,2,1,0:T(8,128)}) custom-call(s32[7]{0:T(128)S(1)} %stack.31.spot, s32[1,512]{1,0:T(1,128)} %signs.7, f32[1,16,128,512]{3,2,1,0:T(8,128)} %gradient.7, f32[2,7,32,256]{3,2,1,0:T(8,128)S(1)} %get-tuple-element.27.rest_0_, f32[2,7,32,256]{3,2,1,0:T(8,128)S(1)} %get-tuple-element.28.rest_1_), custom_call_target="tpu_custom_call" | custom-call | flops 1 | bytes 1 | tf_op jit(solution)/shard_map/pallas_call | solution.py:108
  9.7 3.2 %shard_map.39 = (f32[16,32,256]{2,1,0:T(8,128)S(1)}, f32[16,32,256]{2,1,0:T(8,128)S(1)}, f32[16,32,512]{2,1,0:T(8,128)S(1)}) custom-call(s32[7]{0:T(128)S(1)} %stack.31.spot, s32[1,512]{1,0:T(1,128)} %signs.7, f32[1,16,128,512]{3,2,1,0:T(8,128)} %gradient.7, f32[16,128,512]{2,1,0:T(8,128)} %model.1, f32[2,4,32,256]{3,2,1,0:T(8,128)} %get-tuple-element.29.rest_0_, ...), custom_call_target="tpu_custom_call" | custom-call | flops 1 | bytes 1 | tf_op jit(solution)/shard_map/pallas_call | solution.py:151
  12.9 1.8 %shard_map.40 = (f32[2,5,32,256]{3,2,1,0:T(8,128)S(1)}, f32[2,5,32,256]{3,2,1,0:T(8,128)S(1)}) custom-call(s32[7]{0:T(128)S(1)} %stack.31.spot, s32[1,512]{1,0:T(1,128)} %signs.7, f32[1,16,128,512]{3,2,1,0:T(8,128)} %gradient.7, f32[16,32,512]{2,1,0:T(8,128)S(1)} %get-tuple-element.31.rest_0_.base), custom_call_target="tpu_custom_call" | custom-call | flops 1 | bytes 1 | tf_op jit(solution)/shard_map/pallas_call | solution.py:108
  14.6 1.7 %collective-permute-done.2.near_a.refs_0_ = f32[2,7,32,256]{3,2,1,0:T(8,128)S(1)} collective-permute-done((f32[2,7,32,256]{3,2,1,0:T(8,128)S(1)}, f32[2,7,32,256]{3,2,1,0:T(8,128)S(1)}, u32[]{:S(2)}, u32[]{:S(2)}) %collective-permute-start.2) | collective-permute-done | bytes 458784 | tf_op jit(solution)/shard_map/ppermute | solution.py:33
  16.4 2.1 %collective-permute-done.3.near_b.refs_1_ = f32[2,7,32,256]{3,2,1,0:T(8,128)S(1)} collective-permute-done((f32[2,7,32,256]{3,2,1,0:T(8,128)S(1)}, f32[2,7,32,256]{3,2,1,0:T(8,128)S(1)}, u32[]{:S(2)}, u32[]{:S(2)}) %collective-permute-start.3) | collective-permute-done | bytes 458784 | tf_op jit(solution)/shard_map/ppermute | solution.py:37
  18.4 0.8 shard_map.41
  19.3 0.7 copy-done
  20.0 1.5 %collective-permute-start.6 = (f32[7,32,256]{2,1,0:T(8,128)}, f32[7,32,256]{2,1,0:T(8,128)}, u32[]{:S(2)}, u32[]{:S(2)}) collective-permute-start(f32[7,32,256]{2,1,0:T(8,128)} %get-tuple-element.36.rest_2_), channel_id=1, source_target_pairs={{0,16},{16,0},{8,24},{24,8},{1,17},{17,1},{9,25},{25,9},{2,18},{18... | collective-permute-start | bytes 688136 | tf_op jit(solution)/shard_map/ppermute | solution.py:37
  22.0 2.1 %collective-permute-done.1.near_b.refs_1_ = f32[2,4,32,256]{3,2,1,0:T(8,128)} collective-permute-done((f32[2,4,32,256]{3,2,1,0:T(8,128)}, f32[2,4,32,256]{3,2,1,0:T(8,128)}, u32[]{:S(2)}, u32[]{:S(2)}) %collective-permute-start.1) | collective-permute-done | bytes 262176 | tf_op jit(solution)/shard_map/ppermute | solution.py:37
  24.2 1.0 %copy-done.1 = f32[2,5,32,256]{3,2,1,0:T(8,128)S(1)} copy-done((f32[2,5,32,256]{3,2,1,0:T(8,128)S(1)}, f32[2,5,32,256]{3,2,1,0:T(8,128)}, u32[]{:S(2)}) %copy-start.1) | copy-done | bytes 327704
  25.1 1.2 %shard_map.42 = (f32[4,32,256]{2,1,0:T(8,128)S(1)}, f32[4,32,256]{2,1,0:T(8,128)S(1)}, f32[2,5,32,256]{3,2,1,0:T(8,128)S(1)}, f32[2,5,32,256]{3,2,1,0:T(8,128)S(1)}) custom-call(f32[16,32,256]{2,1,0:T(8,128)S(1)} %get-tuple-element.32.fore_a, f32[16,32,256]{2,1,0:T(8,128)S(1)} %get-tuple-element.33.fore_b, ...), custom_call_target="tpu_custom_call" | custom-call | flops 1 | bytes 1 | tf_op jit(solution)/shard_map/pallas_call | solution.py:185
  26.5 2.0 %collective-permute-start.5 = (f32[2,5,32,256]{3,2,1,0:T(8,128)S(1)}, f32[2,5,32,256]{3,2,1,0:T(8,128)S(1)}, u32[]{:S(2)}, u32[]{:S(2)}) collective-permute-start(f32[2,5,32,256]{3,2,1,0:T(8,128)S(1)} %get-tuple-element.39), channel_id=1, source_target_pairs={{0,16},{16,0},{8,24},{24,8},{1,17},{17,1},{9,25},{25,9},{2,18},{18... | collective-permute-start | bytes 983048 | tf_op jit(solution)/shard_map/ppermute | solution.py:37
  28.5 0.8 collective-permute-done.7.refs_3_
  29.4 1.1 %shard_map.43.refs_0_.refs_1_ = f32[7,32,512]{2,1,0:T(8,128)S(1)} custom-call(s32[7]{0:T(128)S(1)} %stack.31.spot, f32[16,32,512]{2,1,0:T(8,128)S(1)} %get-tuple-element.31.rest_0_.base, f32[2,7,32,256]{3,2,1,0:T(8,128)S(1)} %collective-permute-done.2.near_a.refs_0_, f32[2,7,32,256]{3,2,1,0:T(8,128)S(1)} %collective-permute-done.3.near_b.refs_1_, ...), custom_call_target="tpu_custom_call" | custom-call | flops 1 | bytes 1 | tf_op jit(solution)/shard_map/pallas_call | solution.py:218
  30.6 1.4 %collective-permute-done.8.refs_1_.refs_0_ = f32[3,32,512]{2,1,0:T(8,128)S(1)} collective-permute-done((f32[3,32,512]{2,1,0:T(8,128)S(1)}, f32[3,32,512]{2,1,0:T(8,128)S(1)}, u32[]{:S(2)}, u32[]{:S(2)}) %collective-permute-start.8) | collective-permute-done | bytes 196640 | tf_op jit(solution)/shard_map/ppermute | solution.py:510
  32.6 0.7 collective-permute-start.11
  33.3 0.7 collective-permute-start.12
  34.0 0.8 collective-permute-done.4.near_a.refs_2_
  34.8 2.6 %collective-permute-start.10 = (f32[9,32,256]{2,1,0:T(8,128)S(1)}, f32[9,32,256]{2,1,0:T(8,128)S(1)}, u32[]{:S(2)}, u32[]{:S(2)}) collective-permute-start(f32[9,32,256]{2,1,0:T(8,128)S(1)} %get-tuple-element.45.refs_5_), channel_id=1, source_target_pairs={{0,8},{8,0},{16,24},{24,16},{1,9},{9,1},{17,25},{25,17},{2,10},{10... | collective-permute-start | bytes 884744 | tf_op jit(solution)/shard_map/ppermute | solution.py:33
  37.5 1.3 %collective-permute-start.9 = (f32[9,32,256]{2,1,0:T(8,128)S(1)}, f32[9,32,256]{2,1,0:T(8,128)S(1)}, u32[]{:S(2)}, u32[]{:S(2)}) collective-permute-start(f32[9,32,256]{2,1,0:T(8,128)S(1)} %get-tuple-element.44.refs_4_), channel_id=1, source_target_pairs={{0,16},{16,0},{8,24},{24,8},{1,17},{17,1},{9,25},{25,9},{2,18},{18... | collective-permute-start | bytes 884744 | tf_op jit(solution)/shard_map/ppermute | solution.py:37
  38.8 2.8 %shard_map.46.refs_6_.refs_0_ = f32[2,4,32,256]{3,2,1,0:T(8,128)S(1)} custom-call(s32[7]{0:T(128)S(1)} %stack.31.spot, f32[3,32,512]{2,1,0:T(8,128)S(1)} %collective-permute-done.8.refs_1_.refs_0_, f32[7,32,512]{2,1,0:T(8,128)S(1)} %shard_map.43.refs_0_.refs_1_, f32[10,3,512]{2,1,0:T(4,128)S(1)} %collective-permute-done.11.refs_2_, ...), custom_call_target="tpu_custom_call" | custom-call | flops 1 | bytes 100000000 | tf_op jit(solution)/shard_map/pallas_call | solution.py:361
  41.6 2.4 %collective-permute-start.16 = (f32[2,4,32,256]{3,2,1,0:T(8,128)S(1)}, f32[2,4,32,256]{3,2,1,0:T(8,128)S(1)}, u32[]{:S(2)}, u32[]{:S(2)}) collective-permute-start(f32[2,4,32,256]{3,2,1,0:T(8,128)S(1)} %shard_map.46.refs_6_.refs_0_), channel_id=1, source_target_pairs={{0,16},{16,0},{8,24},{24,8},{1,17},{17,1},{9,25},{25,9},{2,18},{18... | collective-permute-start | bytes 786440 | tf_op jit(solution)/shard_map/ppermute | solution.py:37
  44.0 0.6 collective-permute-start.15
  44.6 2.8 %collective-permute-done.9.refs_4_ = f32[9,32,256]{2,1,0:T(8,128)S(1)} collective-permute-done((f32[9,32,256]{2,1,0:T(8,128)S(1)}, f32[9,32,256]{2,1,0:T(8,128)S(1)}, u32[]{:S(2)}, u32[]{:S(2)}) %collective-permute-start.9) | collective-permute-done | bytes 294944 | tf_op jit(solution)/shard_map/ppermute | solution.py:37
  47.4 1.2 %shard_map.47 = (f32[9,32,512]{2,1,0:T(8,128)S(1)}, f32[9,3,512]{2,1,0:T(4,128)S(1)}, f32[9,3,512]{2,1,0:T(4,128)S(1)}) custom-call(s32[7]{0:T(128)S(1)} %stack.31.spot, f32[16,32,512]{2,1,0:T(8,128)S(1)} %get-tuple-element.31.rest_0_.base, f32[2,4,32,256]{3,2,1,0:T(8,128)} %collective-permute-done.near_a.refs_0_, ...), custom_call_target="tpu_custom_call" | custom-call | flops 1 | bytes 1 | tf_op jit(solution)/shard_map/pallas_call | solution.py:218
  48.6 1.0 %collective-permute-start.13 = (f32[9,3,512]{2,1,0:T(4,128)S(1)}, f32[9,3,512]{2,1,0:T(4,128)S(1)}, u32[]{:S(2)}, u32[]{:S(2)}) collective-permute-start(f32[9,3,512]{2,1,0:T(4,128)S(1)} %get-tuple-element.47), channel_id=1, source_target_pairs={{0,8},{8,0},{24,16},{16,24},{1,9},{9,1},{25,17},{17,25},{2,10},{10... | collective-permute-start | bytes 165896 | tf_op jit(solution)/shard_map/ppermute | solution.py:462
  49.6 0.8 collective-permute-start.14
  50.5 0.8 collective-permute-done.16.refs_5_.refs_4_
  51.3 2.9 %collective-permute-start.27 = (f32[4,32,256]{2,1,0:T(8,128)S(1)}, f32[4,32,256]{2,1,0:T(8,128)S(1)}, u32[]{:S(2)}, u32[]{:S(2)}) collective-permute-start(f32[4,32,256]{2,1,0:T(8,128)S(1)} %slice_bitcast_fusion.5), channel_id=1, source_target_pairs={{0,8},{8,0},{16,24},{24,16},{1,9},{9,1},{17,25},{25,17},{2,10},{10... | collective-permute-start | bytes 393224 | tf_op jit(solution)/shard_map/ppermute | solution.py:33
  54.2 3.4 %shard_map.48.refs_3_.refs_0_ = f32[2,6,32,256]{3,2,1,0:T(8,128)S(1)} custom-call(s32[7]{0:T(128)S(1)} %stack.31.spot, f32[7,32,512]{2,1,0:T(8,128)S(1)} %shard_map.43.refs_0_.refs_1_, f32[9,32,512]{2,1,0:T(8,128)S(1)} %get-tuple-element.46.refs_1_.refs_0_, f32[10,3,512]{2,1,0:T(4,128)S(1)} %collective-permute-done.11.refs_2_, ...), custom_call_target="tpu_custom_call" | custom-call | flops 1 | bytes 100000000 | tf_op jit(solution)/shard_map/pallas_call | solution.py:361
  57.7 4.6 %collective-permute-start.24 = (f32[2,6,32,256]{3,2,1,0:T(8,128)S(1)}, f32[2,6,32,256]{3,2,1,0:T(8,128)S(1)}, u32[]{:S(2)}, u32[]{:S(2)}) collective-permute-start(f32[2,6,32,256]{3,2,1,0:T(8,128)S(1)} %shard_map.48.refs_3_.refs_0_), channel_id=1, source_target_pairs={{0,16},{16,0},{8,24},{24,8},{1,17},{17,1},{9,25},{25,9},{2,18},{18... | collective-permute-start | bytes 1179656 | tf_op jit(solution)/shard_map/ppermute | solution.py:37
  62.5 3.5 %shard_map.49.refs_0_ = f32[2,6,32,256]{3,2,1,0:T(8,128)S(1)} custom-call(s32[7]{0:T(128)S(1)} %stack.31.spot, f32[9,32,512]{2,1,0:T(8,128)S(1)} %get-tuple-element.46.refs_1_.refs_0_, f32[9,3,512]{2,1,0:T(4,128)S(1)} %collective-permute-done.13.refs_3_.refs_1_, f32[9,3,512]{2,1,0:T(4,128)S(1)} %collective-permute-done.14.refs_5_.refs_2_, ...), custom_call_target="tpu_custom_call" | custom-call | flops 1 | bytes 100000000 | tf_op jit(solution)/shard_map/pallas_call | solution.py:361
  66.1 1.9 %collective-permute-start.19 = (f32[6,32,256]{2,1,0:T(8,128)S(1)}, f32[6,32,256]{2,1,0:T(8,128)S(1)}, u32[]{:S(2)}, u32[]{:S(2)}) collective-permute-start(f32[6,32,256]{2,1,0:T(8,128)S(1)} %get-tuple-element.50), channel_id=1, source_target_pairs={{0,16},{16,0},{8,24},{24,8},{1,17},{17,1},{9,25},{25,9},{2,18},{18... | collective-permute-start | bytes 589832 | tf_op jit(solution)/shard_map/ppermute | solution.py:37
  68.0 3.7 %collective-permute-done.24.refs_4_ = f32[2,6,32,256]{3,2,1,0:T(8,128)S(1)} collective-permute-done((f32[2,6,32,256]{3,2,1,0:T(8,128)S(1)}, f32[2,6,32,256]{3,2,1,0:T(8,128)S(1)}, u32[]{:S(2)}, u32[]{:S(2)}) %collective-permute-start.24) | collective-permute-done | bytes 393248 | tf_op jit(solution)/shard_map/ppermute | solution.py:37
  71.7 0.8 collective-permute-start.18
  72.5 1.9 %collective-permute-done.23.refs_1_ = f32[2,6,32,256]{3,2,1,0:T(8,128)S(1)} collective-permute-done((f32[2,6,32,256]{3,2,1,0:T(8,128)S(1)}, f32[2,6,32,256]{3,2,1,0:T(8,128)S(1)}, u32[]{:S(2)}, u32[]{:S(2)}) %collective-permute-start.23) | collective-permute-done | bytes 393248 | tf_op jit(solution)/shard_map/ppermute | solution.py:33
  74.5 2.1 %collective-permute-start.17 = (f32[6,32,256]{2,1,0:T(8,128)S(1)}, f32[6,32,256]{2,1,0:T(8,128)S(1)}, u32[]{:S(2)}, u32[]{:S(2)}) collective-permute-start(f32[6,32,256]{2,1,0:T(8,128)S(1)} %get-tuple-element.50), channel_id=1, source_target_pairs={{0,8},{8,0},{16,24},{24,16},{1,9},{9,1},{17,25},{25,17},{2,10},{10... | collective-permute-start | bytes 589832 | tf_op jit(solution)/shard_map/ppermute | solution.py:33
  76.6 2.0 %collective-permute-start.26 = (f32[6,32,256]{2,1,0:T(8,128)S(1)}, f32[6,32,256]{2,1,0:T(8,128)S(1)}, u32[]{:S(2)}, u32[]{:S(2)}) collective-permute-start(f32[6,32,256]{2,1,0:T(8,128)S(1)} %slice_bitcast_fusion), channel_id=1, source_target_pairs={{0,16},{16,0},{8,24},{24,8},{1,17},{17,1},{9,25},{25,9},{2,18},{18... | collective-permute-start | bytes 589832 | tf_op jit(solution)/shard_map/ppermute | solution.py:37
  78.7 2.5 %collective-permute-start.22 = (f32[6,32,256]{2,1,0:T(8,128)S(1)}, f32[6,32,256]{2,1,0:T(8,128)S(1)}, u32[]{:S(2)}, u32[]{:S(2)}) collective-permute-start(f32[6,32,256]{2,1,0:T(8,128)S(1)} %get-tuple-element.49), channel_id=1, source_target_pairs={{0,16},{16,0},{8,24},{24,8},{1,17},{17,1},{9,25},{25,9},{2,18},{18... | collective-permute-start | bytes 589832 | tf_op jit(solution)/shard_map/ppermute | solution.py:37
  81.2 1.4 %collective-permute-done.25.refs_2_ = f32[6,32,256]{2,1,0:T(8,128)S(1)} collective-permute-done((f32[6,32,256]{2,1,0:T(8,128)S(1)}, f32[6,32,256]{2,1,0:T(8,128)S(1)}, u32[]{:S(2)}, u32[]{:S(2)}) %collective-permute-start.25) | collective-permute-done | bytes 196640 | tf_op jit(solution)/shard_map/ppermute | solution.py:33
  82.6 1.0 %collective-permute-start.21 = (f32[6,32,256]{2,1,0:T(8,128)S(1)}, f32[6,32,256]{2,1,0:T(8,128)S(1)}, u32[]{:S(2)}, u32[]{:S(2)}) collective-permute-start(f32[6,32,256]{2,1,0:T(8,128)S(1)} %collective-permute-done.18.refs_2_), channel_id=1, source_target_pairs={{0,16},{16,0},{8,24},{24,8},{1,17},{17,1},{9,25},{25,9},{2,18},{18... | collective-permute-start | bytes 589832 | tf_op jit(solution)/shard_map/ppermute | solution.py:37
  83.6 1.6 %shard_map.50.refs_5_ = f32[16,128,512]{2,1,0:T(8,128)} custom-call(s32[7]{0:T(128)S(1)} %stack.31.spot, f32[2,4,32,256]{3,2,1,0:T(8,128)S(1)} %shard_map.46.refs_6_.refs_0_, f32[2,4,32,256]{3,2,1,0:T(8,128)S(1)} %collective-permute-done.15.refs_4_.refs_1_, f32[4,32,256]{2,1,0:T(8,128)S(1)} %collective-permute-done.27.refs_2_, ...), custom_call_target="tpu_custom_call" | custom-call | flops 1 | bytes 1 | tf_op jit(solution)/shard_map/pallas_call | solution.py:391
  85.2 1.8 %shard_map.51.refs_7_ = f32[16,128,512]{2,1,0:T(8,128)} custom-call(s32[7]{0:T(128)S(1)} %stack.31.spot, f32[2,6,32,256]{3,2,1,0:T(8,128)S(1)} %shard_map.48.refs_3_.refs_0_, f32[2,6,32,256]{3,2,1,0:T(8,128)S(1)} %collective-permute-done.23.refs_1_, f32[6,32,256]{2,1,0:T(8,128)S(1)} %collective-permute-done.25.refs_2_, ...), custom_call_target="tpu_custom_call", output_to_operand_aliasing={{}: (6, {})} | custom-call | flops 1 | bytes 1 | tf_op jit(solution)/shard_map/pallas_call | solution.py:391
  87.0 1.3 %collective-permute-done.21.refs_4_ = f32[6,32,256]{2,1,0:T(8,128)S(1)} collective-permute-done((f32[6,32,256]{2,1,0:T(8,128)S(1)}, f32[6,32,256]{2,1,0:T(8,128)S(1)}, u32[]{:S(2)}, u32[]{:S(2)}) %collective-permute-start.21) | collective-permute-done | bytes 196640 | tf_op jit(solution)/shard_map/ppermute | solution.py:37
  88.2 1.7 %shard_map.52 = f32[16,128,512]{2,1,0:T(8,128)} custom-call(s32[7]{0:T(128)S(1)} %stack.31.spot, f32[2,6,32,256]{3,2,1,0:T(8,128)S(1)} %shard_map.49.refs_0_, f32[6,32,256]{2,1,0:T(8,128)S(1)} %collective-permute-done.17.refs_1_, f32[6,32,256]{2,1,0:T(8,128)S(1)} %collective-permute-done.18.refs_2_, ...), custom_call_target="tpu_custom_call", output_to_operand_aliasing={{}: (8, {})} | custom-call | flops 1 | bytes 1 | tf_op jit(solution)/shard_map/pallas_call | solution.py:391
  (37 shorter events, 2.6 us)
Async XLA Ops:
  2.0 14.4 %collective-permute-start.2 = (f32[2,7,32,256]{3,2,1,0:T(8,128)S(1)}, f32[2,7,32,256]{3,2,1,0:T(8,128)S(1)}, u32[]{:S(2)}, u32[]{:S(2)}) collective-permute-start(f32[2,7,32,256]{3,2,1,0:T(8,128)S(1)} %get-tuple-element.27.rest_0_), channel_id=1, source_target_pairs={{0,8},{8,0},{16,24},{24,16},{1,9},{9,1},{17,25},{25,17},{2,10},{10... | collective-permute-start | bytes 1376264 | tf_op jit(solution)/shard_map/ppermute | solution.py:33
  5.0 13.4 %collective-permute-start.3 = (f32[2,7,32,256]{3,2,1,0:T(8,128)S(1)}, f32[2,7,32,256]{3,2,1,0:T(8,128)S(1)}, u32[]{:S(2)}, u32[]{:S(2)}) collective-permute-start(f32[2,7,32,256]{3,2,1,0:T(8,128)S(1)} %get-tuple-element.28.rest_1_), channel_id=1, source_target_pairs={{0,16},{16,0},{8,24},{24,8},{1,17},{17,1},{9,25},{25,9},{2,18},{18... | collective-permute-start | bytes 1376264 | tf_op jit(solution)/shard_map/ppermute | solution.py:37
  9.0 13.0 %collective-permute-start = (f32[2,4,32,256]{3,2,1,0:T(8,128)}, f32[2,4,32,256]{3,2,1,0:T(8,128)}, u32[]{:S(2)}, u32[]{:S(2)}) collective-permute-start(f32[2,4,32,256]{3,2,1,0:T(8,128)} %get-tuple-element.29.rest_0_), channel_id=1, source_target_pairs={{0,8},{8,0},{16,24},{24,16},{1,9},{9,1},{17,25},{25,17},{2,10},{10... | collective-permute-start | bytes 786440 | tf_op jit(solution)/shard_map/ppermute | solution.py:33
  9.6 14.5 %collective-permute-start.1 = (f32[2,4,32,256]{3,2,1,0:T(8,128)}, f32[2,4,32,256]{3,2,1,0:T(8,128)}, u32[]{:S(2)}, u32[]{:S(2)}) collective-permute-start(f32[2,4,32,256]{3,2,1,0:T(8,128)} %get-tuple-element.30.rest_1_), channel_id=1, source_target_pairs={{0,16},{16,0},{8,24},{24,8},{1,17},{17,1},{9,25},{25,9},{2,18},{18... | collective-permute-start | bytes 786440 | tf_op jit(solution)/shard_map/ppermute | solution.py:37
  19.3 0.7 copy-start
  20.0 8.5 %collective-permute-start.6 = (f32[7,32,256]{2,1,0:T(8,128)}, f32[7,32,256]{2,1,0:T(8,128)}, u32[]{:S(2)}, u32[]{:S(2)}) collective-permute-start(f32[7,32,256]{2,1,0:T(8,128)} %get-tuple-element.36.rest_2_), channel_id=1, source_target_pairs={{0,16},{16,0},{8,24},{24,8},{1,17},{17,1},{9,25},{25,9},{2,18},{18... | collective-permute-start | bytes 688136 | tf_op jit(solution)/shard_map/ppermute | solution.py:37
  21.5 7.9 %collective-permute-start.7 = (f32[7,32,256]{2,1,0:T(8,128)}, f32[7,32,256]{2,1,0:T(8,128)}, u32[]{:S(2)}, u32[]{:S(2)}) collective-permute-start(f32[7,32,256]{2,1,0:T(8,128)} %get-tuple-element.37.rest_3_), channel_id=1, source_target_pairs={{0,8},{8,0},{16,24},{24,16},{1,9},{9,1},{17,25},{25,17},{2,10},{10... | collective-permute-start | bytes 688136 | tf_op jit(solution)/shard_map/ppermute | solution.py:33
  24.2 1.0 %copy-start.1 = (f32[2,5,32,256]{3,2,1,0:T(8,128)S(1)}, f32[2,5,32,256]{3,2,1,0:T(8,128)}, u32[]{:S(2)}) copy-start(f32[2,5,32,256]{3,2,1,0:T(8,128)} %copy-done) | copy-start | bytes 983044
  26.4 8.4 %collective-permute-start.4 = (f32[2,5,32,256]{3,2,1,0:T(8,128)S(1)}, f32[2,5,32,256]{3,2,1,0:T(8,128)S(1)}, u32[]{:S(2)}, u32[]{:S(2)}) collective-permute-start(f32[2,5,32,256]{3,2,1,0:T(8,128)S(1)} %get-tuple-element.38), channel_id=1, source_target_pairs={{0,8},{8,0},{16,24},{24,16},{1,9},{9,1},{17,25},{25,17},{2,10},{10... | collective-permute-start | bytes 983048 | tf_op jit(solution)/shard_map/ppermute | solution.py:33
  26.5 8.3 %collective-permute-start.5 = (f32[2,5,32,256]{3,2,1,0:T(8,128)S(1)}, f32[2,5,32,256]{3,2,1,0:T(8,128)S(1)}, u32[]{:S(2)}, u32[]{:S(2)}) collective-permute-start(f32[2,5,32,256]{3,2,1,0:T(8,128)S(1)} %get-tuple-element.39), channel_id=1, source_target_pairs={{0,16},{16,0},{8,24},{24,8},{1,17},{17,1},{9,25},{25,9},{2,18},{18... | collective-permute-start | bytes 983048 | tf_op jit(solution)/shard_map/ppermute | solution.py:37
  30.5 1.5 %collective-permute-start.8 = (f32[3,32,512]{2,1,0:T(8,128)S(1)}, f32[3,32,512]{2,1,0:T(8,128)S(1)}, u32[]{:S(2)}, u32[]{:S(2)}) collective-permute-start(f32[3,32,512]{2,1,0:T(8,128)S(1)} %constant_dynamic-slice_fusion), channel_id=1, source_target_pairs={{0,4},{4,0},{1,5},{5,1},{2,6},{6,2},{3,7},{7,3},{8,12},{12,8},{9,1... | collective-permute-start | bytes 589832 | tf_op jit(solution)/shard_map/ppermute | solution.py:510
  32.6 6.2 %collective-permute-start.11 = (f32[10,3,512]{2,1,0:T(4,128)S(1)}, f32[10,3,512]{2,1,0:T(4,128)S(1)}, u32[]{:S(2)}, u32[]{:S(2)}) collective-permute-start(f32[10,3,512]{2,1,0:T(4,128)S(1)} %get-tuple-element.42.rest_2_), channel_id=1, source_target_pairs={{0,8},{8,0},{24,16},{16,24},{1,9},{9,1},{25,17},{17,25},{2,10},{10... | collective-permute-start | bytes 184328 | tf_op jit(solution)/shard_map/ppermute | solution.py:462
  33.3 5.5 %collective-permute-start.12 = (f32[10,3,512]{2,1,0:T(4,128)S(1)}, f32[10,3,512]{2,1,0:T(4,128)S(1)}, u32[]{:S(2)}, u32[]{:S(2)}) collective-permute-start(f32[10,3,512]{2,1,0:T(4,128)S(1)} %get-tuple-element.43.rest_3_), channel_id=1, source_target_pairs={{8,24},{24,8},{16,1},{1,16},{9,25},{25,9},{17,2},{2,17},{10,26},{2... | collective-permute-start | bytes 184328 | tf_op jit(solution)/shard_map/ppermute | solution.py:462
  34.8 9.8 %collective-permute-start.10 = (f32[9,32,256]{2,1,0:T(8,128)S(1)}, f32[9,32,256]{2,1,0:T(8,128)S(1)}, u32[]{:S(2)}, u32[]{:S(2)}) collective-permute-start(f32[9,32,256]{2,1,0:T(8,128)S(1)} %get-tuple-element.45.refs_5_), channel_id=1, source_target_pairs={{0,8},{8,0},{16,24},{24,16},{1,9},{9,1},{17,25},{25,17},{2,10},{10... | collective-permute-start | bytes 884744 | tf_op jit(solution)/shard_map/ppermute | solution.py:33
  37.5 9.9 %collective-permute-start.9 = (f32[9,32,256]{2,1,0:T(8,128)S(1)}, f32[9,32,256]{2,1,0:T(8,128)S(1)}, u32[]{:S(2)}, u32[]{:S(2)}) collective-permute-start(f32[9,32,256]{2,1,0:T(8,128)S(1)} %get-tuple-element.44.refs_4_), channel_id=1, source_target_pairs={{0,16},{16,0},{8,24},{24,8},{1,17},{17,1},{9,25},{25,9},{2,18},{18... | collective-permute-start | bytes 884744 | tf_op jit(solution)/shard_map/ppermute | solution.py:37
  41.6 9.7 %collective-permute-start.16 = (f32[2,4,32,256]{3,2,1,0:T(8,128)S(1)}, f32[2,4,32,256]{3,2,1,0:T(8,128)S(1)}, u32[]{:S(2)}, u32[]{:S(2)}) collective-permute-start(f32[2,4,32,256]{3,2,1,0:T(8,128)S(1)} %shard_map.46.refs_6_.refs_0_), channel_id=1, source_target_pairs={{0,16},{16,0},{8,24},{24,8},{1,17},{17,1},{9,25},{25,9},{2,18},{18... | collective-permute-start | bytes 786440 | tf_op jit(solution)/shard_map/ppermute | solution.py:37
  44.0 18.3 %collective-permute-start.15 = (f32[2,4,32,256]{3,2,1,0:T(8,128)S(1)}, f32[2,4,32,256]{3,2,1,0:T(8,128)S(1)}, u32[]{:S(2)}, u32[]{:S(2)}) collective-permute-start(f32[2,4,32,256]{3,2,1,0:T(8,128)S(1)} %shard_map.46.refs_6_.refs_0_), channel_id=1, source_target_pairs={{0,8},{8,0},{16,24},{24,16},{1,9},{9,1},{17,25},{25,17},{2,10},{10... | collective-permute-start | bytes 786440 | tf_op jit(solution)/shard_map/ppermute | solution.py:33
  48.6 5.6 %collective-permute-start.13 = (f32[9,3,512]{2,1,0:T(4,128)S(1)}, f32[9,3,512]{2,1,0:T(4,128)S(1)}, u32[]{:S(2)}, u32[]{:S(2)}) collective-permute-start(f32[9,3,512]{2,1,0:T(4,128)S(1)} %get-tuple-element.47), channel_id=1, source_target_pairs={{0,8},{8,0},{24,16},{16,24},{1,9},{9,1},{25,17},{17,25},{2,10},{10... | collective-permute-start | bytes 165896 | tf_op jit(solution)/shard_map/ppermute | solution.py:462
  49.6 4.6 %collective-permute-start.14 = (f32[9,3,512]{2,1,0:T(4,128)S(1)}, f32[9,3,512]{2,1,0:T(4,128)S(1)}, u32[]{:S(2)}, u32[]{:S(2)}) collective-permute-start(f32[9,3,512]{2,1,0:T(4,128)S(1)} %get-tuple-element.48), channel_id=1, source_target_pairs={{8,24},{24,8},{16,1},{1,16},{9,25},{25,9},{17,2},{2,17},{10,26},{2... | collective-permute-start | bytes 165896 | tf_op jit(solution)/shard_map/ppermute | solution.py:462
  51.3 23.2 %collective-permute-start.27 = (f32[4,32,256]{2,1,0:T(8,128)S(1)}, f32[4,32,256]{2,1,0:T(8,128)S(1)}, u32[]{:S(2)}, u32[]{:S(2)}) collective-permute-start(f32[4,32,256]{2,1,0:T(8,128)S(1)} %slice_bitcast_fusion.5), channel_id=1, source_target_pairs={{0,8},{8,0},{16,24},{24,16},{1,9},{9,1},{17,25},{25,17},{2,10},{10... | collective-permute-start | bytes 393224 | tf_op jit(solution)/shard_map/ppermute | solution.py:33
  57.7 14.0 %collective-permute-start.24 = (f32[2,6,32,256]{3,2,1,0:T(8,128)S(1)}, f32[2,6,32,256]{3,2,1,0:T(8,128)S(1)}, u32[]{:S(2)}, u32[]{:S(2)}) collective-permute-start(f32[2,6,32,256]{3,2,1,0:T(8,128)S(1)} %shard_map.48.refs_3_.refs_0_), channel_id=1, source_target_pairs={{0,16},{16,0},{8,24},{24,8},{1,17},{17,1},{9,25},{25,9},{2,18},{18... | collective-permute-start | bytes 1179656 | tf_op jit(solution)/shard_map/ppermute | solution.py:37
  62.3 14.3 %collective-permute-start.28 = (f32[4,32,256]{2,1,0:T(8,128)S(1)}, f32[4,32,256]{2,1,0:T(8,128)S(1)}, u32[]{:S(2)}, u32[]{:S(2)}) collective-permute-start(f32[4,32,256]{2,1,0:T(8,128)S(1)} %slice_bitcast_fusion.4), channel_id=1, source_target_pairs={{0,16},{16,0},{8,24},{24,8},{1,17},{17,1},{9,25},{25,9},{2,18},{18... | collective-permute-start | bytes 393224 | tf_op jit(solution)/shard_map/ppermute | solution.py:37
  62.4 12.0 %collective-permute-start.23 = (f32[2,6,32,256]{3,2,1,0:T(8,128)S(1)}, f32[2,6,32,256]{3,2,1,0:T(8,128)S(1)}, u32[]{:S(2)}, u32[]{:S(2)}) collective-permute-start(f32[2,6,32,256]{3,2,1,0:T(8,128)S(1)} %shard_map.48.refs_3_.refs_0_), channel_id=1, source_target_pairs={{0,8},{8,0},{16,24},{24,16},{1,9},{9,1},{17,25},{25,17},{2,10},{10... | collective-permute-start | bytes 1179656 | tf_op jit(solution)/shard_map/ppermute | solution.py:33
  66.1 12.6 %collective-permute-start.19 = (f32[6,32,256]{2,1,0:T(8,128)S(1)}, f32[6,32,256]{2,1,0:T(8,128)S(1)}, u32[]{:S(2)}, u32[]{:S(2)}) collective-permute-start(f32[6,32,256]{2,1,0:T(8,128)S(1)} %get-tuple-element.50), channel_id=1, source_target_pairs={{0,16},{16,0},{8,24},{24,8},{1,17},{17,1},{9,25},{25,9},{2,18},{18... | collective-permute-start | bytes 589832 | tf_op jit(solution)/shard_map/ppermute | solution.py:37
  71.7 9.5 %collective-permute-start.18 = (f32[6,32,256]{2,1,0:T(8,128)S(1)}, f32[6,32,256]{2,1,0:T(8,128)S(1)}, u32[]{:S(2)}, u32[]{:S(2)}) collective-permute-start(f32[6,32,256]{2,1,0:T(8,128)S(1)} %get-tuple-element.49), channel_id=1, source_target_pairs={{0,8},{8,0},{16,24},{24,16},{1,9},{9,1},{17,25},{25,17},{2,10},{10... | collective-permute-start | bytes 589832 | tf_op jit(solution)/shard_map/ppermute | solution.py:33
  74.4 8.1 %collective-permute-start.25 = (f32[6,32,256]{2,1,0:T(8,128)S(1)}, f32[6,32,256]{2,1,0:T(8,128)S(1)}, u32[]{:S(2)}, u32[]{:S(2)}) collective-permute-start(f32[6,32,256]{2,1,0:T(8,128)S(1)} %slice_bitcast_fusion.1), channel_id=1, source_target_pairs={{0,8},{8,0},{16,24},{24,16},{1,9},{9,1},{17,25},{25,17},{2,10},{10... | collective-permute-start | bytes 589832 | tf_op jit(solution)/shard_map/ppermute | solution.py:33
  74.5 12.5 %collective-permute-start.17 = (f32[6,32,256]{2,1,0:T(8,128)S(1)}, f32[6,32,256]{2,1,0:T(8,128)S(1)}, u32[]{:S(2)}, u32[]{:S(2)}) collective-permute-start(f32[6,32,256]{2,1,0:T(8,128)S(1)} %get-tuple-element.50), channel_id=1, source_target_pairs={{0,8},{8,0},{16,24},{24,16},{1,9},{9,1},{17,25},{25,17},{2,10},{10... | collective-permute-start | bytes 589832 | tf_op jit(solution)/shard_map/ppermute | solution.py:33
  76.6 8.6 %collective-permute-start.26 = (f32[6,32,256]{2,1,0:T(8,128)S(1)}, f32[6,32,256]{2,1,0:T(8,128)S(1)}, u32[]{:S(2)}, u32[]{:S(2)}) collective-permute-start(f32[6,32,256]{2,1,0:T(8,128)S(1)} %slice_bitcast_fusion), channel_id=1, source_target_pairs={{0,16},{16,0},{8,24},{24,8},{1,17},{17,1},{9,25},{25,9},{2,18},{18... | collective-permute-start | bytes 589832 | tf_op jit(solution)/shard_map/ppermute | solution.py:37
  78.7 8.3 %collective-permute-start.22 = (f32[6,32,256]{2,1,0:T(8,128)S(1)}, f32[6,32,256]{2,1,0:T(8,128)S(1)}, u32[]{:S(2)}, u32[]{:S(2)}) collective-permute-start(f32[6,32,256]{2,1,0:T(8,128)S(1)} %get-tuple-element.49), channel_id=1, source_target_pairs={{0,16},{16,0},{8,24},{24,8},{1,17},{17,1},{9,25},{25,9},{2,18},{18... | collective-permute-start | bytes 589832 | tf_op jit(solution)/shard_map/ppermute | solution.py:37
  81.2 5.8 %collective-permute-start.20 = (f32[6,32,256]{2,1,0:T(8,128)S(1)}, f32[6,32,256]{2,1,0:T(8,128)S(1)}, u32[]{:S(2)}, u32[]{:S(2)}) collective-permute-start(f32[6,32,256]{2,1,0:T(8,128)S(1)} %collective-permute-done.19.refs_5_), channel_id=1, source_target_pairs={{0,8},{8,0},{16,24},{24,16},{1,9},{9,1},{17,25},{25,17},{2,10},{10... | collective-permute-start | bytes 589832 | tf_op jit(solution)/shard_map/ppermute | solution.py:33
  82.6 5.7 %collective-permute-start.21 = (f32[6,32,256]{2,1,0:T(8,128)S(1)}, f32[6,32,256]{2,1,0:T(8,128)S(1)}, u32[]{:S(2)}, u32[]{:S(2)}) collective-permute-start(f32[6,32,256]{2,1,0:T(8,128)S(1)} %collective-permute-done.18.refs_2_), channel_id=1, source_target_pairs={{0,16},{16,0},{8,24},{24,8},{1,17},{17,1},{9,25},{25,9},{2,18},{18... | collective-permute-start | bytes 589832 | tf_op jit(solution)/shard_map/ppermute | solution.py:37

commit v5 on v4

--- a/solution.py
+++ b/solution.py
@@ -11,6 +11,7 @@
 HALO = 3
 SIDE = 8
 VMEM_LIMIT = 16 * 1024 * 1024
+TOKEN = (8, 128)
 
 step_tau = 0.28
 step_sigma = 0.28
@@ -52,6 +53,18 @@
 
 def tile_rows(rows):
     return slice(rows * SIDE, rows * SIDE + SIDE)
+
+
+def gray(place):
+    return place ^ (place >> 1)
+
+
+def whereabouts(planes, rows, shares, paired):
+    at = gray(lax.axis_index("shot"))
+    layer = lax.axis_index("depth")
+    flip = (1 - layer) if paired else 0 * layer
+    start_x = lax.axis_index("inline") * rows + at * (rows // shares)
+    return (at, at ^ 1, at ^ 2, at ^ 3, flip, layer * planes, start_x)
 
 
 WHOLE = pl.BlockSpec(memory_space=pltpu.VMEM)
@@ -88,7 +101,9 @@
 
 
 def prepare_kernel(chunk, after, spot, signs, gradient, *rest):
-    out_a, out_b, held, held_signs, sems = rest[after:]
+    spot = whereabouts(*spot)
+    out_a, out_b, token, held, held_signs, sems = rest[after:]
+    token[...] = jnp.zeros(token.shape, jnp.float32)
     half = out_a.shape[3]
     copy_signs = pltpu.make_async_copy(signs, held_signs, sems.at[4])
     copy_signs.start()
@@ -106,10 +121,11 @@
     rows, cols = gradient.shape[2:]
     shape = (2, chunk[1], rows // shares, cols // 2)
     return pl.pallas_call(
-        functools.partial(prepare_kernel, chunk, len(after)),
-        in_specs=[SCALARS] + [ANYWHERE] * 2 + [WHOLE] * len(after),
-        out_specs=[WHOLE] * 2,
-        out_shape=[pltpu.VMEM(shape, jnp.float32) if keep else jax.ShapeDtypeStruct(shape, jnp.float32)] * 2,
+        functools.partial(prepare_kernel, chunk, len(after), spot),
+        in_specs=[ANYWHERE] * 2 + [WHOLE] * len(after),
+        out_specs=[WHOLE] * 3,
+        out_shape=[pltpu.VMEM(shape, jnp.float32) if keep else jax.ShapeDtypeStruct(shape, jnp.float32)] * 2
+        + [jax.ShapeDtypeStruct(TOKEN, jnp.float32)],
         scratch_shapes=[
             pltpu.VMEM((4,) + shape[1:], jnp.float32),
             pltpu.VMEM(signs.shape, jnp.int32),
@@ -117,10 +133,11 @@
         ],
         compiler_params=params(),
         cost_estimate=COST,
-    )(spot, signs, gradient, *near_core(after))
+    )(signs, gradient, *near_core(after))
 
 
 def hold_kernel(chunks, after, spot, signs, gradient, model, *rest):
+    spot = whereabouts(*spot)
     fore_a, fore_b, base, held_a, held_b, held, held_signs, sems = rest[after:]
     half = fore_a.shape[2]
     copy_signs = pltpu.make_async_copy(signs, held_signs, sems.at[4 * len(chunks)])
@@ -149,8 +166,8 @@
     whole = (planes, rows // shares, cols)
     part = (planes, rows // shares, cols // 2)
     return pl.pallas_call(
-        functools.partial(hold_kernel, chunks, len(after)),
-        in_specs=[SCALARS] + [ANYWHERE] * 3 + [WHOLE] * len(after),
+        functools.partial(hold_kernel, chunks, len(after), spot),
+        in_specs=[ANYWHERE] * 3 + [WHOLE] * len(after),
         out_specs=[WHOLE] * 3,
         out_shape=[pltpu.VMEM(shape, jnp.float32) for shape in (part, part, whole)],
         scratch_shapes=[
@@ -162,7 +179,7 @@
         ],
         compiler_params=params(),
         cost_estimate=COST,
-    )(spot, signs, gradient, model, *near_core(after))
+    )(signs, gradient, model, *near_core(after))
 
 
 def relay_kernel(chunk, carried, ready, after, fore_a, fore_b, near_a, near_b, *rest):
@@ -177,11 +194,12 @@
     outs[1][at:] = fore_b[here] + near_b[1]
     for source, out in zip(rest[:carried], outs[2:]):
         out[...] = source[...]
+    outs[-1][...] = jnp.zeros(outs[-1].shape, jnp.float32)
 
 
 def relay(chunk, fores, near, carried=(), after=(), ready=()):
     count = chunk[1] + sum(array.shape[0] for array in ready[:1])
-    shapes = [(count,) + near[0].shape[2:]] * 2 + [array.shape for array in carried]
+    shapes = [(count,) + near[0].shape[2:]] * 2 + [array.shape for array in carried] + [TOKEN]
     outs = pl.pallas_call(
         functools.partial(relay_kernel, chunk, len(carried), len(ready), len(after)),
         in_specs=[WHOLE] * (4 + len(carried) + len(ready) + len(after)),
@@ -190,10 +208,11 @@
         compiler_params=params(),
         cost_estimate=COST,
     )(*fores, *near_core((*near, *carried, *ready, *after)))
-    return outs[:2], outs[2:]
+    return outs[:2], outs[2:-1], outs[-1]
 
 
 def settle_kernel(chunks, edges, after, spot, base, *refs):
+    spot = whereabouts(*spot)
     nears, (far_a, far_b) = (refs[: 2 * len(chunks)], refs[2 * len(chunks) : 2 * len(chunks) + 2])
     out, *sides = refs[2 * len(chunks) + 2 + after :]
     half = far_a.shape[2]
@@ -216,16 +235,17 @@
     count, share, half = fars[0].shape
     shapes = [(count, share, 2 * half)] + ([(count, HALO, 2 * half)] * 2 if edges else [])
     return pl.pallas_call(
-        functools.partial(settle_kernel, chunks, edges, len(after)),
-        in_specs=[SCALARS] + [WHOLE] * (3 + len(nears) + len(after)),
+        functools.partial(settle_kernel, chunks, edges, len(after), spot),
+        in_specs=[WHOLE] * (3 + len(nears) + len(after)),
         out_specs=[WHOLE] * len(shapes),
         out_shape=[jax.ShapeDtypeStruct(shape, jnp.float32) for shape in shapes],
         compiler_params=params(),
         cost_estimate=COST,
-    )(spot, base, *near_core((*nears, *fars, *after)))
+    )(base, *near_core((*nears, *fars, *after)))
 
 
 def pack_kernel(count, spot, *refs):
+    spot = whereabouts(*spot)
     parts, (one, two) = (refs[:count], refs[count:])
     odd = spot[0] % 2 == 1
     at = 0
@@ -241,16 +261,17 @@
 def pack(spot, parts):
     shape = (sum(part.shape[0] for part in parts), HALO, parts[0].shape[2])
     return pl.pallas_call(
-        functools.partial(pack_kernel, len(parts)),
-        in_specs=[SCALARS] + [WHOLE] * len(parts),
+        functools.partial(pack_kernel, len(parts), spot),
+        in_specs=[WHOLE] * len(parts),
         out_specs=[WHOLE] * 2,
         out_shape=[jax.ShapeDtypeStruct(shape, jnp.float32)] * 2,
         compiler_params=params(),
         cost_estimate=COST,
-    )(spot, *near_core(parts))
+    )(*near_core(parts))
 
 
 def vary_kernel(span, pieces, sizes, counts, after, spot, *refs):
+    spot = whereabouts(*spot)
     fields, befores, afters = (refs[: counts[0]], refs[counts[0] : counts[0] + counts[1]], refs[counts[0] + counts[1] : counts[0] + 2 * counts[1]])
     out, target, primal, ahead, dual = refs[counts[0] + 2 * counts[1] + after :]
     planes, rows, cols = target.shape
@@ -359,17 +380,18 @@
     field = pltpu.VMEM((planes, rows, cols), jnp.float32)
     counts = (len(fields), len(befores))
     return pl.pallas_call(
-        functools.partial(vary_kernel, span, pieces, sizes, counts, len(after)),
-        in_specs=[SCALARS] + [WHOLE] * (counts[0] + 2 * counts[1]) + [WHOLE] * len(after),
+        functools.partial(vary_kernel, span, pieces, sizes, counts, len(after), spot),
+        in_specs=[WHOLE] * (counts[0] + 2 * counts[1]) + [WHOLE] * len(after),
         out_specs=WHOLE,
         out_shape=jax.ShapeDtypeStruct((2, span[1] - span[0], share, cols // 2), jnp.float32),
         scratch_shapes=[field, field, field, pltpu.VMEM((3, planes, rows, cols), jnp.float32)],
         compiler_params=params(),
         cost_estimate=LONG,
-    )(spot, *near_core((*fields, *befores, *afters, *after)))
+    )(*near_core((*fields, *befores, *afters, *after)))
 
 
 def gather_kernel(span, parts, spot, *refs):
+    spot = whereabouts(*spot)
     out, sems = refs[-2:]
     layers = chunk_planes(spot, (span[0], span[1] - span[0]), out.shape[0])
     copies = []
@@ -389,15 +411,15 @@
     before = [] if so_far is None else [so_far]
     arrays, parts = zip(*((array, (which, sides)) for array, which, sides in pieces))
     return pl.pallas_call(
-        functools.partial(gather_kernel, span, parts),
-        in_specs=[SCALARS] + [ANYWHERE] * (len(arrays) + len(before)),
+        functools.partial(gather_kernel, span, parts, spot),
+        in_specs=[ANYWHERE] * (len(arrays) + len(before)),
         out_specs=pl.BlockSpec(memory_space=pltpu.HBM),
         out_shape=jax.ShapeDtypeStruct(out_shape, jnp.float32),
-        input_output_aliases={1 + len(arrays): 0} if before else {},
+        input_output_aliases={len(arrays): 0} if before else {},
         scratch_shapes=[pltpu.SemaphoreType.DMA((8,))],
         compiler_params=params(),
         cost_estimate=cost,
-    )(spot, *arrays, *before)
+    )(*arrays, *before)
 
 
 def carry_kernel(count, after, *refs):
@@ -414,10 +436,6 @@
         compiler_params=params(),
         cost_estimate=COST,
     )(*near_core((*arrays, *after)))
-
-
-def gray(place):
-    return place ^ (place >> 1)
 
 
 def spread(own):
@@ -445,11 +463,8 @@
     share = rows // shares
     sizes = (planes, planes * layers, rows * lines)
     paired = layers == 2
-    at = gray(lax.axis_index("shot"))
-    layer = lax.axis_index("depth")
-    flip = (1 - layer) if paired else 0 * layer
-    start_x = lax.axis_index("inline") * rows + at * share
-    spot = jnp.stack([at, at ^ 1, at ^ 2, at ^ 3, flip, layer * planes, start_x]).astype(jnp.int32)
+    spot = (planes, rows, shares, paired)
+    flip = whereabouts(*spot)[FLIP]
 
     order = [gray(place) * lines + line for line in range(lines) for place in range(shares)]
     pairs_one = [pair for i, j in zip(order[::2], order[1::2]) for pair in ((i, j), (j, i))]
@@ -476,9 +491,9 @@
 
     if not paired:
         c0 = (0, planes)
-        sent = prep(c0)
+        *sent, token = prep(c0)
         near = both(*sent)
-        *fores, base = hold([c0], spot, signs, gradient, model, shares, sent)
+        *fores, base = hold([c0], spot, signs, gradient, model, shares, (token,))
         far = crossed(*relay(c0, fores, near)[0])
         (target,) = settle([c0], spot, base, near, far)
         low = lax.ppermute(target[planes - HALO :], "depth", ahead_z)
@@ -495,22 +510,22 @@
     n0, n1 = ((7 * planes) // 16, planes // 4)
     n2 = planes - n0 - n1
     c0, c1, c2 = ((0, n0), (n0, n1), (n0 + n1, n2))
-    sent_0 = prep(c0)
+    *sent_0, token_0 = prep(c0)
     near_0 = both(*sent_0)
-    sent_1 = prep(c1, sent_0)
+    *sent_1, token_1 = prep(c1, (token_0,))
     near_1 = both(*sent_1)
-    *fores, base = hold([c0, c1, c2], spot, signs, gradient, model, shares, sent_1)
-    sent_2 = prepare(c2, spot, signs, gradient, shares, (base,), True)
-    passed_0, _ = relay(c0, fores, near_0, after=sent_2)
+    *fores, base = hold([c0, c1, c2], spot, signs, gradient, model, shares, (token_1,))
+    *sent_2, token_2 = prepare(c2, spot, signs, gradient, shares, (base,), True)
+    passed_0, _, token_3 = relay(c0, fores, near_0, after=(token_2,))
     far_0 = crossed(*passed_0)
-    passed_1, sent_2 = relay(c1, fores, near_1, sent_2, passed_0)
+    passed_1, sent_2, token_4 = relay(c1, fores, near_1, sent_2, (token_3,))
     near_2 = both(*sent_2)
-    (mid_0,) = settle([c0], spot, base, near_0, far_0, passed_1)
+    (mid_0,) = settle([c0], spot, base, near_0, far_0, (token_4,))
     edge = lax.dynamic_slice_in_dim(mid_0, turn(flip, 0, HALO, n0), HALO, 0)
     beside = lax.ppermute(edge, "depth", ahead_z + back_z)
     edges_0 = pack(spot, (mid_0, beside))
     before_0, after_0 = across(edges_0)
-    passed_2, _ = relay(c2, fores, near_2, after=edges_0, ready=passed_1)
+    passed_2, _, token_5 = relay(c2, fores, near_2, after=edges_0, ready=passed_1)
     far_1 = crossed(*passed_2)
     arrays = {"beside": beside, "mid_0": mid_0, }
     sides = [(before_0, after_0)]
@@ -546,7 +561,7 @@
     m0 = n0 - HALO
     m1 = (m0 + planes) // 2
     spans = ((0, m0), (m0, m1), (m1, planes))
-    own_0 = update(spans[0], passed_2)
+    own_0 = update(spans[0], (token_5,))
     mid_1, *edges_1 = settle([c1, c2], spot, base, near_1 + near_2, far_1, (own_0,), True)
     before_1, after_1 = across(edges_1)
     arrays["mid_1"] = mid_1

time: 90.5 us -> 87.1 us (0.962)
  Pallas kernels: 29.1 us -> 20.4 us
  waiting for transfers between devices: 21.1 us -> 25.6 us
  local copies, waits for them, and re-layouts: 1.88 us -> 3.5 us
    pallas_call x8, Pallas kernels: 15 us -> 10.1 us  [the longest x3 4.56 us: prepare(): pl.pallas_call(functools.partial(prepare_kernel, chunk, len(after), spot)...]
    ppermute x12, waiting for transfers between devices: 13 us -> 17.2 us  [swap_y(): return lax.ppermute(array, 'shot', PAIRS_Y)]
    unnamed x4 -> x8, local copies, waits for them, and re-layouts: 1.7 us -> 3.41 us
    pallas_call x3, Pallas kernels: 9.72 us -> 8.08 us  [vary(): pl.pallas_call(functools.partial(vary_kernel, span, pieces, sizes, counts...]
    ppermute x12, starting transfers between devices: 20.9 us -> 19.4 us  [swap_y(): return lax.ppermute(array, 'shot', PAIRS_Y)]
    pallas_call x3, Pallas kernels: 2.11 us -> 0.95 us  [relay(): pl.pallas_call(functools.partial(relay_kernel, chunk, len(carried), len(r...]
    pallas_call x2, Pallas kernels: 2.3 us -> 1.24 us  [settle(): pl.pallas_call(functools.partial(settle_kernel, chunks, edges, len(after)...]
    ppermute x12, starting transfers between devices: 13.4 us -> 14.5 us  [swap_x(): return lax.ppermute(array, 'shot', PAIRS_X)]
  transfers between devices with their start and end apart: 29 -> 29, of which waited for: 13 -> 16; matrix products, arithmetic and copies ran while one was open for 0% -> 0% of each run, Pallas kernels for 28% -> 21%
where the time goes in v5:
time: 87.1 us; the launch traced here: 86.8 us
  starting transfers between devices  36.9 us (42%)
  waiting for transfers between devices  25.6 us (29%)
  Pallas kernels  20.4 us (23%)
  local copies, waits for them, and re-layouts  3.5 us (4%)
    ppermute x12, starting transfers between devices, swap_y(): return lax.ppermute(array, 'shot', PAIRS_Y)  19.4 us
    ppermute x12, waiting for transfers between devices, swap_y(): return lax.ppermute(array, 'shot', PAIRS_Y)  17.2 us
    ppermute x12, starting transfers between devices, swap_x(): return lax.ppermute(array, 'shot', PAIRS_X)  14.5 us
    pallas_call x3, Pallas kernels, vary(): pl.pallas_call(functools.partial(vary_kernel, span, pieces, sizes, counts...  8.08 us
    ppermute x12, waiting for transfers between devices, swap_x(): return lax.ppermute(array, 'shot', PAIRS_X)  6.97 us
    pallas_call x3, Pallas kernels, prepare(): pl.pallas_call(functools.partial(prepare_kernel, chunk, len(after), spot)...  4.56 us
    pallas_call x3, Pallas kernels, gather(): pl.pallas_call(functools.partial(gather_kernel, span, parts, spot), in_sp...  3.44 us
    unnamed x8, local copies, waits for them, and re-layouts  3.41 us
  transfers between devices with their start and end apart: 29, of which 16 were waited for; matrix products, arithmetic and copies ran while one was open for 0% of the time, Pallas kernels for 21%

profile of v5, /device:TPU:0, one launch (start us, length us, event | category | flops | bytes accessed | tf_op | source)
XLA Modules:
  0.0 86.8 jit_solution(11346727298778778403)
XLA Ops:
  0.0 1.4 %shard_map.37 = (f32[2,7,32,256]{3,2,1,0:T(8,128)S(1)}, f32[2,7,32,256]{3,2,1,0:T(8,128)S(1)}, f32[8,128]{1,0:T(8,128)S(1)}) custom-call(s32[1,512]{1,0:T(1,128)} %signs.7, f32[1,16,128,512]{3,2,1,0:T(8,128)} %gradient.7), custom_call_target="tpu_custom_call" | custom-call | flops 1 | bytes 1 | tf_op jit(solution)/shard_map/pallas_call | solution.py:123
  1.4 3.0 %collective-permute-start.2 = (f32[2,7,32,256]{3,2,1,0:T(8,128)S(1)}, f32[2,7,32,256]{3,2,1,0:T(8,128)S(1)}, u32[]{:S(2)}, u32[]{:S(2)}) collective-permute-start(f32[2,7,32,256]{3,2,1,0:T(8,128)S(1)} %get-tuple-element.42), channel_id=1, source_target_pairs={{0,8},{8,0},{16,24},{24,16},{1,9},{9,1},{17,25},{25,17},{2,10},{10... | collective-permute-start | bytes 1376264 | tf_op jit(solution)/shard_map/ppermute | solution.py:34
  4.4 1.5 %collective-permute-start.3 = (f32[2,7,32,256]{3,2,1,0:T(8,128)S(1)}, f32[2,7,32,256]{3,2,1,0:T(8,128)S(1)}, u32[]{:S(2)}, u32[]{:S(2)}) collective-permute-start(f32[2,7,32,256]{3,2,1,0:T(8,128)S(1)} %get-tuple-element.43), channel_id=1, source_target_pairs={{0,16},{16,0},{8,24},{24,8},{1,17},{17,1},{9,25},{25,9},{2,18},{18... | collective-permute-start | bytes 1376264 | tf_op jit(solution)/shard_map/ppermute | solution.py:38
  5.9 2.0 %shard_map.38 = (f32[2,4,32,256]{3,2,1,0:T(8,128)}, f32[2,4,32,256]{3,2,1,0:T(8,128)}, f32[8,128]{1,0:T(8,128)S(1)}) custom-call(s32[1,512]{1,0:T(1,128)} %signs.7, f32[1,16,128,512]{3,2,1,0:T(8,128)} %gradient.7, f32[8,128]{1,0:T(8,128)S(1)} %get-tuple-element.33.rest_0_), custom_call_target="tpu_custom_call" | custom-call | flops 1 | bytes 1 | tf_op jit(solution)/shard_map/pallas_call | solution.py:123
  8.5 2.1 %shard_map.39 = (f32[16,32,256]{2,1,0:T(8,128)S(1)}, f32[16,32,256]{2,1,0:T(8,128)S(1)}, f32[16,32,512]{2,1,0:T(8,128)S(1)}) custom-call(s32[1,512]{1,0:T(1,128)} %signs.7, f32[1,16,128,512]{3,2,1,0:T(8,128)} %gradient.7, f32[16,128,512]{2,1,0:T(8,128)} %model.1, f32[8,128]{1,0:T(8,128)S(1)} %get-tuple-element.34.rest_0_), custom_call_target="tpu_custom_call" | custom-call | flops 1 | bytes 1 | tf_op jit(solution)/shard_map/pallas_call | solution.py:168
  10.6 1.2 %shard_map.40 = (f32[2,5,32,256]{3,2,1,0:T(8,128)S(1)}, f32[2,5,32,256]{3,2,1,0:T(8,128)S(1)}, f32[8,128]{1,0:T(8,128)S(1)}) custom-call(s32[1,512]{1,0:T(1,128)} %signs.7, f32[1,16,128,512]{3,2,1,0:T(8,128)} %gradient.7, f32[16,32,512]{2,1,0:T(8,128)S(1)} %get-tuple-element.35.rest_0_.base), custom_call_target="tpu_custom_call" | custom-call | flops 1 | bytes 1 | tf_op jit(solution)/shard_map/pallas_call | solution.py:123
  11.9 0.7 copy-done
  12.6 0.7 copy-done.2
  13.3 2.4 %collective-permute-done.2.near_a.refs_0_ = f32[2,7,32,256]{3,2,1,0:T(8,128)S(1)} collective-permute-done((f32[2,7,32,256]{3,2,1,0:T(8,128)S(1)}, f32[2,7,32,256]{3,2,1,0:T(8,128)S(1)}, u32[]{:S(2)}, u32[]{:S(2)}) %collective-permute-start.2) | collective-permute-done | bytes 458784 | tf_op jit(solution)/shard_map/ppermute | solution.py:34
  15.7 2.1 %collective-permute-done.3.near_b.refs_1_ = f32[2,7,32,256]{3,2,1,0:T(8,128)S(1)} collective-permute-done((f32[2,7,32,256]{3,2,1,0:T(8,128)S(1)}, f32[2,7,32,256]{3,2,1,0:T(8,128)S(1)}, u32[]{:S(2)}, u32[]{:S(2)}) %collective-permute-start.3) | collective-permute-done | bytes 458784 | tf_op jit(solution)/shard_map/ppermute | solution.py:38
  17.8 0.8 shard_map.41
  18.6 1.5 %collective-permute-start.6 = (f32[7,32,256]{2,1,0:T(8,128)}, f32[7,32,256]{2,1,0:T(8,128)}, u32[]{:S(2)}, u32[]{:S(2)}) collective-permute-start(f32[7,32,256]{2,1,0:T(8,128)} %get-tuple-element.50), channel_id=1, source_target_pairs={{0,16},{16,0},{8,24},{24,8},{1,17},{17,1},{9,25},{25,9},{2,18},{18... | collective-permute-start | bytes 688136 | tf_op jit(solution)/shard_map/ppermute | solution.py:38
  21.1 2.4 %collective-permute-done.1.near_b.refs_1_ = f32[2,4,32,256]{3,2,1,0:T(8,128)S(1)} collective-permute-done((f32[2,4,32,256]{3,2,1,0:T(8,128)}, f32[2,4,32,256]{3,2,1,0:T(8,128)S(1)}, u32[]{:S(2)}, u32[]{:S(2)}) %collective-permute-start.1) | collective-permute-done | bytes 262176 | tf_op jit(solution)/shard_map/ppermute | solution.py:38
  23.4 1.0 %copy-done.1 = f32[2,5,32,256]{3,2,1,0:T(8,128)S(1)} copy-done((f32[2,5,32,256]{3,2,1,0:T(8,128)S(1)}, f32[2,5,32,256]{3,2,1,0:T(8,128)}, u32[]{:S(2)}) %copy-start.1) | copy-done | bytes 327704
  24.4 1.0 %copy-done.3 = f32[2,5,32,256]{3,2,1,0:T(8,128)S(1)} copy-done((f32[2,5,32,256]{3,2,1,0:T(8,128)S(1)}, f32[2,5,32,256]{3,2,1,0:T(8,128)}, u32[]{:S(2)}) %copy-start.3) | copy-done | bytes 327704
  25.6 2.0 %collective-permute-start.5 = (f32[2,5,32,256]{3,2,1,0:T(8,128)S(1)}, f32[2,5,32,256]{3,2,1,0:T(8,128)S(1)}, u32[]{:S(2)}, u32[]{:S(2)}) collective-permute-start(f32[2,5,32,256]{3,2,1,0:T(8,128)S(1)} %get-tuple-element.47), channel_id=1, source_target_pairs={{0,16},{16,0},{8,24},{24,8},{1,17},{17,1},{9,25},{25,9},{2,18},{18... | collective-permute-start | bytes 983048 | tf_op jit(solution)/shard_map/ppermute | solution.py:38
  28.1 1.1 %shard_map.43.refs_0_.refs_1_ = f32[7,32,512]{2,1,0:T(8,128)S(1)} custom-call(f32[16,32,512]{2,1,0:T(8,128)S(1)} %get-tuple-element.35.rest_0_.base, f32[2,7,32,256]{3,2,1,0:T(8,128)S(1)} %collective-permute-done.2.near_a.refs_0_, f32[2,7,32,256]{3,2,1,0:T(8,128)S(1)} %collective-permute-done.3.near_b.refs_1_, f32[7,32,256]{2,1,0:T(8,128)} %collective-permute-done.6.refs_2_, ...), custom_call_target="tpu_custom_call" | custom-call | flops 1 | bytes 1 | tf_op jit(solution)/shard_map/pallas_call | solution.py:237
  29.3 1.4 %collective-permute-done.8.refs_1_.refs_0_ = f32[3,32,512]{2,1,0:T(8,128)S(1)} collective-permute-done((f32[3,32,512]{2,1,0:T(8,128)S(1)}, f32[3,32,512]{2,1,0:T(8,128)S(1)}, u32[]{:S(2)}, u32[]{:S(2)}) %collective-permute-start.8) | collective-permute-done | bytes 196640 | tf_op jit(solution)/shard_map/ppermute | solution.py:525
  30.8 1.0 %collective-permute-start.11 = (f32[10,3,512]{2,1,0:T(4,128)S(1)}, f32[10,3,512]{2,1,0:T(4,128)S(1)}, u32[]{:S(2)}, u32[]{:S(2)}) collective-permute-start(f32[10,3,512]{2,1,0:T(4,128)S(1)} %get-tuple-element.53.rest_2_), channel_id=1, source_target_pairs={{0,8},{8,0},{24,16},{16,24},{1,9},{9,1},{25,17},{17,25},{2,10},{10... | collective-permute-start | bytes 184328 | tf_op jit(solution)/shard_map/ppermute | solution.py:477
  31.9 0.7 collective-permute-start.12
  32.5 0.9 %collective-permute-done.4.near_a.refs_2_ = f32[2,5,32,256]{3,2,1,0:T(8,128)S(1)} collective-permute-done((f32[2,5,32,256]{3,2,1,0:T(8,128)S(1)}, f32[2,5,32,256]{3,2,1,0:T(8,128)S(1)}, u32[]{:S(2)}, u32[]{:S(2)}) %collective-permute-start.4) | collective-permute-done | bytes 327712 | tf_op jit(solution)/shard_map/ppermute | solution.py:34
  34.0 2.6 %collective-permute-start.10 = (f32[9,32,256]{2,1,0:T(8,128)S(1)}, f32[9,32,256]{2,1,0:T(8,128)S(1)}, u32[]{:S(2)}, u32[]{:S(2)}) collective-permute-start(f32[9,32,256]{2,1,0:T(8,128)S(1)} %get-tuple-element.56), channel_id=1, source_target_pairs={{0,8},{8,0},{16,24},{24,16},{1,9},{9,1},{17,25},{25,17},{2,10},{10... | collective-permute-start | bytes 884744 | tf_op jit(solution)/shard_map/ppermute | solution.py:34
  37.0 2.3 %shard_map.46.refs_6_.refs_0_ = f32[2,4,32,256]{3,2,1,0:T(8,128)S(1)} custom-call(f32[3,32,512]{2,1,0:T(8,128)S(1)} %collective-permute-done.8.refs_1_.refs_0_, f32[7,32,512]{2,1,0:T(8,128)S(1)} %shard_map.43.refs_0_.refs_1_, f32[10,3,512]{2,1,0:T(4,128)S(1)} %collective-permute-done.11.refs_2_, f32[10,3,512]{2,1,0:T(4,128)S(1)} %collective-permute-done.12.refs_3_.refs_4_, ...), custom_call_target="tpu_custom_call" | custom-call | flops 1 | bytes 100000000 | tf_op jit(solution)/shard_map/pallas_call | solution.py:382
  39.3 3.0 %collective-permute-start.16 = (f32[2,4,32,256]{3,2,1,0:T(8,128)S(1)}, f32[2,4,32,256]{3,2,1,0:T(8,128)S(1)}, u32[]{:S(2)}, u32[]{:S(2)}) collective-permute-start(f32[2,4,32,256]{3,2,1,0:T(8,128)S(1)} %shard_map.46.refs_6_.refs_0_), channel_id=1, source_target_pairs={{0,16},{16,0},{8,24},{24,8},{1,17},{17,1},{9,25},{25,9},{2,18},{18... | collective-permute-start | bytes 786440 | tf_op jit(solution)/shard_map/ppermute | solution.py:38
  42.3 0.8 collective-permute-start.15
  43.4 3.1 %collective-permute-done.9.refs_4_ = f32[9,32,256]{2,1,0:T(8,128)S(1)} collective-permute-done((f32[9,32,256]{2,1,0:T(8,128)S(1)}, f32[9,32,256]{2,1,0:T(8,128)S(1)}, u32[]{:S(2)}, u32[]{:S(2)}) %collective-permute-start.9) | collective-permute-done | bytes 294944 | tf_op jit(solution)/shard_map/ppermute | solution.py:38
  47.1 0.8 collective-permute-start.14
  47.9 2.5 %collective-permute-done.16.refs_5_.refs_4_ = f32[2,4,32,256]{3,2,1,0:T(8,128)S(1)} collective-permute-done((f32[2,4,32,256]{3,2,1,0:T(8,128)S(1)}, f32[2,4,32,256]{3,2,1,0:T(8,128)S(1)}, u32[]{:S(2)}, u32[]{:S(2)}) %collective-permute-start.16) | collective-permute-done | bytes 262176 | tf_op jit(solution)/shard_map/ppermute | solution.py:38
  50.4 1.6 %collective-permute-start.27 = (f32[4,32,256]{2,1,0:T(8,128)S(1)}, f32[4,32,256]{2,1,0:T(8,128)S(1)}, u32[]{:S(2)}, u32[]{:S(2)}) collective-permute-start(f32[4,32,256]{2,1,0:T(8,128)S(1)} %slice_bitcast_fusion.5), channel_id=1, source_target_pairs={{0,8},{8,0},{16,24},{24,16},{1,9},{9,1},{17,25},{25,17},{2,10},{10... | collective-permute-start | bytes 393224 | tf_op jit(solution)/shard_map/ppermute | solution.py:34
  52.0 2.9 %shard_map.48.refs_3_.refs_0_ = f32[2,6,32,256]{3,2,1,0:T(8,128)S(1)} custom-call(f32[7,32,512]{2,1,0:T(8,128)S(1)} %shard_map.43.refs_0_.refs_1_, f32[9,32,512]{2,1,0:T(8,128)S(1)} %get-tuple-element.58.refs_1_.refs_0_, f32[10,3,512]{2,1,0:T(4,128)S(1)} %collective-permute-done.11.refs_2_, f32[9,3,512]{2,1,0:T(4,128)S(1)} %collective-permute-done.13.refs_3_.refs_1_, ...), custom_call_target="tpu_custom_call" | custom-call | flops 1 | bytes 100000000 | tf_op jit(solution)/shard_map/pallas_call | solution.py:382
  54.9 4.3 %collective-permute-start.24 = (f32[2,6,32,256]{3,2,1,0:T(8,128)S(1)}, f32[2,6,32,256]{3,2,1,0:T(8,128)S(1)}, u32[]{:S(2)}, u32[]{:S(2)}) collective-permute-start(f32[2,6,32,256]{3,2,1,0:T(8,128)S(1)} %shard_map.48.refs_3_.refs_0_), channel_id=1, source_target_pairs={{0,16},{16,0},{8,24},{24,8},{1,17},{17,1},{9,25},{25,9},{2,18},{18... | collective-permute-start | bytes 1179656 | tf_op jit(solution)/shard_map/ppermute | solution.py:38
  59.3 0.7 collective-permute-start.23
  60.0 2.9 %shard_map.49.refs_0_ = f32[2,6,32,256]{3,2,1,0:T(8,128)S(1)} custom-call(f32[9,32,512]{2,1,0:T(8,128)S(1)} %get-tuple-element.58.refs_1_.refs_0_, f32[9,3,512]{2,1,0:T(4,128)S(1)} %collective-permute-done.13.refs_3_.refs_1_, f32[9,3,512]{2,1,0:T(4,128)S(1)} %collective-permute-done.14.refs_5_.refs_2_, f32[2,6,32,256]{3,2,1,0:T(8,128)S(1)} %shard_map.48.refs_3_.refs_0_, ...), custom_call_target="tpu_custom_call" | custom-call | flops 1 | bytes 100000000 | tf_op jit(solution)/shard_map/pallas_call | solution.py:382
  63.0 1.3 %collective-permute-start.19 = (f32[6,32,256]{2,1,0:T(8,128)S(1)}, f32[6,32,256]{2,1,0:T(8,128)S(1)}, u32[]{:S(2)}, u32[]{:S(2)}) collective-permute-start(f32[6,32,256]{2,1,0:T(8,128)S(1)} %get-tuple-element.62), channel_id=1, source_target_pairs={{0,16},{16,0},{8,24},{24,8},{1,17},{17,1},{9,25},{25,9},{2,18},{18... | collective-permute-start | bytes 589832 | tf_op jit(solution)/shard_map/ppermute | solution.py:38
  64.4 4.0 %collective-permute-done.24.refs_4_ = f32[2,6,32,256]{3,2,1,0:T(8,128)S(1)} collective-permute-done((f32[2,6,32,256]{3,2,1,0:T(8,128)S(1)}, f32[2,6,32,256]{3,2,1,0:T(8,128)S(1)}, u32[]{:S(2)}, u32[]{:S(2)}) %collective-permute-start.24) | collective-permute-done | bytes 393248 | tf_op jit(solution)/shard_map/ppermute | solution.py:38
  68.4 1.6 %collective-permute-start.18 = (f32[6,32,256]{2,1,0:T(8,128)S(1)}, f32[6,32,256]{2,1,0:T(8,128)S(1)}, u32[]{:S(2)}, u32[]{:S(2)}) collective-permute-start(f32[6,32,256]{2,1,0:T(8,128)S(1)} %get-tuple-element.61), channel_id=1, source_target_pairs={{0,8},{8,0},{16,24},{24,16},{1,9},{9,1},{17,25},{25,17},{2,10},{10... | collective-permute-start | bytes 589832 | tf_op jit(solution)/shard_map/ppermute | solution.py:34
  70.0 1.1 %collective-permute-done.23.refs_1_ = f32[2,6,32,256]{3,2,1,0:T(8,128)S(1)} collective-permute-done((f32[2,6,32,256]{3,2,1,0:T(8,128)S(1)}, f32[2,6,32,256]{3,2,1,0:T(8,128)S(1)}, u32[]{:S(2)}, u32[]{:S(2)}) %collective-permute-start.23) | collective-permute-done | bytes 393248 | tf_op jit(solution)/shard_map/ppermute | solution.py:34
  71.2 2.1 %collective-permute-start.17 = (f32[6,32,256]{2,1,0:T(8,128)S(1)}, f32[6,32,256]{2,1,0:T(8,128)S(1)}, u32[]{:S(2)}, u32[]{:S(2)}) collective-permute-start(f32[6,32,256]{2,1,0:T(8,128)S(1)} %get-tuple-element.62), channel_id=1, source_target_pairs={{0,8},{8,0},{16,24},{24,16},{1,9},{9,1},{17,25},{25,17},{2,10},{10... | collective-permute-start | bytes 589832 | tf_op jit(solution)/shard_map/ppermute | solution.py:34
  73.2 1.4 %collective-permute-start.26 = (f32[6,32,256]{2,1,0:T(8,128)S(1)}, f32[6,32,256]{2,1,0:T(8,128)S(1)}, u32[]{:S(2)}, u32[]{:S(2)}) collective-permute-start(f32[6,32,256]{2,1,0:T(8,128)S(1)} %slice_bitcast_fusion), channel_id=1, source_target_pairs={{0,16},{16,0},{8,24},{24,8},{1,17},{17,1},{9,25},{25,9},{2,18},{18... | collective-permute-start | bytes 589832 | tf_op jit(solution)/shard_map/ppermute | solution.py:38
  74.7 0.7 collective-permute-done.19.refs_5_
  75.4 1.7 %collective-permute-start.22 = (f32[6,32,256]{2,1,0:T(8,128)S(1)}, f32[6,32,256]{2,1,0:T(8,128)S(1)}, u32[]{:S(2)}, u32[]{:S(2)}) collective-permute-start(f32[6,32,256]{2,1,0:T(8,128)S(1)} %get-tuple-element.61), channel_id=1, source_target_pairs={{0,16},{16,0},{8,24},{24,8},{1,17},{17,1},{9,25},{25,9},{2,18},{18... | collective-permute-start | bytes 589832 | tf_op jit(solution)/shard_map/ppermute | solution.py:38
  77.1 0.7 collective-permute-start.20
  77.8 1.9 %collective-permute-done.25.refs_2_ = f32[6,32,256]{2,1,0:T(8,128)S(1)} collective-permute-done((f32[6,32,256]{2,1,0:T(8,128)S(1)}, f32[6,32,256]{2,1,0:T(8,128)S(1)}, u32[]{:S(2)}, u32[]{:S(2)}) %collective-permute-start.25) | collective-permute-done | bytes 196640 | tf_op jit(solution)/shard_map/ppermute | solution.py:34
  79.8 1.9 %collective-permute-start.21 = (f32[6,32,256]{2,1,0:T(8,128)S(1)}, f32[6,32,256]{2,1,0:T(8,128)S(1)}, u32[]{:S(2)}, u32[]{:S(2)}) collective-permute-start(f32[6,32,256]{2,1,0:T(8,128)S(1)} %collective-permute-done.18.refs_2_), channel_id=1, source_target_pairs={{0,16},{16,0},{8,24},{24,8},{1,17},{17,1},{9,25},{25,9},{2,18},{18... | collective-permute-start | bytes 589832 | tf_op jit(solution)/shard_map/ppermute | solution.py:38
  81.7 1.0 %shard_map.50.refs_5_ = f32[16,128,512]{2,1,0:T(8,128)} custom-call(f32[2,4,32,256]{3,2,1,0:T(8,128)S(1)} %shard_map.46.refs_6_.refs_0_, f32[2,4,32,256]{3,2,1,0:T(8,128)S(1)} %collective-permute-done.15.refs_4_.refs_1_, f32[4,32,256]{2,1,0:T(8,128)S(1)} %collective-permute-done.27.refs_2_, f32[4,32,256]{2,1,0:T(8,128)S(1)} %collective-permute-done.28.refs_3_, ...), custom_call_target="tpu_custom_call" | custom-call | flops 1 | bytes 1 | tf_op jit(solution)/shard_map/pallas_call | solution.py:413
  82.8 1.2 %shard_map.51.refs_7_ = f32[16,128,512]{2,1,0:T(8,128)} custom-call(f32[2,6,32,256]{3,2,1,0:T(8,128)S(1)} %shard_map.48.refs_3_.refs_0_, f32[2,6,32,256]{3,2,1,0:T(8,128)S(1)} %collective-permute-done.23.refs_1_, f32[6,32,256]{2,1,0:T(8,128)S(1)} %collective-permute-done.25.refs_2_, ...), custom_call_target="tpu_custom_call", output_to_operand_aliasing={{}: (5, {})} | custom-call | flops 1 | bytes 1 | tf_op jit(solution)/shard_map/pallas_call | solution.py:413
  84.0 1.4 %collective-permute-done.21.refs_4_ = f32[6,32,256]{2,1,0:T(8,128)S(1)} collective-permute-done((f32[6,32,256]{2,1,0:T(8,128)S(1)}, f32[6,32,256]{2,1,0:T(8,128)S(1)}, u32[]{:S(2)}, u32[]{:S(2)}) %collective-permute-start.21) | collective-permute-done | bytes 196640 | tf_op jit(solution)/shard_map/ppermute | solution.py:38
  85.5 1.2 %shard_map.52 = f32[16,128,512]{2,1,0:T(8,128)} custom-call(f32[2,6,32,256]{3,2,1,0:T(8,128)S(1)} %shard_map.49.refs_0_, f32[6,32,256]{2,1,0:T(8,128)S(1)} %collective-permute-done.17.refs_1_, f32[6,32,256]{2,1,0:T(8,128)S(1)} %collective-permute-done.18.refs_2_, f32[6,32,256]{2,1,0:T(8,128)S(1)} %collective-permute-done.20.refs_3_, ...), custom_call_target="tpu_custom_call", output_to_operand_aliasing={{}: (7, {})} | custom-call | flops 1 | bytes 1 | tf_op jit(solution)/shard_map/pallas_call | solution.py:413
  (40 shorter events, 4.4 us)
Async XLA Ops:
  1.4 14.4 %collective-permute-start.2 = (f32[2,7,32,256]{3,2,1,0:T(8,128)S(1)}, f32[2,7,32,256]{3,2,1,0:T(8,128)S(1)}, u32[]{:S(2)}, u32[]{:S(2)}) collective-permute-start(f32[2,7,32,256]{3,2,1,0:T(8,128)S(1)} %get-tuple-element.42), channel_id=1, source_target_pairs={{0,8},{8,0},{16,24},{24,16},{1,9},{9,1},{17,25},{25,17},{2,10},{10... | collective-permute-start | bytes 1376264 | tf_op jit(solution)/shard_map/ppermute | solution.py:34
  4.4 13.4 %collective-permute-start.3 = (f32[2,7,32,256]{3,2,1,0:T(8,128)S(1)}, f32[2,7,32,256]{3,2,1,0:T(8,128)S(1)}, u32[]{:S(2)}, u32[]{:S(2)}) collective-permute-start(f32[2,7,32,256]{3,2,1,0:T(8,128)S(1)} %get-tuple-element.43), channel_id=1, source_target_pairs={{0,16},{16,0},{8,24},{24,8},{1,17},{17,1},{9,25},{25,9},{2,18},{18... | collective-permute-start | bytes 1376264 | tf_op jit(solution)/shard_map/ppermute | solution.py:38
  7.9 13.2 %collective-permute-start = (f32[2,4,32,256]{3,2,1,0:T(8,128)}, f32[2,4,32,256]{3,2,1,0:T(8,128)S(1)}, u32[]{:S(2)}, u32[]{:S(2)}) collective-permute-start(f32[2,4,32,256]{3,2,1,0:T(8,128)} %get-tuple-element.36), channel_id=1, source_target_pairs={{0,8},{8,0},{16,24},{24,16},{1,9},{9,1},{17,25},{25,17},{2,10},{10... | collective-permute-start | bytes 786440 | tf_op jit(solution)/shard_map/ppermute | solution.py:34
  8.5 15.0 %collective-permute-start.1 = (f32[2,4,32,256]{3,2,1,0:T(8,128)}, f32[2,4,32,256]{3,2,1,0:T(8,128)S(1)}, u32[]{:S(2)}, u32[]{:S(2)}) collective-permute-start(f32[2,4,32,256]{3,2,1,0:T(8,128)} %get-tuple-element.37), channel_id=1, source_target_pairs={{0,16},{16,0},{8,24},{24,8},{1,17},{17,1},{9,25},{25,9},{2,18},{18... | collective-permute-start | bytes 786440 | tf_op jit(solution)/shard_map/ppermute | solution.py:38
  11.9 0.7 copy-start
  12.6 0.7 copy-start.2
  18.6 9.5 %collective-permute-start.6 = (f32[7,32,256]{2,1,0:T(8,128)}, f32[7,32,256]{2,1,0:T(8,128)}, u32[]{:S(2)}, u32[]{:S(2)}) collective-permute-start(f32[7,32,256]{2,1,0:T(8,128)} %get-tuple-element.50), channel_id=1, source_target_pairs={{0,16},{16,0},{8,24},{24,8},{1,17},{17,1},{9,25},{25,9},{2,18},{18... | collective-permute-start | bytes 688136 | tf_op jit(solution)/shard_map/ppermute | solution.py:38
  20.2 7.9 %collective-permute-start.7 = (f32[7,32,256]{2,1,0:T(8,128)}, f32[7,32,256]{2,1,0:T(8,128)}, u32[]{:S(2)}, u32[]{:S(2)}) collective-permute-start(f32[7,32,256]{2,1,0:T(8,128)} %get-tuple-element.51), channel_id=1, source_target_pairs={{0,8},{8,0},{16,24},{24,16},{1,9},{9,1},{17,25},{25,17},{2,10},{10... | collective-permute-start | bytes 688136 | tf_op jit(solution)/shard_map/ppermute | solution.py:34
  23.4 1.0 %copy-start.1 = (f32[2,5,32,256]{3,2,1,0:T(8,128)S(1)}, f32[2,5,32,256]{3,2,1,0:T(8,128)}, u32[]{:S(2)}) copy-start(f32[2,5,32,256]{3,2,1,0:T(8,128)} %copy-done) | copy-start | bytes 983044
  24.4 1.0 %copy-start.3 = (f32[2,5,32,256]{3,2,1,0:T(8,128)S(1)}, f32[2,5,32,256]{3,2,1,0:T(8,128)}, u32[]{:S(2)}) copy-start(f32[2,5,32,256]{3,2,1,0:T(8,128)} %copy-done.2) | copy-start | bytes 983044
  25.5 8.0 %collective-permute-start.4 = (f32[2,5,32,256]{3,2,1,0:T(8,128)S(1)}, f32[2,5,32,256]{3,2,1,0:T(8,128)S(1)}, u32[]{:S(2)}, u32[]{:S(2)}) collective-permute-start(f32[2,5,32,256]{3,2,1,0:T(8,128)S(1)} %get-tuple-element.46), channel_id=1, source_target_pairs={{0,8},{8,0},{16,24},{24,16},{1,9},{9,1},{17,25},{25,17},{2,10},{10... | collective-permute-start | bytes 983048 | tf_op jit(solution)/shard_map/ppermute | solution.py:34
  25.6 8.3 %collective-permute-start.5 = (f32[2,5,32,256]{3,2,1,0:T(8,128)S(1)}, f32[2,5,32,256]{3,2,1,0:T(8,128)S(1)}, u32[]{:S(2)}, u32[]{:S(2)}) collective-permute-start(f32[2,5,32,256]{3,2,1,0:T(8,128)S(1)} %get-tuple-element.47), channel_id=1, source_target_pairs={{0,16},{16,0},{8,24},{24,8},{1,17},{17,1},{9,25},{25,9},{2,18},{18... | collective-permute-start | bytes 983048 | tf_op jit(solution)/shard_map/ppermute | solution.py:38
  29.3 1.5 %collective-permute-start.8 = (f32[3,32,512]{2,1,0:T(8,128)S(1)}, f32[3,32,512]{2,1,0:T(8,128)S(1)}, u32[]{:S(2)}, u32[]{:S(2)}) collective-permute-start(f32[3,32,512]{2,1,0:T(8,128)S(1)} %constant_dynamic-slice_fusion), channel_id=1, source_target_pairs={{0,4},{4,0},{1,5},{5,1},{2,6},{6,2},{3,7},{7,3},{8,12},{12,8},{9,1... | collective-permute-start | bytes 589832 | tf_op jit(solution)/shard_map/ppermute | solution.py:525
  30.8 6.2 %collective-permute-start.11 = (f32[10,3,512]{2,1,0:T(4,128)S(1)}, f32[10,3,512]{2,1,0:T(4,128)S(1)}, u32[]{:S(2)}, u32[]{:S(2)}) collective-permute-start(f32[10,3,512]{2,1,0:T(4,128)S(1)} %get-tuple-element.53.rest_2_), channel_id=1, source_target_pairs={{0,8},{8,0},{24,16},{16,24},{1,9},{9,1},{25,17},{17,25},{2,10},{10... | collective-permute-start | bytes 184328 | tf_op jit(solution)/shard_map/ppermute | solution.py:477
  31.9 5.2 %collective-permute-start.12 = (f32[10,3,512]{2,1,0:T(4,128)S(1)}, f32[10,3,512]{2,1,0:T(4,128)S(1)}, u32[]{:S(2)}, u32[]{:S(2)}) collective-permute-start(f32[10,3,512]{2,1,0:T(4,128)S(1)} %get-tuple-element.54.rest_3_), channel_id=1, source_target_pairs={{8,24},{24,8},{16,1},{1,16},{9,25},{25,9},{17,2},{2,17},{10,26},{2... | collective-permute-start | bytes 184328 | tf_op jit(solution)/shard_map/ppermute | solution.py:477
  34.0 9.4 %collective-permute-start.10 = (f32[9,32,256]{2,1,0:T(8,128)S(1)}, f32[9,32,256]{2,1,0:T(8,128)S(1)}, u32[]{:S(2)}, u32[]{:S(2)}) collective-permute-start(f32[9,32,256]{2,1,0:T(8,128)S(1)} %get-tuple-element.56), channel_id=1, source_target_pairs={{0,8},{8,0},{16,24},{24,16},{1,9},{9,1},{17,25},{25,17},{2,10},{10... | collective-permute-start | bytes 884744 | tf_op jit(solution)/shard_map/ppermute | solution.py:34
  36.6 9.9 %collective-permute-start.9 = (f32[9,32,256]{2,1,0:T(8,128)S(1)}, f32[9,32,256]{2,1,0:T(8,128)S(1)}, u32[]{:S(2)}, u32[]{:S(2)}) collective-permute-start(f32[9,32,256]{2,1,0:T(8,128)S(1)} %get-tuple-element.55), channel_id=1, source_target_pairs={{0,16},{16,0},{8,24},{24,8},{1,17},{17,1},{9,25},{25,9},{2,18},{18... | collective-permute-start | bytes 884744 | tf_op jit(solution)/shard_map/ppermute | solution.py:38
  39.3 11.1 %collective-permute-start.16 = (f32[2,4,32,256]{3,2,1,0:T(8,128)S(1)}, f32[2,4,32,256]{3,2,1,0:T(8,128)S(1)}, u32[]{:S(2)}, u32[]{:S(2)}) collective-permute-start(f32[2,4,32,256]{3,2,1,0:T(8,128)S(1)} %shard_map.46.refs_6_.refs_0_), channel_id=1, source_target_pairs={{0,16},{16,0},{8,24},{24,8},{1,17},{17,1},{9,25},{25,9},{2,18},{18... | collective-permute-start | bytes 786440 | tf_op jit(solution)/shard_map/ppermute | solution.py:38
  42.3 16.9 %collective-permute-start.15 = (f32[2,4,32,256]{3,2,1,0:T(8,128)S(1)}, f32[2,4,32,256]{3,2,1,0:T(8,128)S(1)}, u32[]{:S(2)}, u32[]{:S(2)}) collective-permute-start(f32[2,4,32,256]{3,2,1,0:T(8,128)S(1)} %shard_map.46.refs_6_.refs_0_), channel_id=1, source_target_pairs={{0,8},{8,0},{16,24},{24,16},{1,9},{9,1},{17,25},{25,17},{2,10},{10... | collective-permute-start | bytes 786440 | tf_op jit(solution)/shard_map/ppermute | solution.py:34
  46.6 5.4 %collective-permute-start.13 = (f32[9,3,512]{2,1,0:T(4,128)S(1)}, f32[9,3,512]{2,1,0:T(4,128)S(1)}, u32[]{:S(2)}, u32[]{:S(2)}) collective-permute-start(f32[9,3,512]{2,1,0:T(4,128)S(1)} %get-tuple-element.59), channel_id=1, source_target_pairs={{0,8},{8,0},{24,16},{16,24},{1,9},{9,1},{25,17},{17,25},{2,10},{10... | collective-permute-start | bytes 165896 | tf_op jit(solution)/shard_map/ppermute | solution.py:477
  47.1 5.0 %collective-permute-start.14 = (f32[9,3,512]{2,1,0:T(4,128)S(1)}, f32[9,3,512]{2,1,0:T(4,128)S(1)}, u32[]{:S(2)}, u32[]{:S(2)}) collective-permute-start(f32[9,3,512]{2,1,0:T(4,128)S(1)} %get-tuple-element.60), channel_id=1, source_target_pairs={{8,24},{24,8},{16,1},{1,16},{9,25},{25,9},{17,2},{2,17},{10,26},{2... | collective-permute-start | bytes 165896 | tf_op jit(solution)/shard_map/ppermute | solution.py:477
  50.4 20.7 %collective-permute-start.27 = (f32[4,32,256]{2,1,0:T(8,128)S(1)}, f32[4,32,256]{2,1,0:T(8,128)S(1)}, u32[]{:S(2)}, u32[]{:S(2)}) collective-permute-start(f32[4,32,256]{2,1,0:T(8,128)S(1)} %slice_bitcast_fusion.5), channel_id=1, source_target_pairs={{0,8},{8,0},{16,24},{24,16},{1,9},{9,1},{17,25},{25,17},{2,10},{10... | collective-permute-start | bytes 393224 | tf_op jit(solution)/shard_map/ppermute | solution.py:34
  54.9 13.4 %collective-permute-start.24 = (f32[2,6,32,256]{3,2,1,0:T(8,128)S(1)}, f32[2,6,32,256]{3,2,1,0:T(8,128)S(1)}, u32[]{:S(2)}, u32[]{:S(2)}) collective-permute-start(f32[2,6,32,256]{3,2,1,0:T(8,128)S(1)} %shard_map.48.refs_3_.refs_0_), channel_id=1, source_target_pairs={{0,16},{16,0},{8,24},{24,8},{1,17},{17,1},{9,25},{25,9},{2,18},{18... | collective-permute-start | bytes 1179656 | tf_op jit(solution)/shard_map/ppermute | solution.py:38
  59.2 14.0 %collective-permute-start.28 = (f32[4,32,256]{2,1,0:T(8,128)S(1)}, f32[4,32,256]{2,1,0:T(8,128)S(1)}, u32[]{:S(2)}, u32[]{:S(2)}) collective-permute-start(f32[4,32,256]{2,1,0:T(8,128)S(1)} %slice_bitcast_fusion.4), channel_id=1, source_target_pairs={{0,16},{16,0},{8,24},{24,8},{1,17},{17,1},{9,25},{25,9},{2,18},{18... | collective-permute-start | bytes 393224 | tf_op jit(solution)/shard_map/ppermute | solution.py:38
  59.3 11.8 %collective-permute-start.23 = (f32[2,6,32,256]{3,2,1,0:T(8,128)S(1)}, f32[2,6,32,256]{3,2,1,0:T(8,128)S(1)}, u32[]{:S(2)}, u32[]{:S(2)}) collective-permute-start(f32[2,6,32,256]{3,2,1,0:T(8,128)S(1)} %shard_map.48.refs_3_.refs_0_), channel_id=1, source_target_pairs={{0,8},{8,0},{16,24},{24,16},{1,9},{9,1},{17,25},{25,17},{2,10},{10... | collective-permute-start | bytes 1179656 | tf_op jit(solution)/shard_map/ppermute | solution.py:34
  63.0 12.4 %collective-permute-start.19 = (f32[6,32,256]{2,1,0:T(8,128)S(1)}, f32[6,32,256]{2,1,0:T(8,128)S(1)}, u32[]{:S(2)}, u32[]{:S(2)}) collective-permute-start(f32[6,32,256]{2,1,0:T(8,128)S(1)} %get-tuple-element.62), channel_id=1, source_target_pairs={{0,16},{16,0},{8,24},{24,8},{1,17},{17,1},{9,25},{25,9},{2,18},{18... | collective-permute-start | bytes 589832 | tf_op jit(solution)/shard_map/ppermute | solution.py:38
  68.4 8.8 %collective-permute-start.18 = (f32[6,32,256]{2,1,0:T(8,128)S(1)}, f32[6,32,256]{2,1,0:T(8,128)S(1)}, u32[]{:S(2)}, u32[]{:S(2)}) collective-permute-start(f32[6,32,256]{2,1,0:T(8,128)S(1)} %get-tuple-element.61), channel_id=1, source_target_pairs={{0,8},{8,0},{16,24},{24,16},{1,9},{9,1},{17,25},{25,17},{2,10},{10... | collective-permute-start | bytes 589832 | tf_op jit(solution)/shard_map/ppermute | solution.py:34
  71.1 8.7 %collective-permute-start.25 = (f32[6,32,256]{2,1,0:T(8,128)S(1)}, f32[6,32,256]{2,1,0:T(8,128)S(1)}, u32[]{:S(2)}, u32[]{:S(2)}) collective-permute-start(f32[6,32,256]{2,1,0:T(8,128)S(1)} %slice_bitcast_fusion.1), channel_id=1, source_target_pairs={{0,8},{8,0},{16,24},{24,16},{1,9},{9,1},{17,25},{25,17},{2,10},{10... | collective-permute-start | bytes 589832 | tf_op jit(solution)/shard_map/ppermute | solution.py:34
  71.2 12.9 %collective-permute-start.17 = (f32[6,32,256]{2,1,0:T(8,128)S(1)}, f32[6,32,256]{2,1,0:T(8,128)S(1)}, u32[]{:S(2)}, u32[]{:S(2)}) collective-permute-start(f32[6,32,256]{2,1,0:T(8,128)S(1)} %get-tuple-element.62), channel_id=1, source_target_pairs={{0,8},{8,0},{16,24},{24,16},{1,9},{9,1},{17,25},{25,17},{2,10},{10... | collective-permute-start | bytes 589832 | tf_op jit(solution)/shard_map/ppermute | solution.py:34
  73.2 9.5 %collective-permute-start.26 = (f32[6,32,256]{2,1,0:T(8,128)S(1)}, f32[6,32,256]{2,1,0:T(8,128)S(1)}, u32[]{:S(2)}, u32[]{:S(2)}) collective-permute-start(f32[6,32,256]{2,1,0:T(8,128)S(1)} %slice_bitcast_fusion), channel_id=1, source_target_pairs={{0,16},{16,0},{8,24},{24,8},{1,17},{17,1},{9,25},{25,9},{2,18},{18... | collective-permute-start | bytes 589832 | tf_op jit(solution)/shard_map/ppermute | solution.py:38
  75.4 8.6 %collective-permute-start.22 = (f32[6,32,256]{2,1,0:T(8,128)S(1)}, f32[6,32,256]{2,1,0:T(8,128)S(1)}, u32[]{:S(2)}, u32[]{:S(2)}) collective-permute-start(f32[6,32,256]{2,1,0:T(8,128)S(1)} %get-tuple-element.61), channel_id=1, source_target_pairs={{0,16},{16,0},{8,24},{24,8},{1,17},{17,1},{9,25},{25,9},{2,18},{18... | collective-permute-start | bytes 589832 | tf_op jit(solution)/shard_map/ppermute | solution.py:38
  77.1 6.9 %collective-permute-start.20 = (f32[6,32,256]{2,1,0:T(8,128)S(1)}, f32[6,32,256]{2,1,0:T(8,128)S(1)}, u32[]{:S(2)}, u32[]{:S(2)}) collective-permute-start(f32[6,32,256]{2,1,0:T(8,128)S(1)} %collective-permute-done.19.refs_5_), channel_id=1, source_target_pairs={{0,8},{8,0},{16,24},{24,16},{1,9},{9,1},{17,25},{25,17},{2,10},{10... | collective-permute-start | bytes 589832 | tf_op jit(solution)/shard_map/ppermute | solution.py:34
  79.8 5.7 %collective-permute-start.21 = (f32[6,32,256]{2,1,0:T(8,128)S(1)}, f32[6,32,256]{2,1,0:T(8,128)S(1)}, u32[]{:S(2)}, u32[]{:S(2)}) collective-permute-start(f32[6,32,256]{2,1,0:T(8,128)S(1)} %collective-permute-done.18.refs_2_), channel_id=1, source_target_pairs={{0,16},{16,0},{8,24},{24,8},{1,17},{17,1},{9,25},{25,9},{2,18},{18... | collective-permute-start | bytes 589832 | tf_op jit(solution)/shard_map/ppermute | solution.py:38
